TPU v7x, 128 devices: a whole 4x4x4 slice. The times are simulated.
128 devices in a mesh: section: 2 (over core), ctx: 4 (over z), exp: 16 (over x, y).
Axes of the slice: x: 4, y: 4, z: 4, core: 2. Of those that a mesh axis runs over, the one named last changes fastest.
Arguments:
- inputs: bfloat16 [2, 16, 512, 768], P(None, 'exp', 'ctx'), may hold values from -6 to 6
- cotangent: bfloat16 [2, 16, 512, 768], P(None, 'exp', 'ctx'), may hold values from -6 to 6
- routes: int32 [2, 2, 16, 512, 2], P('section', None, 'exp', 'ctx'), may hold values from 0 to 15, all different within a row; in each aligned block of 128 rows (0 to 127, 128 to 255, ..., all dimensions but the last counted through in order) at most 17 rows name the same one
- block_order: int32 [8], replicated, may hold values from 0 to 7, each once
- attn_gain: bfloat16 [2, 768], P('section', ('ctx', 'exp')), may hold values from 0.5 to 1.5
- qkv_weight: bfloat16 [2, 768, 2304], P('section', ('ctx', 'exp')), may hold values from -0.21875 to 0.21875
- out_weight: bfloat16 [2, 768, 768], P('section', ('ctx', 'exp')), may hold values from -4 to 4
- rel_bias: bfloat16 [2, 384], P('section', ('ctx', 'exp')), may hold values from -4 to 4
- moe_gain: bfloat16 [2, 768], P('section', ('ctx', 'exp')), may hold values from 0.5 to 1.5
- router_weight: bfloat16 [2, 768, 16], P('section', ('ctx', 'exp')), may hold values from -0.375 to 0.375
- expert_in: bfloat16 [2, 16, 768, 3072], P('section', 'exp', None, 'ctx'), may hold values from -0.21875 to 0.21875
- expert_out: bfloat16 [2, 16, 768, 3072], P('section', 'exp', None, 'ctx'), may hold values from -0.109375 to 0.109375
Outputs:
- layer_out: bfloat16 [2, 2, 16, 512, 768], P('section', None, 'exp', 'ctx')
- input_grad: float32 [2, 2, 16, 512, 768], P('section', None, 'exp', 'ctx')
- attn_gain_grad: float32 [2, 768], P('section', ('ctx', 'exp'))
- qkv_grad: float32 [2, 768, 2304], P('section', ('ctx', 'exp'))
- out_grad: float32 [2, 768, 768], P('section', ('ctx', 'exp'))
- bias_grad: float32 [2, 384], P('section', ('ctx', 'exp'))
- moe_gain_grad: float32 [2, 768], P('section', ('ctx', 'exp'))
- router_grad: float32 [2, 768, 16], P('section', ('ctx', 'exp'))
- expert_in_grad: float32 [2, 16, 768, 3072], P('section', 'exp', None, 'ctx')
- expert_out_grad: float32 [2, 16, 768, 3072], P('section', 'exp', None, 'ctx')
Inputs may be any that keep to these rules, and one draw needn't show every extreme that they name: `routes`: within every aligned block of 128 rows (one micro-batch, one sequence, rows b * 128 onward) no expert is named by more than 17 of the block's assignments, a bound that some block reaches; the two experts of a token differ. A permutation: stored block j of every sequence, rows j * 64 onward, holds positions block_order[j] * 64 onward.
All inputs are finite; a program needn't handle non-finite values.
Results may differ from a plain program's by a relative error of at most 0.04.
Values may be sent and summed in bfloat16 or wider, within the bound.
A program may use at most 256 MiB of HBM per device.

v0:
```python
import math

import jax
import jax.numpy as jnp
import numpy as np
from jax import lax
from jax.sharding import PartitionSpec as P

HEADS = 12
HEAD_DIM = 64
BUCKETS = 32
REACH = 128
TOP = 2


HIGH = lax.Precision.HIGHEST
EPS = 1e-06
NEG = -1e30


def side_by_side(arrays, axis, dim, along):
    widths = [math.prod(a.shape[along:]) for a in arrays]
    both = jnp.concatenate(
        [a.reshape(*a.shape[:along], w) for a, w in zip(arrays, widths)], axis=along
    )
    result = lax.all_gather(both, axis, axis=dim, tiled=True)
    pieces = jnp.split(result, [sum(widths[:k]) for k in range(1, len(widths))], axis=along)
    return tuple(
        (b.reshape(*result.shape[:along], *a.shape[along:]) for a, b in zip(arrays, pieces))
    )


def split_up(value, dim, length):
    lengths = value.shape
    pieces = value.reshape(*lengths[:dim], length, lengths[dim] // length, *lengths[dim + 1 :])
    return jnp.moveaxis(pieces, dim, 0)


def sum_at_owner(value, axis, dim):
    length = lax.axis_size(axis)
    pieces = lax.all_to_all(split_up(value, dim, length), axis, 0, 0, tiled=True)
    return jnp.sum(pieces.astype(jnp.float32), axis=0)


def sent_together(arrays, axis, dim, along):
    both = jnp.concatenate(arrays, axis=along)
    result, at, gathered = (sum_at_owner(both, axis, dim), 0, [])
    for a in arrays:
        gathered.append(lax.slice_in_dim(result, at, at + a.shape[along], axis=along))
        at += a.shape[along]
    return tuple(gathered)


def from_behind(value, axis, steps):
    count = lax.axis_size(axis)
    first, last = (max(0, -steps), min(count, count - steps))
    return lax.ppermute(value, axis, [(source, source + steps) for source in range(first, last)])


def rms_norm(values, gain):
    return values * lax.rsqrt(jnp.mean(values * values, -1, keepdims=True) + EPS) * gain


def bucket_of(distance):
    half = BUCKETS // 2
    powers = np.arange(1, BUCKETS - half) / (BUCKETS - half)
    bounds = jnp.asarray(np.ceil(half * (REACH / half) ** powers).astype(np.int32))
    distance = jnp.maximum(distance, 0)
    above = (distance[..., None] >= bounds).astype(jnp.int32)
    return jnp.minimum(distance, half) + jnp.sum(above, -1, dtype=jnp.int32)


def positions(block_order, seq_len):
    count = block_order.shape[0]
    span = seq_len // count
    index = jnp.arange(seq_len, dtype=jnp.int32)
    owner = (index // span)[:, None] == jnp.arange(count, dtype=jnp.int32)[None, :]
    start = jnp.sum(jnp.where(owner, block_order[None, :], 0), -1, dtype=jnp.int32)
    return start * span + index % span


def slot_tables(route_rows, experts, capacity):
    tok_count, top_count = route_rows.shape
    route_hot = (route_rows[:, :, None] == jnp.arange(experts, dtype=jnp.int32)).astype(jnp.int32)
    flat_hot = route_hot.reshape(tok_count * top_count, experts)
    earlier = jnp.cumsum(flat_hot, 0, dtype=jnp.int32) - flat_hot
    slot_number = jnp.sum(earlier * flat_hot, -1, dtype=jnp.int32).reshape(tok_count, top_count)
    target = route_rows * capacity + slot_number
    slot_hot = target[:, :, None] == jnp.arange(experts * capacity, dtype=jnp.int32)
    return (route_hot, slot_hot)


def contract_first(left, right):
    return lax.dot_general(
        left, right, (((0,), (0,)), ((), ())), preferred_element_type=jnp.float32
    )


def contract_last(left, right):
    return lax.dot_general(
        left, right, (((1,), (1,)), ((), ())), preferred_element_type=jnp.float32
    )


def to_experts(buffer):
    return lax.all_to_all(buffer, "exp", split_axis=0, concat_axis=0, tiled=True)


def to_sources(buffer):
    return lax.all_to_all(buffer, "exp", split_axis=0, concat_axis=0, tiled=True)


def on_device(
    inputs,
    cotangent,
    routes,
    block_order,
    attn_gain,
    qkv_weight,
    out_weight,
    rel_bias,
    moe_gain,
    router_weight,
    expert_in,
    expert_out,
):
    micro_count = inputs.shape[0]
    row_count = inputs.shape[2]
    model_width = inputs.shape[3]
    ctx_count = lax.axis_size("ctx")
    exp_count = lax.axis_size("exp")
    seq_len = row_count * ctx_count
    capacity = row_count * TOP // exp_count + max(1, row_count * TOP // (16 * exp_count))
    slot_count = exp_count * capacity
    section_index = lax.axis_index("section")
    ctx_index = lax.axis_index("ctx")
    is_first = section_index == 0
    score_scale = HEAD_DIM ** (-0.5)
    dense_parts = (
        *side_by_side((attn_gain[0], qkv_weight[0], out_weight[0]), ("ctx", "exp"), 0, 1),
        lax.all_gather(rel_bias[0], ("ctx", "exp"), axis=0, tiled=True),
        *side_by_side((moe_gain[0], router_weight[0]), ("ctx", "exp"), 0, 1),
    )
    gain_one = dense_parts[0].astype(jnp.float32)
    w_qkv = dense_parts[1]
    w_proj = dense_parts[2]
    bias_table = dense_parts[3].astype(jnp.float32).reshape(BUCKETS, HEADS)
    gain_two = dense_parts[4].astype(jnp.float32)
    w_router = dense_parts[5]
    own_in = expert_in[0, 0]
    own_out = expert_out[0, 0]
    apply_in, apply_out = (
        lax.all_gather(own_in, "ctx", axis=1, tiled=True),
        lax.all_gather(own_out, "ctx", axis=1, tiled=True),
    )
    pos_all = positions(block_order, seq_len)
    pos_mine = lax.dynamic_slice_in_dim(pos_all, ctx_index * row_count, row_count)
    distance = pos_mine[:, None] - pos_all[None, :]
    visible = distance >= 0
    bucket_hot = (bucket_of(distance)[:, :, None] == jnp.arange(BUCKETS, dtype=jnp.int32)).astype(
        jnp.float32
    )
    bias_all = jnp.einsum("qkb,bh->hqk", bucket_hot, bias_table, precision=HIGH)

    def scores_of(q_heads, k_heads):
        raw_scores = (
            jnp.einsum("qhd,khd->hqk", q_heads, k_heads, preferred_element_type=jnp.float32)
            * score_scale
        )
        return jnp.where(visible[None], raw_scores + bias_all, NEG)

    def expert_backward(grad_arrived, expert_keep):
        entering, before = expert_keep
        hidden, gelu_back = jax.vjp(lambda pre_act: jax.nn.gelu(pre_act, approximate=True), before)
        hidden = hidden.astype(jnp.bfloat16)
        grad_rows = grad_arrived.reshape(-1, model_width)
        grad_hidden = jnp.dot(grad_rows, apply_out, preferred_element_type=jnp.float32)
        grad_before = gelu_back(grad_hidden)[0].astype(jnp.bfloat16)
        grad_enter = contract_last(grad_before, apply_in)
        grad_down = contract_first(grad_rows, hidden)
        grad_up = contract_first(entering, grad_before)
        return (
            grad_enter.astype(jnp.bfloat16).reshape(exp_count, capacity, model_width),
            grad_up,
            grad_down,
        )

    def backward(grad_result, keep):
        (
            carried,
            normed,
            query_rows,
            key_all,
            value_all,
            log_total,
            attended,
            middle,
            mixed,
            chosen,
            picked,
            route_rows,
            expert_keep,
        ) = keep
        route_hot, slot_hot = slot_tables(route_rows, exp_count, capacity)
        gates, gate_back = jax.vjp(lambda chosen_logits: jax.nn.softmax(chosen_logits, -1), chosen)
        grad_gates = jnp.sum(picked * grad_result[None], -1).T
        grad_picked = gates.T[:, :, None] * grad_result[None]
        grad_back = jnp.einsum(
            "tks,ktd->sd", slot_hot.astype(jnp.float32), grad_picked, precision=HIGH
        )
        grad_back = grad_back.astype(jnp.bfloat16).reshape(exp_count, capacity, model_width)
        grad_enter, grad_up, grad_down = expert_backward(to_experts(grad_back), expert_keep)
        grad_leave = to_sources(grad_enter).reshape(slot_count, model_width)
        placing = jnp.sum(slot_hot.astype(jnp.float32), 1).astype(jnp.bfloat16)
        grad_mixed = jnp.dot(placing, grad_leave, preferred_element_type=jnp.float32)
        grad_chosen = gate_back(grad_gates)[0]
        grad_logits = jnp.sum(grad_chosen[:, :, None] * route_hot.astype(jnp.float32), 1)
        grad_router = jnp.einsum(
            "td,te->de", mixed, grad_logits, precision=HIGH, preferred_element_type=jnp.float32
        )
        grad_mixed = grad_mixed + jnp.einsum(
            "te,de->td", grad_logits, w_router, precision=HIGH, preferred_element_type=jnp.float32
        )
        _, norm_two_back = jax.vjp(rms_norm, middle, gain_two)
        grad_mid_norm, grad_gain_two = norm_two_back(grad_mixed)
        grad_middle = grad_result + grad_mid_norm
        grad_branch = grad_middle.astype(jnp.bfloat16)
        grad_proj_out = contract_first(attended, grad_branch)
        grad_attended = contract_last(grad_branch, w_proj).astype(jnp.bfloat16)
        q_heads = query_rows.reshape(row_count, HEADS, HEAD_DIM)
        k_heads = key_all.reshape(seq_len, HEADS, HEAD_DIM)
        v_heads = value_all.reshape(seq_len, HEADS, HEAD_DIM)
        probs_full = jnp.exp(scores_of(q_heads, k_heads) - log_total)
        probs = probs_full.astype(jnp.bfloat16)
        grad_heads = grad_attended.reshape(row_count, HEADS, HEAD_DIM)
        grad_probs = jnp.einsum(
            "qhd,khd->hqk", grad_heads, v_heads, preferred_element_type=jnp.float32
        )
        grad_value_all = jnp.einsum(
            "hqk,qhd->khd", probs, grad_heads, preferred_element_type=jnp.float32
        ).reshape(seq_len, model_width)
        grad_scores = probs_full * (
            grad_probs - jnp.sum(probs_full * grad_probs, -1, keepdims=True)
        )
        grad_scores = grad_scores.astype(jnp.bfloat16)
        grad_query = (
            jnp.einsum("hqk,khd->qhd", grad_scores, k_heads, preferred_element_type=jnp.float32)
            * score_scale
        )
        grad_key_all = (
            jnp.einsum("hqk,qhd->khd", grad_scores, q_heads, preferred_element_type=jnp.float32)
            * score_scale
        )
        grad_table = jnp.einsum(
            "qkb,hqk->bh", bucket_hot, grad_scores.astype(jnp.float32), precision=HIGH
        )
        grad_key, grad_value = sent_together(
            (
                grad_key_all.reshape(seq_len, model_width).astype(jnp.bfloat16),
                grad_value_all.astype(jnp.bfloat16),
            ),
            "ctx",
            0,
            1,
        )
        grad_proj = jnp.concatenate(
            [
                grad_query.reshape(row_count, model_width).astype(jnp.bfloat16),
                grad_key.astype(jnp.bfloat16),
                grad_value.astype(jnp.bfloat16),
            ],
            1,
        )
        grad_qkv = contract_first(normed, grad_proj)
        grad_normed = contract_last(grad_proj, w_qkv)
        _, norm_one_back = jax.vjp(rms_norm, carried, gain_one)
        grad_carried_norm, grad_gain_one = norm_one_back(grad_normed)
        grad_carried = grad_middle + grad_carried_norm
        grads = (
            grad_gain_one,
            grad_qkv,
            grad_proj_out,
            grad_table.reshape(-1),
            grad_gain_two,
            grad_router,
            grad_up,
            grad_down,
        )
        return (grad_carried, grads)

    own_inputs = inputs[:, 0]
    own_cotangent = cotangent[:, 0]
    own_routes = routes[0, :, 0]
    received = jnp.zeros((row_count, model_width), jnp.bfloat16)
    results = []
    caches = []
    for tick in range(micro_count + 1):
        micro_id = jnp.clip(tick - section_index, 0, micro_count - 1)
        fresh = lax.dynamic_index_in_dim(own_inputs, micro_id, 0, keepdims=False)
        carried = jnp.where(is_first, fresh, received).astype(jnp.float32)
        route_rows = lax.dynamic_index_in_dim(own_routes, micro_id, 0, keepdims=False)
        forward_normed = rms_norm(carried, gain_one).astype(jnp.bfloat16)
        proj = jnp.dot(forward_normed, w_qkv, preferred_element_type=jnp.float32).astype(
            jnp.bfloat16
        )
        forward_query_rows = proj[:, :model_width]
        key_rows = proj[:, model_width : 2 * model_width]
        value_rows = proj[:, 2 * model_width :]
        forward_key_all = lax.all_gather(key_rows, "ctx", axis=0, tiled=True)
        forward_value_all = lax.all_gather(value_rows, "ctx", axis=0, tiled=True)
        forward_q_heads = forward_query_rows.reshape(row_count, HEADS, HEAD_DIM)
        forward_k_heads = forward_key_all.reshape(seq_len, HEADS, HEAD_DIM)
        forward_v_heads = forward_value_all.reshape(seq_len, HEADS, HEAD_DIM)
        scores = scores_of(forward_q_heads, forward_k_heads)
        row_peak = jnp.max(scores, -1, keepdims=True)
        forward_log_total = (
            jnp.log(jnp.sum(jnp.exp(scores - row_peak), -1, keepdims=True)) + row_peak
        )
        forward_probs = jnp.exp(scores - forward_log_total).astype(jnp.bfloat16)
        forward_attended = jnp.einsum(
            "hqk,khd->qhd", forward_probs, forward_v_heads, preferred_element_type=jnp.float32
        )
        forward_attended = forward_attended.reshape(row_count, model_width).astype(jnp.bfloat16)
        forward_middle = carried + jnp.dot(
            forward_attended, w_proj, preferred_element_type=jnp.float32
        )
        forward_mixed = rms_norm(forward_middle, gain_two).astype(jnp.bfloat16)
        logits = jnp.dot(forward_mixed, w_router, preferred_element_type=jnp.float32)
        forward_route_hot, forward_slot_hot = slot_tables(route_rows, exp_count, capacity)
        forward_chosen = jnp.sum(forward_route_hot.astype(jnp.float32) * logits[:, None, :], -1)
        forward_gates = jax.nn.softmax(forward_chosen, -1)
        forward_placing = jnp.sum(forward_slot_hot.astype(jnp.float32), 1).astype(jnp.bfloat16)
        outgoing = (
            contract_first(forward_placing, forward_mixed)
            .astype(jnp.bfloat16)
            .reshape(exp_count, capacity, model_width)
        )
        expert_entering = to_experts(outgoing).reshape(-1, model_width)
        expert_before = jnp.dot(expert_entering, apply_in, preferred_element_type=jnp.float32)
        expert_hidden = jax.nn.gelu(expert_before, approximate=True).astype(jnp.bfloat16)
        leaving = contract_last(expert_hidden, apply_out)
        returned = leaving.astype(jnp.bfloat16).reshape(exp_count, capacity, model_width)
        forward_expert_keep = (expert_entering, expert_before)
        back_rows = to_sources(returned).reshape(slot_count, model_width)
        forward_picked = jnp.einsum(
            "tks,sd->ktd",
            forward_slot_hot.astype(jnp.bfloat16),
            back_rows,
            preferred_element_type=jnp.float32,
        )
        result = forward_middle + jnp.sum(forward_gates.T[:, :, None] * forward_picked, 0)
        forward_keep = (
            carried,
            forward_normed,
            forward_query_rows,
            forward_key_all,
            forward_value_all,
            forward_log_total,
            forward_attended,
            forward_middle,
            forward_mixed,
            forward_chosen,
            forward_picked,
            route_rows,
            forward_expert_keep,
        )
        result, keep = (result, forward_keep)
        handed = result.astype(jnp.bfloat16)
        if tick < micro_count:
            received = from_behind(handed, "section", 1)
        results.append(handed)
        caches.append(keep)
    stacked = jax.tree.map(lambda *parts: jnp.stack(parts), *caches)
    grad_received = jnp.zeros((row_count, model_width), jnp.bfloat16)
    input_grads = []
    totals = None
    for tick in range(micro_count + 1):
        micro_raw = tick - 1 + section_index
        is_valid = ((micro_raw >= 0) & (micro_raw < micro_count)).astype(jnp.float32)
        micro_id = jnp.clip(micro_raw, 0, micro_count - 1)
        given = lax.dynamic_index_in_dim(own_cotangent, micro_id, 0, keepdims=False)
        grad_result = jnp.where(is_first, grad_received, given).astype(jnp.float32)
        which = jnp.clip(tick - 1 + 2 * section_index, 0, micro_count)
        keep = jax.tree.map(
            lambda part: lax.dynamic_index_in_dim(part, which, 0, keepdims=False), stacked
        )
        grad_carried, grads = backward(grad_result, keep)
        if totals is None:
            totals = jax.tree.map(lambda part: is_valid * part, grads)
        else:
            totals = jax.tree.map(lambda total, part: total + is_valid * part, totals, grads)
        grad_handed = grad_carried.astype(jnp.bfloat16)
        if tick < micro_count:
            grad_received = from_behind(grad_handed, "section", -1)
        input_grads.append(jnp.where(is_first, grad_carried, grad_handed.astype(jnp.float32)))
    dense_sums = lax.psum_scatter(totals[:6], ("ctx", "exp"), scatter_dimension=0, tiled=True)
    grad_up, grad_down = (
        lax.psum_scatter(
            totals[6].astype(jnp.bfloat16), "ctx", scatter_dimension=1, tiled=True
        ).astype(jnp.float32),
        lax.psum_scatter(
            totals[7].astype(jnp.bfloat16), "ctx", scatter_dimension=1, tiled=True
        ).astype(jnp.float32),
    )
    layer_out = jnp.stack(
        [jnp.where(is_first, results[m], results[m + 1]) for m in range(micro_count)]
    )
    input_grad = jnp.stack(
        [jnp.where(is_first, input_grads[m + 1], input_grads[m]) for m in range(micro_count)]
    )
    layer_out = layer_out.reshape(1, micro_count, 1, row_count, model_width)
    input_grad = input_grad.reshape(1, micro_count, 1, row_count, model_width)
    return (
        layer_out,
        input_grad,
        dense_sums[0][None],
        dense_sums[1][None],
        dense_sums[2][None],
        dense_sums[3][None],
        dense_sums[4][None],
        dense_sums[5][None],
        grad_up[None, None],
        grad_down[None, None],
    )


def solution(mesh):
    return jax.shard_map(
        on_device,
        mesh=mesh,
        in_specs=(
            P(None, "exp", "ctx", None),
            P(None, "exp", "ctx", None),
            P("section", None, "exp", "ctx", None),
            P(),
            P("section", ("ctx", "exp")),
            P("section", ("ctx", "exp"), None),
            P("section", ("ctx", "exp"), None),
            P("section", ("ctx", "exp")),
            P("section", ("ctx", "exp")),
            P("section", ("ctx", "exp"), None),
            P("section", "exp", None, "ctx"),
            P("section", "exp", None, "ctx"),
        ),
        out_specs=(
            P("section", None, "exp", "ctx", None),
            P("section", None, "exp", "ctx", None),
            P("section", ("ctx", "exp")),
            P("section", ("ctx", "exp"), None),
            P("section", ("ctx", "exp"), None),
            P("section", ("ctx", "exp")),
            P("section", ("ctx", "exp")),
            P("section", ("ctx", "exp"), None),
            P("section", "exp", None, "ctx"),
            P("section", "exp", None, "ctx"),
        ),
        check_vma=False,
    )
```

profile of v0, /device:TPU:2, one launch (start us, length us, event | category | flops | bytes accessed | tf_op | source)
XLA Modules:
  0.0 1839.1 jit_solution(3967321093002657093)
XLA Ops:
  16.7 12.6 copy.335
  30.8 171.7 %all-reduce = bf16[384]{0:T(512)(128)(2,1)S(1)} all-reduce(bf16[384]{0:T(512)(128)(2,1)S(1)} %dynamic-update-slice), channel_id=2, replica_groups=mesh['section'=2,'ctx'=4,'exp'=16] {'ctx','exp'}, use_global_device_ids=true, to_apply=%add | all-reduce | flops 384 | bytes 1536
  202.9 171.0 %all-gather.4 = bf16[64,12,17]{2,1,0:T(8,128)(2,1)S(1)} all-gather(bf16[1,12,17]{2,1,0:T(8,128)(2,1)S(1)} %maximum_bitcast_fusion.2), channel_id=1, replica_groups=mesh['section'=2,'ctx'=4,'exp'=16] {'ctx','exp'}, dimensions={0}, use_global_device_ids=true | all-gather | bytes 26520 | tf_op jit(solution)/shard_map/all_gather | solution.py:26
  386.5 9.7 reshape.1057
  401.4 13.3 all_gather.34
  415.8 13.3 all_gather.35
  440.4 14.9 all-to-all-start
  482.1 8.3 all-to-all-done.1
  500.7 14.5 all_gather.40
  517.2 13.7 all_gather.41
  598.3 15.2 all_gather.42
  616.0 14.1 all_gather.43
  672.7 7.1 all-to-all-start.5
  703.5 9.1 pad_maximum_fusion
  726.3 7.3 all-to-all-start.7
  893.0 11.0 all-to-all-done.11
  924.0 7.3 all-to-all-start.12
  931.3 7.9 fusion.249
  944.3 7.1 fusion.53
  952.6 7.4 add_convert_fusion.1
  963.1 8.5 fusion.120
  987.1 8.4 fusion.118
  1052.3 11.5 add_convert_fusion
  1074.6 9.4 multiply_add_fusion
  1084.1 200.6 %fusion.469 = (f32[16,2304]{1,0:T(8,128)S(1)}, f32[16,768]{1,0:T(8,128)S(1)}, f32[16,16]{1,0:T(8,128)S(1)}) fusion(f32[768,2304]{1,0:T(8,128)} %multiply_add_fusion, f32[768,768]{1,0:T(8,128)} %multiply_add_fusion.1, f32[768,16]{1,0:T(8,128)S(1)} %copy-done.89), kind=kCustom, calls=%all-reduce-scatter.3 | all-reduce-scatter fusion | flops 3162113 | bytes 9684480
  1294.6 13.8 collective-permute-start.48
  1312.3 11.5 collective-permute-start.44
  1396.3 333.6 %all-reduce.10 = (f32[768]{0:T(1024)S(1)}, f32[384]{0:T(512)S(1)}, f32[768]{0:T(1024)S(1)}) all-reduce(f32[768]{0:T(1024)S(1)} %multiply_add_fusion.3, f32[384]{0:T(512)} %add.571, f32[768]{0:T(1024)S(1)} %copy-done.178), channel_id=5, replica_groups=mesh['section'=2,'ctx'=4,'exp'=16] {'ctx','exp'}, use_global_device_ids=true, to_apply=%region_86.87.clone | all-reduce | flops 1920 | bytes 15360
  1741.6 20.7 %collective-permute-start.12 = (f32[16,2304]{1,0:T(8,128)S(1)}, f32[16,2304]{1,0:T(8,128)S(1)}, u32[]{:S(2)}, u32[]{:S(2)}) collective-permute-start(f32[16,2304]{1,0:T(8,128)S(1)} %get-tuple-element.85), channel_id=1, source_target_pairs={{0,9},{1,10},{2,11},{3,12},{4,13},{5,14},{6,15},{7,16},{8,17},{9,1... | collective-permute-start | bytes 442376
  1773.0 12.3 concatenate.40
  1800.9 8.8 concatenate.39
  1811.8 14.0 concatenate.38
  (1021 shorter events, 628.7 us)
Async XLA Ops:
  7.2 379.3 %all-gather.13.cloned.1.call-start = ((), (), s32[]{:S(2)}) async-start(), calls=%async_computation.21 | async-start | bytes 6656000 | tf_op jit(solution)/shard_map/all_gather | solution.py:26
  9.7 454.0 %all-gather.9.cloned.1.call-start = ((), (), s32[]{:S(2)}) async-start(), calls=%async_computation.19 | async-start | bytes 5898240 | tf_op jit(solution)/shard_map/all_gather | solution.py:153
  10.4 458.8 %all-gather.11.cloned.1.call-start = ((), (), s32[]{:S(2)}) async-start(), calls=%async_computation.20 | async-start | bytes 5898240 | tf_op jit(solution)/shard_map/all_gather | solution.py:154
  440.4 23.1 %all-to-all-start = ((bf16[16,17,768]{2,1,0:T(8,128)(2,1)}), bf16[16,17,768]{2,1,0:T(8,128)(2,1)S(1)}, u32[]{:S(2)}, u32[]{:S(2)}) async-start(bf16[16,17,768]{2,1,0:T(8,128)(2,1)} %reshape.988), calls=%async_computation | async-start | bytes 1179648 | tf_op jit(solution)/shard_map/all_to_all | solution.py:106
  879.9 24.1 %all-to-all-start.11 = ((bf16[4,128,1536]{1,2,0:T(8,128)(2,1)}), bf16[4,128,1536]{1,2,0:T(8,128)(2,1)}, u32[]{:S(2)}, u32[]{:S(2)}) async-start(bf16[4,128,1536]{1,2,0:T(8,128)(2,1)} %pad_maximum_fusion.5), calls=%async_computation.11 | async-start | bytes 3145728 | tf_op jit(solution)/shard_map/all_to_all | solution.py:41
  931.2 895.4 %reduce-scatter.9.cloned.1.call-start = ((), (), s32[]{:S(2)}) async-start(), calls=%async_computation.17 | async-start | bytes 5898240 | tf_op jit(solution)/shard_map/reduce_scatter | solution.py:398
  1047.9 24.4 %all-to-all-start.14 = ((bf16[4,128,1536]{1,2,0:T(8,128)(2,1)}), bf16[4,128,1536]{1,2,0:T(8,128)(2,1)}, u32[]{:S(2)}, u32[]{:S(2)}) async-start(bf16[4,128,1536]{1,2,0:T(8,128)(2,1)} %pad_maximum_fusion.6), calls=%async_computation.14 | async-start | bytes 3145728 | tf_op jit(solution)/shard_map/all_to_all | solution.py:41
  1052.3 777.3 %reduce-scatter.11.cloned.1.call-start = ((), (), s32[]{:S(2)}) async-start(), calls=%async_computation.18 | async-start | bytes 5898240 | tf_op jit(solution)/shard_map/reduce_scatter | solution.py:401
  1284.7 26.3 %collective-permute-start.50 = (f32[16,16]{1,0:T(8,128)S(1)}, f32[16,16]{1,0:T(8,128)S(1)}, u32[]{:S(2)}, u32[]{:S(2)}) collective-permute-start(f32[16,16]{1,0:T(8,128)S(1)} %get-tuple-element.87), channel_id=1, source_target_pairs={{0,15},{1,16},{2,17},{3,18},{4,19},{5,20},{6,21},{7,22},{8,23},{9,... | collective-permute-start | bytes 3080
  1286.0 26.3 %collective-permute-start.49 = (f32[16,16]{1,0:T(8,128)S(1)}, f32[16,16]{1,0:T(8,128)S(1)}, u32[]{:S(2)}, u32[]{:S(2)}) collective-permute-start(f32[16,16]{1,0:T(8,128)S(1)} %get-tuple-element.87), channel_id=1, source_target_pairs={{0,14},{1,15},{2,16},{3,17},{4,18},{5,19},{6,20},{7,21},{8,22},{9,... | collective-permute-start | bytes 3080
  1287.3 22.4 %collective-permute-start.51 = (f32[12,16]{1,0:T(8,128)S(1)}, f32[12,16]{1,0:T(8,128)S(1)}, u32[]{:S(2)}, u32[]{:S(2)}) collective-permute-start(f32[12,16]{1,0:T(8,128)S(1)} %slice.134), channel_id=1, source_target_pairs={{0,16},{1,17},{2,18},{3,19},{4,20},{5,21},{6,22},{7,23},{8,24},{9,... | collective-permute-start | bytes 2312
  1294.6 32.2 %collective-permute-start.48 = (f32[16,16]{1,0:T(8,128)S(1)}, f32[16,16]{1,0:T(8,128)S(1)}, u32[]{:S(2)}, u32[]{:S(2)}) collective-permute-start(f32[16,16]{1,0:T(8,128)S(1)} %get-tuple-element.87), channel_id=1, source_target_pairs={{0,13},{1,14},{2,15},{3,16},{4,17},{5,18},{6,19},{7,20},{8,21},{9,... | collective-permute-start | bytes 3080
  1308.4 20.6 %collective-permute-start.47 = (f32[16,16]{1,0:T(8,128)S(1)}, f32[16,16]{1,0:T(8,128)S(1)}, u32[]{:S(2)}, u32[]{:S(2)}) collective-permute-start(f32[16,16]{1,0:T(8,128)S(1)} %get-tuple-element.87), channel_id=1, source_target_pairs={{0,12},{1,13},{2,14},{3,15},{4,16},{5,17},{6,18},{7,19},{8,20},{9,... | collective-permute-start | bytes 3080
  1309.7 22.9 %collective-permute-start.46 = (f32[16,16]{1,0:T(8,128)S(1)}, f32[16,16]{1,0:T(8,128)S(1)}, u32[]{:S(2)}, u32[]{:S(2)}) collective-permute-start(f32[16,16]{1,0:T(8,128)S(1)} %get-tuple-element.87), channel_id=1, source_target_pairs={{0,11},{1,12},{2,13},{3,14},{4,15},{5,16},{6,17},{7,18},{8,19},{9,... | collective-permute-start | bytes 3080
  1311.0 23.6 %collective-permute-start.45 = (f32[16,16]{1,0:T(8,128)S(1)}, f32[16,16]{1,0:T(8,128)S(1)}, u32[]{:S(2)}, u32[]{:S(2)}) collective-permute-start(f32[16,16]{1,0:T(8,128)S(1)} %get-tuple-element.87), channel_id=1, source_target_pairs={{0,10},{1,11},{2,12},{3,13},{4,14},{5,15},{6,16},{7,17},{8,18},{9,... | collective-permute-start | bytes 3080
  1312.3 25.4 %collective-permute-start.44 = (f32[16,16]{1,0:T(8,128)S(1)}, f32[16,16]{1,0:T(8,128)S(1)}, u32[]{:S(2)}, u32[]{:S(2)}) collective-permute-start(f32[16,16]{1,0:T(8,128)S(1)} %get-tuple-element.87), channel_id=1, source_target_pairs={{0,9},{1,10},{2,11},{3,12},{4,13},{5,14},{6,15},{7,16},{8,17},{9,1... | collective-permute-start | bytes 3080
  1341.5 26.1 %collective-permute-start.34 = (f32[16,768]{1,0:T(8,128)S(1)}, f32[16,768]{1,0:T(8,128)S(1)}, u32[]{:S(2)}, u32[]{:S(2)}) collective-permute-start(f32[16,768]{1,0:T(8,128)S(1)} %get-tuple-element.86), channel_id=1, source_target_pairs={{0,15},{1,16},{2,17},{3,18},{4,19},{5,20},{6,21},{7,22},{8,23},{9,... | collective-permute-start | bytes 147464
  1383.5 346.4 %collective-permute-start.23 = (f32[16,768]{1,0:T(8,128)S(1)}, f32[16,768]{1,0:T(8,128)S(1)}, u32[]{:S(2)}, u32[]{:S(2)}) collective-permute-start(f32[16,768]{1,0:T(8,128)S(1)} %get-tuple-element.86), channel_id=1, source_target_pairs={{0,4},{1,5},{2,6},{3,7},{4,8},{5,9},{6,10},{7,11},{8,12},{9,13},{1... | collective-permute-start | bytes 147464
  1385.5 345.7 %collective-permute-start.22 = (f32[16,768]{1,0:T(8,128)S(1)}, f32[16,768]{1,0:T(8,128)S(1)}, u32[]{:S(2)}, u32[]{:S(2)}) collective-permute-start(f32[16,768]{1,0:T(8,128)S(1)} %get-tuple-element.86), channel_id=1, source_target_pairs={{0,3},{1,4},{2,5},{3,6},{4,7},{5,8},{6,9},{7,10},{8,11},{9,12},{10... | collective-permute-start | bytes 147464
  1388.9 343.6 %collective-permute-start.21 = (f32[16,768]{1,0:T(8,128)S(1)}, f32[16,768]{1,0:T(8,128)S(1)}, u32[]{:S(2)}, u32[]{:S(2)}) collective-permute-start(f32[16,768]{1,0:T(8,128)S(1)} %get-tuple-element.86), channel_id=1, source_target_pairs={{0,2},{1,3},{2,4},{3,5},{4,6},{5,7},{6,8},{7,9},{8,10},{9,11},{10,... | collective-permute-start | bytes 147464
  1392.6 341.3 %collective-permute-start.20 = (f32[16,768]{1,0:T(8,128)S(1)}, f32[16,768]{1,0:T(8,128)S(1)}, u32[]{:S(2)}, u32[]{:S(2)}) collective-permute-start(f32[16,768]{1,0:T(8,128)S(1)} %get-tuple-element.86), channel_id=1, source_target_pairs={{0,1},{1,2},{2,3},{3,4},{4,5},{5,6},{6,7},{7,8},{8,9},{9,10},{10,1... | collective-permute-start | bytes 147464
  1394.9 341.8 %collective-permute-start.19 = (f32[12,2304]{1,0:T(8,128)S(1)}, f32[12,2304]{1,0:T(8,128)S(1)}, u32[]{:S(2)}, u32[]{:S(2)}) collective-permute-start(f32[12,2304]{1,0:T(8,128)S(1)} %slice.132), channel_id=1, source_target_pairs={{0,16},{1,17},{2,18},{3,19},{4,20},{5,21},{6,22},{7,23},{8,24},{9,... | collective-permute-start | bytes 331784
  1732.6 29.7 %collective-permute-start.16 = (f32[16,2304]{1,0:T(8,128)S(1)}, f32[16,2304]{1,0:T(8,128)S(1)}, u32[]{:S(2)}, u32[]{:S(2)}) collective-permute-start(f32[16,2304]{1,0:T(8,128)S(1)} %get-tuple-element.85), channel_id=1, source_target_pairs={{0,13},{1,14},{2,15},{3,16},{4,17},{5,18},{6,19},{7,20},{8,21},{9,... | collective-permute-start | bytes 442376
  1733.9 30.0 %collective-permute-start.15 = (f32[16,2304]{1,0:T(8,128)S(1)}, f32[16,2304]{1,0:T(8,128)S(1)}, u32[]{:S(2)}, u32[]{:S(2)}) collective-permute-start(f32[16,2304]{1,0:T(8,128)S(1)} %get-tuple-element.85), channel_id=1, source_target_pairs={{0,12},{1,13},{2,14},{3,15},{4,16},{5,17},{6,18},{7,19},{8,20},{9,... | collective-permute-start | bytes 442376
  1736.8 32.0 %collective-permute-start.14 = (f32[16,2304]{1,0:T(8,128)S(1)}, f32[16,2304]{1,0:T(8,128)S(1)}, u32[]{:S(2)}, u32[]{:S(2)}) collective-permute-start(f32[16,2304]{1,0:T(8,128)S(1)} %get-tuple-element.85), channel_id=1, source_target_pairs={{0,11},{1,12},{2,13},{3,14},{4,15},{5,16},{6,17},{7,18},{8,19},{9,... | collective-permute-start | bytes 442376
  1740.3 45.0 %collective-permute-start.13 = (f32[16,2304]{1,0:T(8,128)S(1)}, f32[16,2304]{1,0:T(8,128)S(1)}, u32[]{:S(2)}, u32[]{:S(2)}) collective-permute-start(f32[16,2304]{1,0:T(8,128)S(1)} %get-tuple-element.85), channel_id=1, source_target_pairs={{0,10},{1,11},{2,12},{3,13},{4,14},{5,15},{6,16},{7,17},{8,18},{9,... | collective-permute-start | bytes 442376
  1741.6 46.7 %collective-permute-start.12 = (f32[16,2304]{1,0:T(8,128)S(1)}, f32[16,2304]{1,0:T(8,128)S(1)}, u32[]{:S(2)}, u32[]{:S(2)}) collective-permute-start(f32[16,2304]{1,0:T(8,128)S(1)} %get-tuple-element.85), channel_id=1, source_target_pairs={{0,9},{1,10},{2,11},{3,12},{4,13},{5,14},{6,15},{7,16},{8,17},{9,1... | collective-permute-start | bytes 442376
  1762.3 28.3 %collective-permute-start.11 = (f32[16,2304]{1,0:T(8,128)S(1)}, f32[16,2304]{1,0:T(8,128)S(1)}, u32[]{:S(2)}, u32[]{:S(2)}) collective-permute-start(f32[16,2304]{1,0:T(8,128)S(1)} %get-tuple-element.85), channel_id=1, source_target_pairs={{0,8},{1,9},{2,10},{3,11},{4,12},{5,13},{6,14},{7,15},{8,16},{9,17... | collective-permute-start | bytes 442376
  1764.0 30.6 %collective-permute-start.10 = (f32[16,2304]{1,0:T(8,128)S(1)}, f32[16,2304]{1,0:T(8,128)S(1)}, u32[]{:S(2)}, u32[]{:S(2)}) collective-permute-start(f32[16,2304]{1,0:T(8,128)S(1)} %get-tuple-element.85), channel_id=1, source_target_pairs={{0,7},{1,8},{2,9},{3,10},{4,11},{5,12},{6,13},{7,14},{8,15},{9,16}... | collective-permute-start | bytes 442376
  1769.5 28.8 %collective-permute-start.9 = (f32[16,2304]{1,0:T(8,128)S(1)}, f32[16,2304]{1,0:T(8,128)S(1)}, u32[]{:S(2)}, u32[]{:S(2)}) collective-permute-start(f32[16,2304]{1,0:T(8,128)S(1)} %get-tuple-element.85), channel_id=1, source_target_pairs={{0,6},{1,7},{2,8},{3,9},{4,10},{5,11},{6,12},{7,13},{8,14},{9,15},... | collective-permute-start | bytes 442376
  1785.3 25.1 %collective-permute-start.8 = (f32[16,2304]{1,0:T(8,128)S(1)}, f32[16,2304]{1,0:T(8,128)S(1)}, u32[]{:S(2)}, u32[]{:S(2)}) collective-permute-start(f32[16,2304]{1,0:T(8,128)S(1)} %get-tuple-element.85), channel_id=1, source_target_pairs={{0,5},{1,6},{2,7},{3,8},{4,9},{5,10},{6,11},{7,12},{8,13},{9,14},{... | collective-permute-start | bytes 442376
  1788.3 22.1 %collective-permute-start.7 = (f32[16,2304]{1,0:T(8,128)S(1)}, f32[16,2304]{1,0:T(8,128)S(1)}, u32[]{:S(2)}, u32[]{:S(2)}) collective-permute-start(f32[16,2304]{1,0:T(8,128)S(1)} %get-tuple-element.85), channel_id=1, source_target_pairs={{0,4},{1,5},{2,6},{3,7},{4,8},{5,9},{6,10},{7,11},{8,12},{9,13},{1... | collective-permute-start | bytes 442376
  (292 other events, 9551.5 us)
Sparse Core Ops, SparseCore 0:
  11.5 75.4 all-gather.12
  88.6 52.3 all-gather.8
  142.7 53.3 all-gather.10
  960.2 48.8 reduce-scatter.8
  1064.0 51.3 reduce-scatter.10
where the time goes:
time: 1860 us; the launch traced here: 1840 us
  blocking collectives  961 us (52%)
  matrix products  257 us (14%)
  starting transfers between devices  255 us (14%)
  local copies, waits for them, and re-layouts  190 us (10%)
  other arithmetic  90.3 us (5%)
  waiting for transfers between devices  64.9 us (3%)
  between operations  20.8 us (1%)
    unnamed x3, blocking collectives  706 us
    all_gather x1, blocking collectives, side_by_side(): result = lax.all_gather(both, axis, axis=dim, tiled=True)  171 us
    unnamed x48, starting transfers between devices  150 us
    dot_general x15, matrix products, contract_first(): lax.dot_general(left, right, (((0,), (0,)), ((), ())), preferred_element_...  78.4 us
    unnamed x521, local copies, waits for them, and re-layouts  76.4 us
    dot_general x12, matrix products, contract_last(): lax.dot_general(left, right, (((1,), (1,)), ((), ())), preferred_element_...  48.8 us
    all_to_all x6, starting transfers between devices, to_experts(): lax.all_to_all(buffer, 'exp', split_axis=0, concat_axis=0, tiled=True)  46.1 us
    all_gather x3, blocking collectives, on_device(): forward_value_all = lax.all_gather(value_rows, 'ctx', axis=0, tiled=True)  43 us
  transfers between devices with their start and end apart: 72, of which 16 were waited for; matrix products, arithmetic and copies ran while one was open for 27% of the time, Pallas kernels for 0%

commit v1 on v0

v1 whole, which is shorter than its diff:
```python
import functools
import math

import jax
import jax.numpy as jnp
import numpy as np
from jax import lax
from jax.experimental import pallas as pl
from jax.experimental.pallas import tpu as pltpu
from jax.sharding import PartitionSpec as P

HEADS = 12
HEAD_DIM = 64
BUCKETS = 32
REACH = 128
TOP = 2
EPS = 1e-06
NEG = -1e30
SPAN = 64
KINDS = 4
MESH = pl.DeviceIdType.MESH
BF16 = jnp.bfloat16
F32 = jnp.float32
GELU_C = math.sqrt(2.0 / math.pi)


def dot(a, b, dims):
    return lax.dot_general(a, b, (dims, ((), ())), preferred_element_type=F32)


def mm(a, b):
    return dot(a, b, ((1,), (0,)))


def mm_nt(a, b):
    return dot(a, b, ((1,), (1,)))


def mm_tn(a, b):
    return dot(a, b, ((0,), (0,)))


def meet_neighbours(axis, count):
    me = lax.axis_index(axis)
    right, left = lax.rem(me + 1, count), lax.rem(me + count - 1, count)
    barrier = pltpu.get_barrier_semaphore()
    for neighbour in (left, right):
        pl.semaphore_signal(barrier, inc=1, device_id={axis: neighbour}, device_id_type=MESH)
    pl.semaphore_wait(barrier, 2)
    return me, right, left


def remote(src, dst, send, recv, k, axis, to):
    return pltpu.make_async_remote_copy(
        src_ref=src,
        dst_ref=dst,
        send_sem=send.at[k],
        recv_sem=recv.at[k],
        device_id={axis: to},
        device_id_type=MESH,
    )


def halves(rows):
    first = (rows // 2 + 15) // 16 * 16
    return (pl.ds(0, first), pl.ds(first, rows - first))


def gather_kernel(axis, rows, x_ref, out_ref, send, recv, own_sem):
    me, right, left = meet_neighbours(axis, 4)
    low, high = halves(rows)
    own = pltpu.make_async_copy(x_ref, out_ref.at[me], own_sem)

    def step(k, src, slot, part, to):
        return remote(src.at[part], out_ref.at[slot, part], send, recv, k, axis, to)

    to_right_low = step(0, x_ref, me, low, right)
    to_left_high = step(1, x_ref, me, high, left)
    to_right_high = step(2, x_ref, me, high, right)
    to_left_low = step(3, x_ref, me, low, left)
    to_right_low.start()
    to_left_high.start()
    to_right_high.start()
    to_left_low.start()
    own.start()
    to_right_low.wait_recv()
    on_right = step(4, out_ref.at[left], left, low, right)
    on_right.start()
    to_left_high.wait_recv()
    on_left = step(5, out_ref.at[right], right, high, left)
    on_left.start()
    to_right_high.wait_recv()
    to_left_low.wait_recv()
    on_right.wait_recv()
    on_left.wait_recv()
    for c in (to_right_low, to_left_high, to_right_high, to_left_low, on_right, on_left):
        c.wait_send()
    own.wait()


def ctx_gather(x, cid):
    rows, width = x.shape
    return pl.pallas_call(
        functools.partial(gather_kernel, "ctx", rows),
        out_shape=jax.ShapeDtypeStruct((4, rows, width), x.dtype),
        in_specs=[pl.BlockSpec(memory_space=pltpu.VMEM)],
        out_specs=pl.BlockSpec(memory_space=pltpu.VMEM),
        scratch_shapes=[
            pltpu.SemaphoreType.DMA((6,)),
            pltpu.SemaphoreType.DMA((6,)),
            pltpu.SemaphoreType.DMA,
        ],
        compiler_params=pltpu.CompilerParams(
            collective_id=cid, has_side_effects=True, vmem_limit_bytes=16 << 20
        ),
    )(x)


def scatter_kernel(
    axis, rows, x_ref, out_ref, far_l, far_r, sum_l, sum_r, in_l, in_r, send, recv
):
    me, right, left = meet_neighbours(axis, 4)
    far = lax.rem(me + 2, 4)
    low, high = halves(rows)
    n_low = low.size
    n_high = high.size

    def step(k, src, dst, to):
        return remote(src, dst, send, recv, k, axis, to)

    a = step(0, x_ref.at[far, low], far_l, right)
    b = step(1, x_ref.at[far, high], far_r, left)
    c = step(2, x_ref.at[right, high], in_l.at[high], right)
    d = step(3, x_ref.at[left, low], in_r.at[low], left)
    a.start()
    b.start()
    c.start()
    d.start()
    a.wait_recv()
    sum_r[...] = (x_ref[right, :n_low, :].astype(F32) + far_l[...].astype(F32)).astype(BF16)
    e = step(4, sum_r, in_l.at[low], right)
    e.start()
    b.wait_recv()
    sum_l[...] = (x_ref[left, n_low:, :].astype(F32) + far_r[...].astype(F32)).astype(BF16)
    f = step(5, sum_l, in_r.at[high], left)
    f.start()
    c.wait_recv()
    d.wait_recv()
    e.wait_recv()
    f.wait_recv()
    out_ref[...] = (
        x_ref[me].astype(F32) + in_l[...].astype(F32) + in_r[...].astype(F32)
    ).astype(out_ref.dtype)
    for s in (a, b, c, d, e, f):
        s.wait_send()


def ctx_scatter(x, dtype, cid):
    _, rows, width = x.shape
    low, high = halves(rows)
    v = lambda n: pltpu.VMEM((n, width), BF16)
    return pl.pallas_call(
        functools.partial(scatter_kernel, "ctx", rows),
        out_shape=jax.ShapeDtypeStruct((rows, width), dtype),
        in_specs=[pl.BlockSpec(memory_space=pltpu.VMEM)],
        out_specs=pl.BlockSpec(memory_space=pltpu.VMEM),
        scratch_shapes=[
            v(low.size),
            v(high.size),
            v(high.size),
            v(low.size),
            v(rows),
            v(rows),
            pltpu.SemaphoreType.DMA((6,)),
            pltpu.SemaphoreType.DMA((6,)),
        ],
        compiler_params=pltpu.CompilerParams(
            collective_id=cid, has_side_effects=True, vmem_limit_bytes=16 << 20
        ),
    )(x)


def bias_rows(tiles_ref, kind_ref, head, block):
    kind = kind_ref[block : block + 1, :]
    rows = jnp.where(kind == 3, tiles_ref[head, 3], NEG)
    for k in (2, 1, 0):
        rows = jnp.where(kind == k, tiles_ref[head, k], rows)
    return rows


def attend_kernel(heads, proj_ref, tiles_ref, kind_ref, out_ref, s_ref, p_ref):
    width = heads * HEAD_DIM
    seq = proj_ref.shape[0]
    parts = []
    for h in range(heads):
        q = proj_ref[:, h * HEAD_DIM : (h + 1) * HEAD_DIM]
        k = proj_ref[:, width + h * HEAD_DIM : width + (h + 1) * HEAD_DIM]
        v = proj_ref[:, 2 * width + h * HEAD_DIM : 2 * width + (h + 1) * HEAD_DIM]
        s_ref[...] = mm_nt(q, k)
        for b in range(seq // SPAN):
            at = slice(b * SPAN, (b + 1) * SPAN)
            s = s_ref[at, :] * HEAD_DIM**-0.5 + bias_rows(tiles_ref, kind_ref, h, b)
            e = jnp.exp(s - jnp.max(s, -1, keepdims=True))
            p_ref[at, :] = (e * (1.0 / jnp.sum(e, -1, keepdims=True))).astype(BF16)
        parts.append(mm(p_ref[...], v).astype(BF16))
    out_ref[...] = jnp.concatenate(parts, 1)


def attend(proj, tiles, kind):
    seq, width = proj.shape
    heads = width // (3 * HEAD_DIM)
    vm = pl.BlockSpec(memory_space=pltpu.VMEM)
    return pl.pallas_call(
        functools.partial(attend_kernel, heads),
        out_shape=jax.ShapeDtypeStruct((seq, width // 3), BF16),
        in_specs=[vm] * 3,
        out_specs=vm,
        scratch_shapes=[pltpu.VMEM((seq, seq), F32), pltpu.VMEM((seq, seq), BF16)],
        compiler_params=pltpu.CompilerParams(vmem_limit_bytes=32 << 20),
    )(proj, tiles, kind)


def attend_back_kernel(
    heads, proj_ref, da_ref, tiles_ref, kind_ref, dproj_ref, dtiles_ref, s_ref, dp_ref, p_ref, ds_ref
):
    width = heads * HEAD_DIM
    seq = proj_ref.shape[0]
    scale = HEAD_DIM**-0.5
    dq, dk, dv = [], [], []
    for h in range(heads):
        q = proj_ref[:, h * HEAD_DIM : (h + 1) * HEAD_DIM]
        k = proj_ref[:, width + h * HEAD_DIM : width + (h + 1) * HEAD_DIM]
        v = proj_ref[:, 2 * width + h * HEAD_DIM : 2 * width + (h + 1) * HEAD_DIM]
        da = da_ref[:, h * HEAD_DIM : (h + 1) * HEAD_DIM]
        s_ref[...] = mm_nt(q, k)
        dp_ref[...] = mm_nt(da, v)
        dtiles_ref[h] = jnp.zeros(dtiles_ref.shape[1:], F32)
        for b in range(seq // SPAN):
            at = slice(b * SPAN, (b + 1) * SPAN)
            s = s_ref[at, :] * scale + bias_rows(tiles_ref, kind_ref, h, b)
            e = jnp.exp(s - jnp.max(s, -1, keepdims=True))
            p = e * (1.0 / jnp.sum(e, -1, keepdims=True))
            dp = dp_ref[at, :]
            ds = p * (dp - jnp.sum(p * dp, -1, keepdims=True))
            p_ref[at, :] = p.astype(BF16)
            ds_ref[at, :] = ds.astype(BF16)
            kind = kind_ref[b : b + 1, :]
            for n in range(KINDS):
                dtiles_ref[h, n] += jnp.where(kind == n, ds, 0.0)
        p = p_ref[...]
        ds = ds_ref[...]
        dq.append((mm(ds, k) * scale).astype(BF16))
        dk.append((mm_tn(ds, q) * scale).astype(BF16))
        dv.append(mm_tn(p, da).astype(BF16))
    dproj_ref[...] = jnp.concatenate(dq + dk + dv, 1)


def attend_back(proj, da, tiles, kind):
    seq, width = proj.shape
    heads = width // (3 * HEAD_DIM)
    vm = pl.BlockSpec(memory_space=pltpu.VMEM)
    return pl.pallas_call(
        functools.partial(attend_back_kernel, heads),
        out_shape=(
            jax.ShapeDtypeStruct((seq, width), BF16),
            jax.ShapeDtypeStruct(tiles.shape, F32),
        ),
        in_specs=[vm] * 4,
        out_specs=(vm, vm),
        scratch_shapes=[
            pltpu.VMEM((seq, seq), F32),
            pltpu.VMEM((seq, seq), F32),
            pltpu.VMEM((seq, seq), BF16),
            pltpu.VMEM((seq, seq), BF16),
        ],
        compiler_params=pltpu.CompilerParams(vmem_limit_bytes=32 << 20),
    )(proj, da, tiles, kind)


def bucket_of(distance):
    half = BUCKETS // 2
    powers = np.arange(1, BUCKETS - half) / (BUCKETS - half)
    bounds = np.ceil(half * (REACH / half) ** powers).astype(np.int32)
    n = np.maximum(distance, 0)
    return np.minimum(n, half) + (n[..., None] >= bounds).sum(-1)


def tile_buckets():
    row, col = np.arange(SPAN)[:, None], np.arange(SPAN)[None, :]
    return np.stack([bucket_of(k * SPAN + row - col) for k in range(KINDS)])


def bias_tiles(table, seq):
    hot = (tile_buckets()[..., None] == np.arange(BUCKETS)).astype(np.float32)
    hot = jnp.asarray(hot.reshape(KINDS * SPAN * SPAN, BUCKETS), BF16)
    tiles = mm_nt(table.T.astype(BF16), hot).reshape(-1, KINDS, SPAN, SPAN)
    row, col = np.arange(SPAN)[:, None], np.arange(SPAN)[None, :]
    unseen = np.zeros((KINDS, SPAN, SPAN), bool)
    unseen[0] = row < col
    tiles = jnp.where(jnp.asarray(unseen), NEG, tiles)
    return jnp.tile(tiles, (1, 1, 1, seq // SPAN))


def bias_tiles_back(dtiles):
    heads, kinds, span, seq = dtiles.shape
    hot = (tile_buckets()[..., None] == np.arange(BUCKETS)).astype(np.float32)
    hot = jnp.asarray(hot.reshape(KINDS * SPAN * SPAN, BUCKETS), BF16)
    sums = jnp.sum(dtiles.reshape(heads, kinds, span, seq // span, span), 3)
    sums = sums.reshape(heads, -1)
    high = sums.astype(BF16)
    low = (sums - high.astype(F32)).astype(BF16)
    return (mm(high, hot) + mm(low, hot)).T


def norm_scale(v):
    return lax.rsqrt(jnp.mean(v * v, -1, keepdims=True) + EPS)


def norm(v, gain):
    return (v * norm_scale(v) * gain).astype(BF16)


def norm_back(v, gain, du):
    r = norm_scale(v)
    dug = du * gain
    dv = r * dug - v * (r * r * r) * jnp.mean(dug * v, -1, keepdims=True)
    return dv, jnp.sum(du * v * r, 0)


def gelu_parts(v):
    t = jnp.tanh(GELU_C * (v + 0.044715 * v * v * v))
    value = 0.5 * v * (1.0 + t)
    slope = 0.5 * (1.0 + t) + 0.5 * v * (1.0 - t * t) * GELU_C * (1.0 + 3 * 0.044715 * v * v)
    return value, slope


def slot_tables(routes, experts, capacity):
    rows = routes.shape[0]
    flat = routes.reshape(rows * TOP)
    hot = flat[:, None] == jnp.arange(experts, dtype=jnp.int32)
    before = np.tril(np.ones((rows * TOP, rows * TOP), np.float32), -1)
    earlier = mm(jnp.asarray(before, BF16), hot.astype(BF16))
    slot = jnp.sum(jnp.where(hot, earlier, 0.0), -1).astype(jnp.int32)
    target = (flat * capacity + slot).reshape(rows, TOP)
    slots = jnp.arange(experts * capacity, dtype=jnp.int32)
    slot_hot = [(target[:, c : c + 1] == slots).astype(BF16) for c in range(TOP)]
    route_hot = [(routes[:, c : c + 1] == jnp.arange(experts)).astype(F32) for c in range(TOP)]
    return route_hot, slot_hot


def exp_swap(x):
    return lax.all_to_all(x, "exp", split_axis=0, concat_axis=0, tiled=True)


def on_device(
    inputs,
    cotangent,
    routes,
    block_order,
    attn_gain,
    qkv_weight,
    out_weight,
    rel_bias,
    moe_gain,
    router_weight,
    expert_in,
    expert_out,
):
    rows, width = inputs.shape[2:]
    n_ctx, n_exp = lax.axis_size("ctx"), lax.axis_size("exp")
    seq = rows * n_ctx
    own_rows = qkv_weight.shape[1]
    heads = HEADS // n_ctx
    part = heads * HEAD_DIM
    capacity = rows * TOP // n_exp + max(1, rows * TOP // (16 * n_exp))
    slots = n_exp * capacity
    section = lax.axis_index("section")
    ctx = lax.axis_index("ctx")
    first = section == 0

    def both(mine):
        other = lax.ppermute(mine, "section", [(0, 1), (1, 0)])
        return jnp.where(first, mine, other), jnp.where(first, other, mine)

    small = jnp.concatenate(
        [attn_gain[0], moe_gain[0], rel_bias[0], router_weight[0].reshape(-1)]
    )
    n_small = small.shape[0]
    columns = qkv_weight[0].reshape(own_rows, 3, n_ctx, part).transpose(2, 0, 1, 3)
    columns = columns.reshape(n_ctx, own_rows, 3 * part)
    small_row = jnp.pad(small, (0, 3 * part - n_small))
    small_rows = jnp.broadcast_to(small_row, (n_ctx, 1, 3 * part))
    columns = jnp.concatenate([columns, small_rows], 1)
    columns = jnp.pad(columns, ((0, 0), (0, 15 - own_rows), (0, 0)))
    columns = lax.all_to_all(columns, "ctx", 0, 0, tiled=True)
    columns = lax.all_gather(columns.reshape(n_ctx * 16, 3 * part), "exp", axis=0)
    out_rows = lax.all_gather(jnp.pad(out_weight[0], ((0, 4), (0, 0))), "exp", axis=0)

    def dense(columns, out_rows):
        columns = columns.reshape(n_exp, n_ctx, 16, 3 * part).transpose(1, 0, 2, 3)
        w_qkv = columns[:, :, :own_rows].reshape(width, 3 * part)
        w_out = out_rows[:, :own_rows].reshape(part, width)
        small = columns[:, :, own_rows, :n_small]
        gain_one = small[:, :, :own_rows].reshape(width).astype(F32)
        gain_two = small[:, :, own_rows : 2 * own_rows].reshape(width).astype(F32)
        n_bias = BUCKETS * HEADS // (n_ctx * n_exp)
        table = small[:, :, 2 * own_rows : 2 * own_rows + n_bias].reshape(BUCKETS, HEADS)
        table = lax.dynamic_slice_in_dim(table, ctx * heads, heads, 1)
        router = small[:, :, 2 * own_rows + n_bias :].reshape(width, n_exp)
        return w_qkv, w_out, gain_one, gain_two, bias_tiles(table, seq), router

    weights = [
        (*dense(c, o), w_in, w_out)
        for c, o, w_in, w_out in zip(
            both(columns), both(out_rows), both(expert_in[0, 0]), both(expert_out[0, 0])
        )
    ]
    ahead = block_order[:, None] - block_order[None, :]
    kind = jnp.repeat(jnp.where(ahead < 0, -1, jnp.minimum(ahead, 3)), SPAN, 1)

    own_routes = routes[0, :, 0]
    kept = jnp.where(first, own_routes[0], own_routes[1])
    given = jnp.where(first, own_routes[1], own_routes[0])
    taken = lax.ppermute(given, "section", [(0, 1), (1, 0)])
    layer_routes = (jnp.where(first, kept, taken), jnp.where(first, taken, kept))
    tables = [slot_tables(r, n_exp, capacity) for r in layer_routes]

    def forward(x, layer):
        w_qkv, w_out, gain_one, gain_two, tiles, router, w_in, w_back = weights[layer]
        route_hot, slot_hot = tables[layer]
        normed = ctx_gather(norm(x, gain_one), 0).reshape(seq, width)
        proj = mm(normed, w_qkv).astype(BF16)
        attended = attend(proj, tiles, kind)
        branch = mm(attended, w_out).astype(BF16).reshape(n_ctx, rows, width)
        middle = x + ctx_scatter(branch, F32, 1)
        mixed = norm(middle, gain_two)
        logits = mm(mixed, router)
        chosen = [jnp.sum(h * logits, -1, keepdims=True) for h in route_hot]
        peak = jnp.maximum(chosen[0], chosen[1])
        raised = [jnp.exp(c - peak) for c in chosen]
        gates = [r / (raised[0] + raised[1]) for r in raised]
        placing = slot_hot[0] + slot_hot[1]
        outgoing = mm_tn(placing, mixed).astype(BF16).reshape(n_exp, capacity, width)
        entering = exp_swap(outgoing).reshape(slots, width)
        entering = ctx_gather(entering, 2).reshape(n_ctx * slots, width)
        pre = mm(entering, w_in)
        hidden = gelu_parts(pre)[0].astype(BF16)
        leaving = mm_nt(hidden, w_back).astype(BF16).reshape(n_ctx, slots, width)
        leaving = ctx_scatter(leaving, BF16, 3).reshape(n_exp, capacity, width)
        returned = exp_swap(leaving).reshape(slots, width)
        picked = [mm(h, returned) for h in slot_hot]
        y = middle + gates[0] * picked[0] + gates[1] * picked[1]
        keep = (x, normed, proj, attended, middle, mixed, gates, picked, entering, pre)
        return y, keep

    def backward(g, keep, layer):
        x, normed, proj, attended, middle, mixed, gates, picked, entering, pre = keep
        w_qkv, w_out, gain_one, gain_two, tiles, router, w_in, w_back = weights[layer]
        route_hot, slot_hot = tables[layer]
        dreturned = mm_tn(slot_hot[0], (gates[0] * g).astype(BF16)) + mm_tn(
            slot_hot[1], (gates[1] * g).astype(BF16)
        )
        dreturned = dreturned.astype(BF16).reshape(n_exp, capacity, width)
        darrived = exp_swap(dreturned).reshape(slots, width)
        darrived = ctx_gather(darrived, 2).reshape(n_ctx * slots, width)
        hidden, slope = gelu_parts(pre)
        dpre = (mm(darrived, w_back) * slope).astype(BF16)
        dentering = mm_nt(dpre, w_in).astype(BF16).reshape(n_ctx, slots, width)
        dentering = ctx_scatter(dentering, BF16, 3).reshape(n_exp, capacity, width)
        dleft = exp_swap(dentering).reshape(slots, width)
        d_in = mm_tn(entering, dpre)
        d_back = mm_tn(darrived, hidden.astype(BF16))
        dgates = [jnp.sum(g * p, -1, keepdims=True) for p in picked]
        mean = gates[0] * dgates[0] + gates[1] * dgates[1]
        dchosen = [a * (b - mean) for a, b in zip(gates, dgates)]
        dlogits = route_hot[0] * dchosen[0] + route_hot[1] * dchosen[1]
        dlogits = dlogits.astype(BF16)
        d_router = mm_tn(mixed, dlogits)
        dmixed = mm(slot_hot[0] + slot_hot[1], dleft) + mm_nt(dlogits, router)
        dnorm, d_gain_two = norm_back(middle, gain_two, dmixed)
        dmiddle = g + dnorm
        dbranch = ctx_gather(dmiddle.astype(BF16), 0).reshape(seq, width)
        d_out = mm_tn(attended, dbranch)
        dattended = mm_nt(dbranch, w_out).astype(BF16)
        dproj, dtiles = attend_back(proj, dattended, tiles, kind)
        d_qkv = mm_tn(normed, dproj)
        dnormed = mm_nt(dproj, w_qkv).astype(BF16).reshape(n_ctx, rows, width)
        dnormed = ctx_scatter(dnormed, F32, 1)
        dnorm, d_gain_one = norm_back(x, gain_one, dnormed)
        d_table = bias_tiles_back(dtiles)
        full = jnp.zeros((BUCKETS, HEADS), F32)
        d_table = lax.dynamic_update_slice_in_dim(full, d_table, ctx * heads, 1)
        owners = (n_ctx * n_exp, -1)
        d_small = jnp.concatenate(
            [
                d_gain_one.reshape(owners),
                d_gain_two.reshape(owners),
                d_table.reshape(owners),
                d_router.reshape(owners),
            ],
            1,
        )
        return dmiddle + dnorm, (d_in, d_back, d_qkv, d_out, d_small)

    def swap(x):
        return lax.ppermute(x, "section", [(0, 1), (1, 0)])

    x = jnp.where(first, inputs[0, 0], inputs[1, 0]).astype(F32)
    cot = jnp.where(first, cotangent[0, 0], cotangent[1, 0]).astype(F32)
    y0, keep0 = forward(x, 0)
    h = y0.astype(BF16)
    y1, keep1 = forward(h.astype(F32), 1)
    top = y1.astype(BF16)
    dh, grads1 = backward(cot, keep1, 1)
    dh = dh.astype(BF16)
    sent1 = [lax.ppermute(p.astype(BF16), "section", [(0, 1)]) for p in grads1]
    dx, grads0 = backward(dh.astype(F32), keep0, 0)
    sent0 = [lax.ppermute(p.astype(BF16), "section", [(1, 0)]) for p in grads0]
    d_in, d_back, d_qkv, d_out, d_small = [
        jnp.where(first, a, b) + (c.astype(F32) + d.astype(F32))
        for a, b, c, d in zip(grads0, grads1, sent0, sent1)
    ]

    d_qkv = d_qkv.reshape(n_ctx, n_exp, own_rows, 3 * part).transpose(1, 0, 2, 3)
    d_small = d_small.reshape(n_ctx, n_exp, -1).transpose(1, 0, 2)
    d_small = jnp.pad(d_small, ((0, 0), (0, 0), (0, 3 * part - n_small)))
    pieces = jnp.concatenate([d_qkv, d_small[:, :, None]], 2).astype(BF16)
    pieces = jnp.sum(exp_swap(pieces).astype(F32), 0)
    pieces = lax.all_to_all(pieces, "ctx", 0, 0, tiled=True)
    qkv_grad = pieces[:, :own_rows].reshape(n_ctx, own_rows, 3, part)
    qkv_grad = qkv_grad.transpose(1, 2, 0, 3).reshape(own_rows, 3 * width)
    small = jnp.sum(pieces[:, own_rows, :n_small], 0)
    n_bias = BUCKETS * HEADS // (n_ctx * n_exp)
    out_grad = exp_swap(d_out.reshape(n_exp, own_rows, width).astype(BF16))
    out_grad = jnp.sum(out_grad.astype(F32), 0)

    other = swap(jnp.where(first, top, h))
    layer_out = jnp.where(
        first, jnp.stack([h, other]), jnp.stack([other, top])
    ).reshape(1, 2, 1, rows, width)
    dh = dh.astype(F32)
    other = swap(jnp.where(first, dh, dx))
    input_grad = jnp.where(
        first, jnp.stack([dx, other]), jnp.stack([other, dh])
    ).reshape(1, 2, 1, rows, width)
    return (
        layer_out,
        input_grad,
        small[:own_rows][None],
        qkv_grad[None],
        out_grad[None],
        small[2 * own_rows : 2 * own_rows + n_bias][None],
        small[own_rows : 2 * own_rows][None],
        small[2 * own_rows + n_bias :].reshape(1, own_rows, n_exp),
        d_in[None, None],
        d_back[None, None],
    )


def solution(mesh):
    return jax.shard_map(
        on_device,
        mesh=mesh,
        in_specs=(
            P(None, "exp", "ctx", None),
            P(None, "exp", "ctx", None),
            P("section", None, "exp", "ctx", None),
            P(),
            P("section", ("ctx", "exp")),
            P("section", ("ctx", "exp"), None),
            P("section", ("ctx", "exp"), None),
            P("section", ("ctx", "exp")),
            P("section", ("ctx", "exp")),
            P("section", ("ctx", "exp"), None),
            P("section", "exp", None, "ctx"),
            P("section", "exp", None, "ctx"),
        ),
        out_specs=(
            P("section", None, "exp", "ctx", None),
            P("section", None, "exp", "ctx", None),
            P("section", ("ctx", "exp")),
            P("section", ("ctx", "exp"), None),
            P("section", ("ctx", "exp"), None),
            P("section", ("ctx", "exp")),
            P("section", ("ctx", "exp")),
            P("section", ("ctx", "exp"), None),
            P("section", "exp", None, "ctx"),
            P("section", "exp", None, "ctx"),
        ),
        check_vma=False,
    )
```

time: 1860 us -> 655 us (0.35)
  the two profiles are of different devices: /device:TPU:2 before, /device:TPU:0 now
where the time goes in v1:
time: 655 us; the launch traced here: 643 us
  Pallas kernels  205 us (31%)
  matrix products  94.8 us (14%)
  local copies, waits for them, and re-layouts  90.5 us (14%)
  starting transfers between devices  74.1 us (11%)
  waiting for transfers between devices  63.5 us (10%)
  blocking collectives  53.4 us (8%)
  other arithmetic  45.2 us (7%)
  between operations  16.8 us (3%)
    pallas_call x8, Pallas kernels, ctx_scatter(): pl.pallas_call(functools.partial(scatter_kernel, 'ctx', rows), out_shape=...  96.3 us
    dot_general x50, matrix products, dot(): return lax.dot_general(a, b, (dims, ((), ())), preferred_element_type=F32)  94.8 us
    pallas_call x8, Pallas kernels, ctx_gather(): pl.pallas_call(functools.partial(gather_kernel, 'ctx', rows), out_shape=j...  94.3 us
    all_to_all x9, starting transfers between devices, exp_swap(): return lax.all_to_all(x, 'exp', split_axis=0, concat_axis=0, tiled=True)  45.7 us
    all_to_all x9, waiting for transfers between devices, exp_swap(): return lax.all_to_all(x, 'exp', split_axis=0, concat_axis=0, tiled=True)  45.4 us
    all_gather x1, blocking collectives, on_device(): lax.all_gather(jnp.pad(out_weight[0], ((0, 4), (0, 0))), 'exp', axis=0)  24.5 us
    all_to_all x1, blocking collectives, exp_swap(): return lax.all_to_all(x, 'exp', split_axis=0, concat_axis=0, tiled=True)  17.9 us
    ppermute x5, starting transfers between devices, on_device(): sent1 = [lax.ppermute(p.astype(BF16), 'section', [(0, 1)]) for p in grads1]  17.2 us
  transfers between devices with their start and end apart: 28, of which 8 were waited for; matrix products, arithmetic and copies ran while one was open for 28% of the time, Pallas kernels for 22%

profile of v1, /device:TPU:0, one launch (start us, length us, event | category | flops | bytes accessed | tf_op | source)
XLA Modules:
  0.0 643.1 jit_solution(12003461093903902969)
XLA Ops:
  10.1 11.0 %all_to_all.60 = bf16[4,16,576]{2,1,0:T(8,128)(2,1)} all-to-all(bf16[4,16,576]{2,1,0:T(8,128)(2,1)S(1)} %pad.18.clone), channel_id=1, replica_groups=mesh['section'=2,'ctx'=4,'exp'=16] {'ctx'}, dimensions={0} | all-to-all | bytes 147456 | tf_op jit(solution)/shard_map/all_to_all | solution.py:395
  23.0 24.5 %all-gather = bf16[256,768]{1,0:T(8,128)(2,1)S(1)} all-gather(bf16[16,768]{1,0:T(8,128)(2,1)S(1)} %pad.19), channel_id=2, replica_groups=mesh['section'=2,'ctx'=4,'exp'=16] {'exp'}, dimensions={0}, use_global_device_ids=true | all-gather | bytes 417792 | tf_op jit(solution)/shard_map/all_gather | solution.py:397
  48.3 15.8 %all-gather.3.cloned.1.call-done = bf16[16,64,576]{2,1,0:T(8,128)(2,1)} async-done(((bf16[1,64,576]{2,1,0:T(8,128)(2,1)}), bf16[16,64,576]{2,1,0:T(8,128)(2,1)}) %all-gather.3.cloned.1.call-update) | async-done | bytes 1179664 | tf_op jit(solution)/shard_map/all_gather | solution.py:396
  72.0 11.4 %shard_map.267 = bf16[4,128,768]{2,1,0:T(8,128)(2,1)S(1)} custom-call(bf16[128,768]{1,0:T(8,128)(2,1)S(1)} %fusion.36.x_ref), custom_call_target="tpu_custom_call" | custom-call | tf_op jit(solution)/shard_map/pallas_call | solution.py:103
  101.5 11.1 %shard_map.269 = f32[128,768]{1,0:T(8,128)S(1)} custom-call(bf16[4,128,768]{2,1,0:T(8,128)(2,1)S(1)} %bitcast.216), custom_call_target="tpu_custom_call" | custom-call | tf_op jit(solution)/shard_map/pallas_call | solution.py:162
  115.0 5.1 all-to-all-start.1
  123.4 7.1 %all-to-all-done.1 = bf16[16,17,768]{2,1,0:T(8,128)(2,1)S(1)} async-done(((bf16[16,17,768]{2,1,0:T(8,128)(2,1)}), bf16[16,17,768]{2,1,0:T(8,128)(2,1)S(1)}, u32[]{:S(2)}, u32[]{:S(2)}) %all-to-all-start.1) | async-done | bytes 417824 | tf_op jit(solution)/shard_map/all_to_all | solution.py:352
  130.7 14.2 %shard_map.270 = bf16[4,272,768]{2,1,0:T(8,128)(2,1)S(1)} custom-call(bf16[272,768]{1,0:T(8,128)(2,1)S(1)} %reshape.597.x_ref), custom_call_target="tpu_custom_call" | custom-call | tf_op jit(solution)/shard_map/pallas_call | solution.py:103
  152.6 14.8 %shard_map.271 = bf16[272,768]{1,0:T(8,128)(2,1)S(1)} custom-call(bf16[4,272,768]{2,1,0:T(8,128)(2,1)S(1)} %bitcast.231), custom_call_target="tpu_custom_call" | custom-call | tf_op jit(solution)/shard_map/pallas_call | solution.py:162
  190.7 9.5 %shard_map.272 = bf16[4,128,768]{2,1,0:T(8,128)(2,1)S(1)} custom-call(bf16[128,768]{1,0:T(8,128)(2,1)S(1)} %fusion.26.x_ref), custom_call_target="tpu_custom_call" | custom-call | tf_op jit(solution)/shard_map/pallas_call | solution.py:103
  204.8 9.9 %shard_map.274 = f32[128,768]{1,0:T(8,128)S(1)} custom-call(bf16[4,128,768]{2,1,0:T(8,128)(2,1)S(1)} %bitcast.217), custom_call_target="tpu_custom_call" | custom-call | tf_op jit(solution)/shard_map/pallas_call | solution.py:162
  219.4 17.9 %all_to_all.61 = bf16[16,17,768]{2,1,0:T(8,128)(2,1)} all-to-all(bf16[16,17,768]{2,1,0:T(8,128)(2,1)} %reshape.610), channel_id=1, replica_groups=mesh['section'=2,'ctx'=4,'exp'=16] {'exp'}, dimensions={0} | all-to-all | bytes 835584 | tf_op jit(solution)/shard_map/all_to_all | solution.py:352
  240.2 12.0 %shard_map.275 = bf16[4,272,768]{2,1,0:T(8,128)(2,1)S(1)} custom-call(bf16[272,768]{1,0:T(8,128)(2,1)S(1)} %copy-done.15), custom_call_target="tpu_custom_call" | custom-call | tf_op jit(solution)/shard_map/pallas_call | solution.py:103
  261.6 12.4 %shard_map.276 = bf16[272,768]{1,0:T(8,128)(2,1)S(1)} custom-call(bf16[4,272,768]{2,1,0:T(8,128)(2,1)S(1)} %bitcast.232), custom_call_target="tpu_custom_call" | custom-call | tf_op jit(solution)/shard_map/pallas_call | solution.py:162
  283.2 8.3 %all-to-all-done.4 = bf16[16,17,768]{2,1,0:T(8,128)(2,1)} async-done(((bf16[16,17,768]{2,1,0:T(8,128)(2,1)}), bf16[16,17,768]{2,1,0:T(8,128)(2,1)}, u32[]{:S(2)}, u32[]{:S(2)}) %all-to-all-start.4) | async-done | bytes 417824 | tf_op jit(solution)/shard_map/all_to_all | solution.py:352
  308.3 10.1 %all-to-all-done.5 = bf16[16,17,768]{2,1,0:T(8,128)(2,1)} async-done(((bf16[16,17,768]{2,1,0:T(8,128)(2,1)}), bf16[16,17,768]{2,1,0:T(8,128)(2,1)}, u32[]{:S(2)}, u32[]{:S(2)}) %all-to-all-start.5) | async-done | bytes 417824 | tf_op jit(solution)/shard_map/all_to_all | solution.py:352
  321.4 16.8 %shard_map.277 = bf16[4,272,768]{2,1,0:T(8,128)(2,1)S(1)} custom-call(bf16[272,768]{1,0:T(8,128)(2,1)S(1)} %copy-done.17), custom_call_target="tpu_custom_call" | custom-call | tf_op jit(solution)/shard_map/pallas_call | solution.py:103
  338.2 5.8 fusion.146
  352.6 15.4 %shard_map.278 = bf16[272,768]{1,0:T(8,128)(2,1)S(1)} custom-call(bf16[4,272,768]{2,1,0:T(8,128)(2,1)S(1)} %bitcast.233), custom_call_target="tpu_custom_call" | custom-call | tf_op jit(solution)/shard_map/pallas_call | solution.py:162
  375.4 5.5 fusion.144
  392.3 8.9 %shard_map.279 = bf16[4,128,768]{2,1,0:T(8,128)(2,1)S(1)} custom-call(bf16[128,768]{1,0:T(8,128)(2,1)S(1)} %get-tuple-element.86.x_ref), custom_call_target="tpu_custom_call" | custom-call | tf_op jit(solution)/shard_map/pallas_call | solution.py:103
  415.5 10.5 %shard_map.281 = f32[128,768]{1,0:T(8,128)S(1)} custom-call(bf16[4,128,768]{2,1,0:T(8,128)(2,1)S(1)} %bitcast.235), custom_call_target="tpu_custom_call" | custom-call | tf_op jit(solution)/shard_map/pallas_call | solution.py:162
  456.6 11.9 %shard_map.282 = bf16[4,272,768]{2,1,0:T(8,128)(2,1)S(1)} custom-call(bf16[272,768]{1,0:T(8,128)(2,1)S(1)} %reshape.625.x_ref), custom_call_target="tpu_custom_call" | custom-call | tf_op jit(solution)/shard_map/pallas_call | solution.py:103
  468.5 5.8 fusion.147
  482.3 12.7 %shard_map.283 = bf16[272,768]{1,0:T(8,128)(2,1)S(1)} custom-call(bf16[4,272,768]{2,1,0:T(8,128)(2,1)S(1)} %bitcast.230), custom_call_target="tpu_custom_call" | custom-call | tf_op jit(solution)/shard_map/pallas_call | solution.py:162
  497.6 7.5 %all-to-all-start.8 = ((bf16[16,17,768]{2,1,0:T(8,128)(2,1)}), bf16[16,17,768]{2,1,0:T(8,128)(2,1)}, u32[]{:S(2)}, u32[]{:S(2)}) async-start(bf16[16,17,768]{2,1,0:T(8,128)(2,1)} %reshape.628), calls=%async_computation.8 | async-start | bytes 1179648 | tf_op jit(solution)/shard_map/all_to_all | solution.py:352
  510.3 5.4 all-to-all-done.8
  519.1 9.7 %shard_map.284 = bf16[4,128,768]{2,1,0:T(8,128)(2,1)S(1)} custom-call(bf16[128,768]{1,0:T(8,128)(2,1)S(1)} %get-tuple-element.84.x_ref), custom_call_target="tpu_custom_call" | custom-call | tf_op jit(solution)/shard_map/pallas_call | solution.py:103
  540.8 9.5 %shard_map.286 = f32[128,768]{1,0:T(8,128)S(1)} custom-call(bf16[4,128,768]{2,1,0:T(8,128)(2,1)S(1)} %bitcast.234), custom_call_target="tpu_custom_call" | custom-call | tf_op jit(solution)/shard_map/pallas_call | solution.py:162
  581.7 5.0 collective-permute-start.16
  595.0 6.9 %all-to-all-start.9 = ((bf16[16,4,13,576]{3,1,2,0:T(4,128)(2,1)}), bf16[16,4,13,576]{3,1,2,0:T(4,128)(2,1)S(1)}, u32[]{:S(2)}, u32[]{:S(2)}) async-start(bf16[16,4,13,576]{3,1,2,0:T(4,128)(2,1)} %copy.133), calls=%async_computation.9 | async-start | bytes 2129920 | tf_op jit(solution)/shard_map/all_to_all | solution.py:352
  612.0 9.6 %all-to-all-done.9 = bf16[16,4,13,576]{3,1,2,0:T(4,128)(2,1)S(1)} async-done(((bf16[16,4,13,576]{3,1,2,0:T(4,128)(2,1)}), bf16[16,4,13,576]{3,1,2,0:T(4,128)(2,1)S(1)}, u32[]{:S(2)}, u32[]{:S(2)}) %all-to-all-start.9) | async-done | bytes 958496 | tf_op jit(solution)/shard_map/all_to_all | solution.py:352
  (524 shorter events, 284.5 us)
Async XLA Ops:
  7.2 57.9 %copy-start.71 = (bf16[256,256]{1,0:T(8,128)(2,1)S(1)}, bf16[256,256]{1,0:T(8,128)(2,1)}, u32[]{:S(2)}) copy-start(bf16[256,256]{1,0:T(8,128)(2,1)} %constant.71.clone) | copy-start | bytes 393220
  7.2 41.0 %copy-start.125 = (s32[8]{0:T(128)S(1)}, s32[8]{0:T(128)}, u32[]{:S(2)}) copy-start(s32[8]{0:T(128)} %param.23) | copy-start | bytes 100
  7.2 56.9 %all-gather.3.cloned.1.call-start = ((), (), s32[]{:S(2)}) async-start(), calls=%async_computation.12 | async-start | bytes 1392640 | tf_op jit(solution)/shard_map/all_gather | solution.py:396
  22.1 42.6 %collective-permute-start.2 = (s32[128,2]{1,0:T(8,128)S(1)}, s32[128,2]{1,0:T(8,128)S(1)}, u32[]{:S(2)}, u32[]{:S(2)}) collective-permute-start(s32[128,2]{1,0:T(8,128)S(1)} %select_bitcast_fusion), channel_id=1, source_target_pairs={{0,64},{64,0},{1,65},{65,1},{2,66},{66,2},{3,67},{67,3},{4,68},{68... | collective-permute-start | bytes 3080 | tf_op jit(solution)/shard_map/ppermute | solution.py:424
  47.5 19.7 %collective-permute-start.1 = (bf16[16,16,768]{2,1,0:T(8,128)(2,1)S(1)}, bf16[16,16,768]{2,1,0:T(8,128)(2,1)S(1)}, u32[]{:S(2)}, u32[]{:S(2)}) collective-permute-start(bf16[16,16,768]{2,1,0:T(8,128)(2,1)S(1)} %bitcast.242), channel_id=1, source_target_pairs={{0,64},{64,0},{1,65},{65,1},{2,66},{66,2},{3,67},{67,3},{4,68},{68... | collective-permute-start | bytes 1179656 | tf_op jit(solution)/shard_map/ppermute | solution.py:382
  47.5 100.8 %collective-permute-start.4 = (bf16[768,768]{1,0:T(8,128)(2,1)}, bf16[768,768]{1,0:T(8,128)(2,1)}, u32[]{:S(2)}, u32[]{:S(2)}) collective-permute-start(bf16[768,768]{1,0:T(8,128)(2,1)} %bitcast.19), channel_id=1, source_target_pairs={{0,64},{64,0},{1,65},{65,1},{2,66},{66,2},{3,67},{67,3},{4,68},{68... | collective-permute-start | bytes 3538952 | tf_op jit(solution)/shard_map/ppermute | solution.py:382
  48.0 96.9 %collective-permute-start.3 = (bf16[768,768]{1,0:T(8,128)(2,1)}, bf16[768,768]{1,0:T(8,128)(2,1)}, u32[]{:S(2)}, u32[]{:S(2)}) collective-permute-start(bf16[768,768]{1,0:T(8,128)(2,1)} %bitcast.18), channel_id=1, source_target_pairs={{0,64},{64,0},{1,65},{65,1},{2,66},{66,2},{3,67},{67,3},{4,68},{68... | collective-permute-start | bytes 3538952 | tf_op jit(solution)/shard_map/ppermute | solution.py:382
  48.2 64.4 %copy-start.42 = (bf16[1,1,128,768]{3,2,1,0:T(8,128)(2,1)}, bf16[1,1,128,768]{3,2,1,0:T(8,128)(2,1)S(1)}, u32[]{:S(2)}) copy-start(bf16[1,1,128,768]{3,2,1,0:T(8,128)(2,1)S(1)} %get-tuple-element.101) | copy-start | bytes 589828
  64.1 4.0 collective-permute-start
  115.0 15.5 %all-to-all-start.1 = ((bf16[16,17,768]{2,1,0:T(8,128)(2,1)}), bf16[16,17,768]{2,1,0:T(8,128)(2,1)S(1)}, u32[]{:S(2)}, u32[]{:S(2)}) async-start(bf16[16,17,768]{2,1,0:T(8,128)(2,1)} %reshape.596), calls=%async_computation.1 | async-start | bytes 1179648 | tf_op jit(solution)/shard_map/all_to_all | solution.py:352
  168.4 15.9 %all-to-all-start.2 = ((bf16[16,17,768]{2,1,0:T(8,128)(2,1)}), bf16[16,17,768]{2,1,0:T(8,128)(2,1)}, u32[]{:S(2)}, u32[]{:S(2)}) async-start(bf16[16,17,768]{2,1,0:T(8,128)(2,1)} %reshape.600), calls=%async_computation.2 | async-start | bytes 1179648 | tf_op jit(solution)/shard_map/all_to_all | solution.py:352
  276.8 14.7 %all-to-all-start.4 = ((bf16[16,17,768]{2,1,0:T(8,128)(2,1)}), bf16[16,17,768]{2,1,0:T(8,128)(2,1)}, u32[]{:S(2)}, u32[]{:S(2)}) async-start(bf16[16,17,768]{2,1,0:T(8,128)(2,1)} %reshape.614), calls=%async_computation.4 | async-start | bytes 1179648 | tf_op jit(solution)/shard_map/all_to_all | solution.py:352
  297.4 294.0 %collective-permute-start.5 = (bf16[128,768]{1,0:T(8,128)(2,1)}, bf16[128,768]{1,0:T(8,128)(2,1)}, u32[]{:S(2)}, u32[]{:S(2)}) collective-permute-start(bf16[128,768]{1,0:T(8,128)(2,1)} %get-tuple-element.92), channel_id=1, source_target_pairs={{0,64},{64,0},{1,65},{65,1},{2,66},{66,2},{3,67},{67,3},{4,68},{68... | collective-permute-start | bytes 589832 | tf_op jit(solution)/shard_map/ppermute | solution.py:506
  300.9 17.5 %all-to-all-start.5 = ((bf16[16,17,768]{2,1,0:T(8,128)(2,1)}), bf16[16,17,768]{2,1,0:T(8,128)(2,1)}, u32[]{:S(2)}, u32[]{:S(2)}) async-start(bf16[16,17,768]{2,1,0:T(8,128)(2,1)} %reshape.616), calls=%async_computation.5 | async-start | bytes 1179648 | tf_op jit(solution)/shard_map/all_to_all | solution.py:352
  308.3 138.7 %copy-start.67 = (f32[64,192]{1,0:T(8,128)}, f32[64,192]{1,0:T(8,128)S(1)}, u32[]{:S(2)}) copy-start(f32[64,192]{1,0:T(8,128)S(1)} %reshape.644) | copy-start | bytes 147460
  370.7 15.1 %all-to-all-start.6 = ((bf16[16,17,768]{2,1,0:T(8,128)(2,1)}), bf16[16,17,768]{2,1,0:T(8,128)(2,1)}, u32[]{:S(2)}, u32[]{:S(2)}) async-start(bf16[16,17,768]{2,1,0:T(8,128)(2,1)} %reshape.620), calls=%async_computation.6 | async-start | bytes 1179648 | tf_op jit(solution)/shard_map/all_to_all | solution.py:352
  431.6 23.8 %all-to-all-start.7 = ((bf16[16,17,768]{2,1,0:T(8,128)(2,1)}), bf16[16,17,768]{2,1,0:T(8,128)(2,1)}, u32[]{:S(2)}, u32[]{:S(2)}) async-start(bf16[16,17,768]{2,1,0:T(8,128)(2,1)} %reshape.624), calls=%async_computation.7 | async-start | bytes 1179648 | tf_op jit(solution)/shard_map/all_to_all | solution.py:352
  447.7 113.5 %collective-permute-start.10 = (bf16[64,222]{1,0:T(8,128)(2,1)}, bf16[64,222]{1,0:T(8,128)(2,1)}, u32[]{:S(2)}, u32[]{:S(2)}) collective-permute-start(bf16[64,222]{1,0:T(8,128)(2,1)} %fusion.131), channel_id=1, source_target_pairs={{0,64},{1,65},{2,66},{3,67},{4,68},{5,69},{6,70},{7,71},{8,72},{9,... | collective-permute-start | bytes 85256 | tf_op jit(solution)/shard_map/ppermute | solution.py:516
  451.8 129.9 %collective-permute-start.8 = (bf16[768,576]{0,1:T(8,128)(2,1)}, bf16[768,576]{0,1:T(8,128)(2,1)}, u32[]{:S(2)}, u32[]{:S(2)}) collective-permute-start(bf16[768,576]{0,1:T(8,128)(2,1)} %get-tuple-element.136), channel_id=1, source_target_pairs={{0,64},{1,65},{2,66},{3,67},{4,68},{5,69},{6,70},{7,71},{8,72},{9,... | collective-permute-start | bytes 2654216 | tf_op jit(solution)/shard_map/ppermute | solution.py:516
  497.6 18.0 %all-to-all-start.8 = ((bf16[16,17,768]{2,1,0:T(8,128)(2,1)}), bf16[16,17,768]{2,1,0:T(8,128)(2,1)}, u32[]{:S(2)}, u32[]{:S(2)}) async-start(bf16[16,17,768]{2,1,0:T(8,128)(2,1)} %reshape.628), calls=%async_computation.8 | async-start | bytes 1179648 | tf_op jit(solution)/shard_map/all_to_all | solution.py:352
  557.3 29.4 %collective-permute-start.7 = (bf16[768,576]{0,1:T(8,128)(2,1)}, bf16[768,576]{0,1:T(8,128)(2,1)}, u32[]{:S(2)}, u32[]{:S(2)}) collective-permute-start(bf16[768,576]{0,1:T(8,128)(2,1)} %get-tuple-element.138), channel_id=1, source_target_pairs={{64,0},{65,1},{66,2},{67,3},{68,4},{69,5},{70,6},{71,7},{72,8},{73... | collective-permute-start | bytes 2654216 | tf_op jit(solution)/shard_map/ppermute | solution.py:518
  558.7 6.4 collective-permute-start.9
  561.2 7.0 %collective-permute-start.12 = (bf16[192,768]{1,0:T(8,128)(2,1)S(1)}, bf16[192,768]{1,0:T(8,128)(2,1)S(1)}, u32[]{:S(2)}, u32[]{:S(2)}) collective-permute-start(bf16[192,768]{1,0:T(8,128)(2,1)S(1)} %copy-done.81), channel_id=1, source_target_pairs={{0,64},{1,65},{2,66},{3,67},{4,68},{5,69},{6,70},{7,71},{8,72},{9,... | collective-permute-start | bytes 884744 | tf_op jit(solution)/shard_map/ppermute | solution.py:516
  565.1 7.2 %collective-permute-start.11 = (bf16[192,768]{1,0:T(8,128)(2,1)S(1)}, bf16[192,768]{1,0:T(8,128)(2,1)S(1)}, u32[]{:S(2)}, u32[]{:S(2)}) collective-permute-start(bf16[192,768]{1,0:T(8,128)(2,1)S(1)} %get-tuple-element.142), channel_id=1, source_target_pairs={{64,0},{65,1},{66,2},{67,3},{68,4},{69,5},{70,6},{71,7},{72,8},{73... | collective-permute-start | bytes 884744 | tf_op jit(solution)/shard_map/ppermute | solution.py:518
  568.2 39.5 %collective-permute-start.14 = (bf16[768,768]{1,0:T(8,128)(2,1)}, bf16[768,768]{1,0:T(8,128)(2,1)}, u32[]{:S(2)}, u32[]{:S(2)}) collective-permute-start(bf16[768,768]{1,0:T(8,128)(2,1)} %get-tuple-element.144), channel_id=1, source_target_pairs={{0,64},{1,65},{2,66},{3,67},{4,68},{5,69},{6,70},{7,71},{8,72},{9,... | collective-permute-start | bytes 3538952 | tf_op jit(solution)/shard_map/ppermute | solution.py:516
  572.3 35.4 %collective-permute-start.13 = (bf16[768,768]{1,0:T(8,128)(2,1)}, bf16[768,768]{1,0:T(8,128)(2,1)}, u32[]{:S(2)}, u32[]{:S(2)}) collective-permute-start(bf16[768,768]{1,0:T(8,128)(2,1)} %get-tuple-element.146), channel_id=1, source_target_pairs={{64,0},{65,1},{66,2},{67,3},{68,4},{69,5},{70,6},{71,7},{72,8},{73... | collective-permute-start | bytes 3538952 | tf_op jit(solution)/shard_map/ppermute | solution.py:518
  577.4 17.5 %all-to-all-start.11 = ((bf16[16,12,768]{2,1,0:T(8,128)(2,1)}), bf16[16,12,768]{2,1,0:T(8,128)(2,1)}, u32[]{:S(2)}, u32[]{:S(2)}) async-start(bf16[16,12,768]{2,1,0:T(8,128)(2,1)} %convert_element_type.374), calls=%async_computation.11 | async-start | bytes 786432 | tf_op jit(solution)/shard_map/all_to_all | solution.py:352
  581.7 45.0 %collective-permute-start.16 = (bf16[768,768]{1,0:T(8,128)(2,1)}, bf16[768,768]{1,0:T(8,128)(2,1)}, u32[]{:S(2)}, u32[]{:S(2)}) collective-permute-start(bf16[768,768]{1,0:T(8,128)(2,1)} %get-tuple-element.148), channel_id=1, source_target_pairs={{0,64},{1,65},{2,66},{3,67},{4,68},{5,69},{6,70},{7,71},{8,72},{9,... | collective-permute-start | bytes 3538952 | tf_op jit(solution)/shard_map/ppermute | solution.py:516
  586.7 17.2 %collective-permute-start.6 = (f32[128,768]{1,0:T(8,128)}, f32[128,768]{1,0:T(8,128)}, u32[]{:S(2)}, u32[]{:S(2)}) collective-permute-start(f32[128,768]{1,0:T(8,128)} %get-tuple-element.105), channel_id=1, source_target_pairs={{0,64},{64,0},{1,65},{65,1},{2,66},{66,2},{3,67},{67,3},{4,68},{68... | collective-permute-start | bytes 1179656 | tf_op jit(solution)/shard_map/ppermute | solution.py:506
  591.3 35.3 %collective-permute-start.15 = (bf16[768,768]{1,0:T(8,128)(2,1)}, bf16[768,768]{1,0:T(8,128)(2,1)S(1)}, u32[]{:S(2)}, u32[]{:S(2)}) collective-permute-start(bf16[768,768]{1,0:T(8,128)(2,1)} %get-tuple-element.150), channel_id=1, source_target_pairs={{64,0},{65,1},{66,2},{67,3},{68,4},{69,5},{70,6},{71,7},{72,8},{73... | collective-permute-start | bytes 3538952 | tf_op jit(solution)/shard_map/ppermute | solution.py:518
  595.0 26.6 %all-to-all-start.9 = ((bf16[16,4,13,576]{3,1,2,0:T(4,128)(2,1)}), bf16[16,4,13,576]{3,1,2,0:T(4,128)(2,1)S(1)}, u32[]{:S(2)}, u32[]{:S(2)}) async-start(bf16[16,4,13,576]{3,1,2,0:T(4,128)(2,1)} %copy.133), calls=%async_computation.9 | async-start | bytes 2129920 | tf_op jit(solution)/shard_map/all_to_all | solution.py:352
  622.7 10.2 %all-to-all-start.10 = ((f32[4,13,576]{2,1,0:T(8,128)}), f32[4,13,576]{2,1,0:T(8,128)S(1)}, u32[]{:S(2)}, u32[]{:S(2)}) async-start(f32[4,13,576]{2,1,0:T(8,128)} %convert_reduce_fusion), calls=%async_computation.10 | async-start | bytes 327680 | tf_op jit(solution)/shard_map/all_to_all | solution.py:529
  (132 other events, 1025.0 us)
Sparse Core Ops, SparseCore 0:
  21.3 42.7 all-gather.2

commit v2 on v1

--- a/solution.py
+++ b/solution.py
@@ -178,6 +178,245 @@
             collective_id=cid, has_side_effects=True, vmem_limit_bytes=16 << 20
         ),
     )(x)
+
+
+PAD = 32
+
+
+class Exchange:
+    def __init__(self, src, dst, send, recv):
+        self.src, self.dst, self.send, self.recv = src, dst, send, recv
+        self.me, self.count = lax.axis_index("exp"), lax.axis_size("exp")
+
+    def copy(self, k):
+        peer = lax.rem(self.me + k, self.count)
+        return remote(
+            self.src.at[peer], self.dst.at[self.me], self.send, self.recv, k, "exp", peer
+        )
+
+    def each(self, act):
+        def body(k, carry):
+            act(self.copy(k))
+            return carry
+
+        lax.fori_loop(1, self.count, body, 0)
+
+    def start(self):
+        self.each(lambda c: c.start())
+        self.dst[self.me] = self.src[self.me]
+
+    def wait_recv(self):
+        self.each(lambda c: c.wait_recv())
+
+    def wait_send(self):
+        self.each(lambda c: c.wait_send())
+
+
+def meet_all():
+    barrier = pltpu.get_barrier_semaphore()
+    me, count = lax.axis_index("exp"), lax.axis_size("exp")
+
+    def greet(k, carry):
+        peer = lax.rem(me + k, count)
+        pl.semaphore_signal(barrier, inc=1, device_id={"exp": peer}, device_id_type=MESH)
+        return carry
+
+    lax.fori_loop(1, count, greet, 0)
+    ctx = lax.axis_index("ctx")
+    right, left = lax.rem(ctx + 1, 4), lax.rem(ctx + 3, 4)
+    for neighbour in (left, right):
+        pl.semaphore_signal(barrier, inc=1, device_id={"ctx": neighbour}, device_id_type=MESH)
+    pl.semaphore_wait(barrier, count + 1)
+    return ctx, right, left
+
+
+def run_experts(
+    rows, out_ref, sel_ref, all_ref, ret_ref, block, beside_one, beside_two, scratch
+):
+    (inbox, part, far_l, far_r, sum_l, sum_r, in_l, in_r, res) = scratch[:9]
+    s_in, r_in, s_out, r_out, s_ag, r_ag, s_rs, r_rs = scratch[9:]
+    me, right, left = meet_all()
+    far = lax.rem(me + 2, 4)
+    low, high = halves(rows)
+    n_low = low.size
+    flat = inbox.shape[0] * inbox.shape[1]
+    width = inbox.shape[2]
+
+    arriving = Exchange(out_ref, inbox, s_in, r_in)
+    arriving.start()
+    arriving.wait_recv()
+    all_ref[me] = mm(sel_ref[...], inbox[...].reshape(flat, width)).astype(BF16)
+
+    def pass_on(k, slot, half, to):
+        at = all_ref.at[slot, half]
+        return remote(at, at, s_ag, r_ag, k, "ctx", to)
+
+    to_right_low = pass_on(0, me, low, right)
+    to_left_high = pass_on(1, me, high, left)
+    to_right_high = pass_on(2, me, high, right)
+    to_left_low = pass_on(3, me, low, left)
+    on_right = pass_on(4, left, low, right)
+    on_left = pass_on(5, right, high, left)
+    to_right_low.start()
+    to_left_high.start()
+    to_right_high.start()
+    to_left_low.start()
+
+    def send(k, src, dst, to):
+        return remote(src, dst, s_rs, r_rs, k, "ctx", to)
+
+    a = send(0, part.at[far, low], far_l, right)
+    b = send(1, part.at[far, high], far_r, left)
+    c = send(2, part.at[right, high], in_l.at[high], right)
+    d = send(3, part.at[left, low], in_r.at[low], left)
+    e = send(4, sum_r, in_l.at[low], right)
+    f = send(5, sum_l, in_r.at[high], left)
+
+    block(me, part)
+    to_right_low.wait_recv()
+    on_right.start()
+    to_left_high.wait_recv()
+    on_left.start()
+    to_right_high.wait_recv()
+    block(left, part)
+    d.start()
+    to_left_low.wait_recv()
+    block(right, part)
+    c.start()
+    on_right.wait_recv()
+    on_left.wait_recv()
+    block(far, part)
+    a.start()
+    b.start()
+    beside_one()
+    a.wait_recv()
+    sum_r[...] = (part[right, :n_low, :].astype(F32) + far_l[...].astype(F32)).astype(BF16)
+    e.start()
+    b.wait_recv()
+    sum_l[...] = (part[left, n_low:, :].astype(F32) + far_r[...].astype(F32)).astype(BF16)
+    f.start()
+    beside_two()
+    for x in (c, d, e, f):
+        x.wait_recv()
+    total = part[me].astype(F32) + in_l[...].astype(F32) + in_r[...].astype(F32)
+    padded = mm_tn(sel_ref[...], total.astype(BF16)).astype(BF16)
+    res[...] = padded.reshape(res.shape)
+    leaving = Exchange(res, ret_ref, s_out, r_out)
+    leaving.start()
+    leaving.wait_recv()
+    for x in (to_right_low, to_left_high, to_right_high, to_left_low, on_right, on_left):
+        x.wait_send()
+    for x in (a, b, c, d, e, f):
+        x.wait_send()
+    arriving.wait_send()
+    leaving.wait_send()
+
+
+def expert_scratch(experts, rows, width):
+    low, high = halves(rows)
+    v = lambda *shape: pltpu.VMEM((*shape, width), BF16)
+    return [
+        v(experts, PAD),
+        v(4, rows),
+        v(low.size),
+        v(high.size),
+        v(high.size),
+        v(low.size),
+        v(rows),
+        v(rows),
+        v(experts, PAD),
+        *[pltpu.SemaphoreType.DMA((experts,))] * 4,
+        *[pltpu.SemaphoreType.DMA((6,))] * 4,
+    ]
+
+
+def experts_kernel(rows, out_ref, sel_ref, w_in, w_back, ret_ref, all_ref, pre_ref, *scratch):
+    def block(j, part):
+        pre = mm(all_ref[j], w_in[...])
+        pre_ref[j] = pre
+        hidden = gelu_parts(pre)[0].astype(BF16)
+        part[j] = mm_nt(hidden, w_back[...]).astype(BF16)
+
+    nothing = lambda: None
+    run_experts(rows, out_ref, sel_ref, all_ref, ret_ref, block, nothing, nothing, scratch)
+
+
+def experts_back_kernel(
+    rows, out_ref, sel_ref, w_in, w_back, ent_ref, pre_ref, ret_ref, d_in, d_back,
+    all_ref, hid_ref, dpre_ref, *scratch
+):
+    width = w_in.shape[0]
+
+    def block(j, part):
+        hidden, slope = gelu_parts(pre_ref[j])
+        hid_ref[j] = hidden.astype(BF16)
+        dpre = (mm(all_ref[j], w_back[...]) * slope).astype(BF16)
+        dpre_ref[j] = dpre
+        part[j] = mm_nt(dpre, w_in[...]).astype(BF16)
+
+    def flat(ref):
+        return ref[...].reshape(4 * rows, ref.shape[2])
+
+    def beside_one():
+        d_back[...] = mm_tn(flat(all_ref), flat(hid_ref))
+
+    def beside_two():
+        d_in[...] = mm_tn(flat(ent_ref), flat(dpre_ref))
+
+    run_experts(rows, out_ref, sel_ref, all_ref, ret_ref, block, beside_one, beside_two, scratch)
+
+
+def selection(experts, capacity):
+    sel = np.zeros((experts * capacity, experts, PAD), np.float32)
+    for e in range(experts):
+        for s in range(capacity):
+            sel[e * capacity + s, e, s] = 1
+    return jnp.asarray(sel.reshape(experts * capacity, experts * PAD), BF16)
+
+
+def experts_forward(outgoing, sel, w_in, w_back):
+    experts, _, width = outgoing.shape
+    rows = sel.shape[0]
+    vm = pl.BlockSpec(memory_space=pltpu.VMEM)
+    return pl.pallas_call(
+        functools.partial(experts_kernel, rows),
+        out_shape=(
+            jax.ShapeDtypeStruct(outgoing.shape, BF16),
+            jax.ShapeDtypeStruct((4, rows, width), BF16),
+            jax.ShapeDtypeStruct((4, rows, w_in.shape[1]), F32),
+        ),
+        in_specs=[vm] * 4,
+        out_specs=(vm,) * 3,
+        scratch_shapes=expert_scratch(experts, rows, width),
+        compiler_params=pltpu.CompilerParams(
+            collective_id=2, has_side_effects=True, vmem_limit_bytes=48 << 20
+        ),
+    )(outgoing, sel, w_in, w_back)
+
+
+def experts_backward(outgoing, sel, w_in, w_back, entering, pre):
+    experts, _, width = outgoing.shape
+    rows, hid = sel.shape[0], w_in.shape[1]
+    vm = pl.BlockSpec(memory_space=pltpu.VMEM)
+    return pl.pallas_call(
+        functools.partial(experts_back_kernel, rows),
+        out_shape=(
+            jax.ShapeDtypeStruct(outgoing.shape, BF16),
+            jax.ShapeDtypeStruct(w_in.shape, F32),
+            jax.ShapeDtypeStruct(w_back.shape, F32),
+        ),
+        in_specs=[vm] * 6,
+        out_specs=(vm,) * 3,
+        scratch_shapes=[
+            pltpu.VMEM((4, rows, width), BF16),
+            pltpu.VMEM((4, rows, hid), BF16),
+            pltpu.VMEM((4, rows, hid), BF16),
+            *expert_scratch(experts, rows, width),
+        ],
+        compiler_params=pltpu.CompilerParams(
+            collective_id=3, has_side_effects=True, vmem_limit_bytes=48 << 20
+        ),
+    )(outgoing, sel, w_in, w_back, entering, pre)
 
 
 def bias_rows(tiles_ref, kind_ref, head, block):
@@ -334,15 +573,15 @@
     return value, slope
 
 
-def slot_tables(routes, experts, capacity):
+def slot_tables(routes, experts):
     rows = routes.shape[0]
     flat = routes.reshape(rows * TOP)
     hot = flat[:, None] == jnp.arange(experts, dtype=jnp.int32)
     before = np.tril(np.ones((rows * TOP, rows * TOP), np.float32), -1)
     earlier = mm(jnp.asarray(before, BF16), hot.astype(BF16))
     slot = jnp.sum(jnp.where(hot, earlier, 0.0), -1).astype(jnp.int32)
-    target = (flat * capacity + slot).reshape(rows, TOP)
-    slots = jnp.arange(experts * capacity, dtype=jnp.int32)
+    target = (flat * PAD + slot).reshape(rows, TOP)
+    slots = jnp.arange(experts * PAD, dtype=jnp.int32)
     slot_hot = [(target[:, c : c + 1] == slots).astype(BF16) for c in range(TOP)]
     route_hot = [(routes[:, c : c + 1] == jnp.arange(experts)).astype(F32) for c in range(TOP)]
     return route_hot, slot_hot
@@ -373,7 +612,8 @@
     heads = HEADS // n_ctx
     part = heads * HEAD_DIM
     capacity = rows * TOP // n_exp + max(1, rows * TOP // (16 * n_exp))
-    slots = n_exp * capacity
+    slots = n_exp * PAD
+    sel = selection(n_exp, capacity)
     section = lax.axis_index("section")
     ctx = lax.axis_index("ctx")
     first = section == 0
@@ -423,7 +663,7 @@
     given = jnp.where(first, own_routes[1], own_routes[0])
     taken = lax.ppermute(given, "section", [(0, 1), (1, 0)])
     layer_routes = (jnp.where(first, kept, taken), jnp.where(first, taken, kept))
-    tables = [slot_tables(r, n_exp, capacity) for r in layer_routes]
+    tables = [slot_tables(r, n_exp) for r in layer_routes]
 
     def forward(x, layer):
         w_qkv, w_out, gain_one, gain_two, tiles, router, w_in, w_back = weights[layer]
@@ -440,14 +680,9 @@
         raised = [jnp.exp(c - peak) for c in chosen]
         gates = [r / (raised[0] + raised[1]) for r in raised]
         placing = slot_hot[0] + slot_hot[1]
-        outgoing = mm_tn(placing, mixed).astype(BF16).reshape(n_exp, capacity, width)
-        entering = exp_swap(outgoing).reshape(slots, width)
-        entering = ctx_gather(entering, 2).reshape(n_ctx * slots, width)
-        pre = mm(entering, w_in)
-        hidden = gelu_parts(pre)[0].astype(BF16)
-        leaving = mm_nt(hidden, w_back).astype(BF16).reshape(n_ctx, slots, width)
-        leaving = ctx_scatter(leaving, BF16, 3).reshape(n_exp, capacity, width)
-        returned = exp_swap(leaving).reshape(slots, width)
+        outgoing = mm_tn(placing, mixed).astype(BF16).reshape(n_exp, PAD, width)
+        returned, entering, pre = experts_forward(outgoing, sel, w_in, w_back)
+        returned = returned.reshape(slots, width)
         picked = [mm(h, returned) for h in slot_hot]
         y = middle + gates[0] * picked[0] + gates[1] * picked[1]
         keep = (x, normed, proj, attended, middle, mixed, gates, picked, entering, pre)
@@ -460,16 +695,9 @@
         dreturned = mm_tn(slot_hot[0], (gates[0] * g).astype(BF16)) + mm_tn(
             slot_hot[1], (gates[1] * g).astype(BF16)
         )
-        dreturned = dreturned.astype(BF16).reshape(n_exp, capacity, width)
-        darrived = exp_swap(dreturned).reshape(slots, width)
-        darrived = ctx_gather(darrived, 2).reshape(n_ctx * slots, width)
-        hidden, slope = gelu_parts(pre)
-        dpre = (mm(darrived, w_back) * slope).astype(BF16)
-        dentering = mm_nt(dpre, w_in).astype(BF16).reshape(n_ctx, slots, width)
-        dentering = ctx_scatter(dentering, BF16, 3).reshape(n_exp, capacity, width)
-        dleft = exp_swap(dentering).reshape(slots, width)
-        d_in = mm_tn(entering, dpre)
-        d_back = mm_tn(darrived, hidden.astype(BF16))
+        dreturned = dreturned.astype(BF16).reshape(n_exp, PAD, width)
+        dleft, d_in, d_back = experts_backward(dreturned, sel, w_in, w_back, entering, pre)
+        dleft = dleft.reshape(slots, width)
         dgates = [jnp.sum(g * p, -1, keepdims=True) for p in picked]
         mean = gates[0] * dgates[0] + gates[1] * dgates[1]
         dchosen = [a * (b - mean) for a, b in zip(gates, dgates)]

time: 655 us -> 587 us (0.90)
  the two profiles are of different devices: /device:TPU:0 before, /device:TPU:2 now
where the time goes in v2:
time: 587 us; the launch traced here: 578 us
  Pallas kernels  321 us (55%)
  local copies, waits for them, and re-layouts  63.5 us (11%)
  other arithmetic  49.5 us (8%)
  starting transfers between devices  41.9 us (7%)
  blocking collectives  35 us (6%)
  matrix products  28 us (5%)
  waiting for transfers between devices  23.2 us (4%)
  between operations  16 us (3%)
    pallas_call x2, Pallas kernels, experts_backward(): pl.pallas_call(functools.partial(experts_back_kernel, rows), out_shape=(j...  115 us
    pallas_call x2, Pallas kernels, experts_forward(): pl.pallas_call(functools.partial(experts_kernel, rows), out_shape=(jax.Sh...  109 us
    pallas_call x4, Pallas kernels, ctx_gather(): pl.pallas_call(functools.partial(gather_kernel, 'ctx', rows), out_shape=j...  42.2 us
    pallas_call x4, Pallas kernels, ctx_scatter(): pl.pallas_call(functools.partial(scatter_kernel, 'ctx', rows), out_shape=...  40.7 us
    dot_general x38, matrix products, dot(): return lax.dot_general(a, b, (dims, ((), ())), preferred_element_type=F32)  28 us
    all_gather x1, blocking collectives, on_device(): lax.all_gather(jnp.pad(out_weight[0], ((0, 4), (0, 0))), 'exp', axis=0)  24 us
    ppermute x5, starting transfers between devices, on_device(): sent1 = [lax.ppermute(p.astype(BF16), 'section', [(0, 1)]) for p in grads1]  16.8 us
    all_to_all x2, starting transfers between devices, exp_swap(): return lax.all_to_all(x, 'exp', split_axis=0, concat_axis=0, tiled=True)  14.3 us
  transfers between devices with their start and end apart: 21, of which 3 were waited for; matrix products, arithmetic and copies ran while one was open for 12% of the time, Pallas kernels for 2%

profile of v2, /device:TPU:2, one launch (start us, length us, event | category | flops | bytes accessed | tf_op | source)
XLA Modules:
  0.0 578.3 jit_solution(3767600665877865949)
XLA Ops:
  10.1 10.9 %all_to_all.20 = bf16[4,16,576]{2,1,0:T(8,128)(2,1)} all-to-all(bf16[4,16,576]{2,1,0:T(8,128)(2,1)S(1)} %pad.18.clone), channel_id=1, replica_groups=mesh['section'=2,'ctx'=4,'exp'=16] {'ctx'}, dimensions={0} | all-to-all | bytes 147456 | tf_op jit(solution)/shard_map/all_to_all | solution.py:635
  22.9 24.0 %all-gather = bf16[256,768]{1,0:T(8,128)(2,1)S(1)} all-gather(bf16[16,768]{1,0:T(8,128)(2,1)S(1)} %pad.19), channel_id=2, replica_groups=mesh['section'=2,'ctx'=4,'exp'=16] {'exp'}, dimensions={0}, use_global_device_ids=true | all-gather | bytes 417792 | tf_op jit(solution)/shard_map/all_gather | solution.py:637
  49.7 14.1 %all-gather.3.cloned.1.call-done = bf16[16,64,576]{2,1,0:T(8,128)(2,1)} async-done(((bf16[1,64,576]{2,1,0:T(8,128)(2,1)}), bf16[16,64,576]{2,1,0:T(8,128)(2,1)}) %all-gather.3.cloned.1.call-update) | async-done | bytes 1179664 | tf_op jit(solution)/shard_map/all_gather | solution.py:636
  65.8 3.2 broadcast_select_fusion.2
  69.0 3.3 broadcast_select_fusion.3
  79.0 11.3 %shard_map.276 = bf16[4,128,768]{2,1,0:T(8,128)(2,1)S(1)} custom-call(bf16[128,768]{1,0:T(8,128)(2,1)S(1)} %fusion.20.x_ref), custom_call_target="tpu_custom_call" | custom-call | tf_op jit(solution)/shard_map/pallas_call | solution.py:103
  92.3 3.0 reshape.552
  96.5 3.0 reshape.541
  114.5 11.0 %shard_map.278 = f32[128,768]{1,0:T(8,128)S(1)} custom-call(bf16[4,128,768]{2,1,0:T(8,128)(2,1)S(1)} %bitcast.182), custom_call_target="tpu_custom_call" | custom-call | tf_op jit(solution)/shard_map/pallas_call | solution.py:162
  127.4 53.9 %shard_map.279 = (bf16[16,32,768]{2,1,0:T(8,128)(2,1)S(1)}, bf16[4,272,768]{2,1,0:T(8,128)(2,1)S(1)}, f32[4,272,768]{2,1,0:T(8,128)}) custom-call(bf16[16,32,768]{2,1,0:T(8,128)(2,1)S(1)} %bitcast.185, bf16[272,512]{1,0:T(8,128)(2,1)S(1)} %copy-done.6, bf16[768,768]{1,0:T(8,128)(2,1)S(1)} %copy-done.2, bf16[768,768]{1,0:T(8,128)(2,1)S(1)} %copy-done), custom_call_target="tpu_custom_call" | custom-call | tf_op jit(solution)/shard_map/pallas_call | solution.py:381
  183.1 10.8 %shard_map.280 = bf16[4,128,768]{2,1,0:T(8,128)(2,1)S(1)} custom-call(bf16[128,768]{1,0:T(8,128)(2,1)S(1)} %fusion.10.x_ref), custom_call_target="tpu_custom_call" | custom-call | tf_op jit(solution)/shard_map/pallas_call | solution.py:103
  198.5 9.1 %shard_map.282 = f32[128,768]{1,0:T(8,128)S(1)} custom-call(bf16[4,128,768]{2,1,0:T(8,128)(2,1)S(1)} %bitcast.183), custom_call_target="tpu_custom_call" | custom-call | tf_op jit(solution)/shard_map/pallas_call | solution.py:162
  209.4 55.2 %shard_map.283 = (bf16[16,32,768]{2,1,0:T(8,128)(2,1)S(1)}, bf16[4,272,768]{2,1,0:T(8,128)(2,1)S(1)}, f32[4,272,768]{2,1,0:T(8,128)}) custom-call(bf16[16,32,768]{2,1,0:T(8,128)(2,1)S(1)} %bitcast.184, bf16[272,512]{1,0:T(8,128)(2,1)S(1)} %copy-done.6, bf16[768,768]{1,0:T(8,128)(2,1)S(1)} %copy-done.5, bf16[768,768]{1,0:T(8,128)(2,1)S(1)} %copy-done.4), custom_call_target="tpu_custom_call" | custom-call | tf_op jit(solution)/shard_map/pallas_call | solution.py:381
  268.6 58.9 %shard_map.284 = (bf16[16,32,768]{2,1,0:T(8,128)(2,1)S(1)}, f32[768,768]{1,0:T(8,128)}, f32[768,768]{1,0:T(8,128)}) custom-call(bf16[16,32,768]{2,1,0:T(8,128)(2,1)S(1)} %bitcast.181, bf16[272,512]{1,0:T(8,128)(2,1)S(1)} %copy-done.6, bf16[768,768]{1,0:T(8,128)(2,1)S(1)} %copy-done.5, bf16[768,768]{1,0:T(8,128)(2,1)S(1)} %copy-done.4, ...), custom_call_target="tpu_custom_call" | custom-call | tf_op jit(solution)/shard_map/pallas_call | solution.py:401
  328.8 9.6 %shard_map.285 = bf16[4,128,768]{2,1,0:T(8,128)(2,1)S(1)} custom-call(bf16[128,768]{1,0:T(8,128)(2,1)S(1)} %get-tuple-element.110.x_ref), custom_call_target="tpu_custom_call" | custom-call | tf_op jit(solution)/shard_map/pallas_call | solution.py:103
  344.6 4.7 shard_map.286
  350.2 9.7 %shard_map.287 = f32[128,768]{1,0:T(8,128)S(1)} custom-call(bf16[4,128,768]{2,1,0:T(8,128)(2,1)S(1)} %bitcast.193), custom_call_target="tpu_custom_call" | custom-call | tf_op jit(solution)/shard_map/pallas_call | solution.py:162
  364.9 56.0 %shard_map.288 = (bf16[16,32,768]{2,1,0:T(8,128)(2,1)S(1)}, f32[768,768]{1,0:T(8,128)}, f32[768,768]{1,0:T(8,128)}) custom-call(bf16[16,32,768]{2,1,0:T(8,128)(2,1)S(1)} %bitcast.178, bf16[272,512]{1,0:T(8,128)(2,1)S(1)} %copy-done.6, bf16[768,768]{1,0:T(8,128)(2,1)S(1)} %copy-done.3, bf16[768,768]{1,0:T(8,128)(2,1)S(1)} %copy-done.1, ...), custom_call_target="tpu_custom_call" | custom-call | tf_op jit(solution)/shard_map/pallas_call | solution.py:401
  422.3 10.5 %shard_map.289 = bf16[4,128,768]{2,1,0:T(8,128)(2,1)S(1)} custom-call(bf16[128,768]{1,0:T(8,128)(2,1)S(1)} %get-tuple-element.108.x_ref), custom_call_target="tpu_custom_call" | custom-call | tf_op jit(solution)/shard_map/pallas_call | solution.py:103
  434.7 4.7 shard_map.290
  450.0 10.8 %shard_map.291 = f32[128,768]{1,0:T(8,128)S(1)} custom-call(bf16[4,128,768]{2,1,0:T(8,128)(2,1)S(1)} %bitcast.190), custom_call_target="tpu_custom_call" | custom-call | tf_op jit(solution)/shard_map/pallas_call | solution.py:162
  464.3 2.9 reduce_sum.279
  485.5 5.5 collective-permute-start.8
  493.6 3.0 convert_element_type.344
  506.3 4.1 collective-permute-start.16
  512.7 7.0 %all-to-all-start.3 = ((bf16[16,12,768]{2,1,0:T(8,128)(2,1)}), bf16[16,12,768]{2,1,0:T(8,128)(2,1)S(1)}, u32[]{:S(2)}, u32[]{:S(2)}) async-start(bf16[16,12,768]{2,1,0:T(8,128)(2,1)} %convert_element_type.340), calls=%async_computation.3 | async-start | bytes 786432 | tf_op jit(solution)/shard_map/all_to_all | solution.py:591
  519.7 4.6 collective-permute-start.14
  532.4 7.4 %all-to-all-start.1 = ((bf16[16,4,13,576]{3,1,2,0:T(4,128)(2,1)}), bf16[16,4,13,576]{3,1,2,0:T(4,128)(2,1)}, u32[]{:S(2)}, u32[]{:S(2)}) async-start(bf16[16,4,13,576]{3,1,2,0:T(4,128)(2,1)} %copy.134), calls=%async_computation.1 | async-start | bytes 2129920 | tf_op jit(solution)/shard_map/all_to_all | solution.py:591
  544.6 4.4 add_bitcast_fusion
  549.0 6.4 %all-to-all-done.1 = bf16[16,4,13,576]{3,1,2,0:T(4,128)(2,1)} async-done(((bf16[16,4,13,576]{3,1,2,0:T(4,128)(2,1)}), bf16[16,4,13,576]{3,1,2,0:T(4,128)(2,1)}, u32[]{:S(2)}, u32[]{:S(2)}) %all-to-all-start.1) | async-done | bytes 958496 | tf_op jit(solution)/shard_map/all_to_all | solution.py:591
  557.7 3.5 all-to-all-start.2
  561.2 4.2 add_bitcast_fusion.1
  (393 shorter events, 131.8 us)
Async XLA Ops:
  7.2 41.5 %copy-start.73 = (bf16[256,256]{1,0:T(8,128)(2,1)S(1)}, bf16[256,256]{1,0:T(8,128)(2,1)}, u32[]{:S(2)}) copy-start(bf16[256,256]{1,0:T(8,128)(2,1)} %constant.64.clone) | copy-start | bytes 393220
  7.2 40.4 %copy-start.74 = (bf16[2,1,128,768]{3,2,1,0:T(8,128)(2,1)S(1)}, bf16[2,1,128,768]{3,2,1,0:T(8,128)(2,1)}, u32[]{:S(2)}) copy-start(bf16[2,1,128,768]{3,2,1,0:T(8,128)(2,1)} %param.21) | copy-start | bytes 1179652
  7.2 40.5 %copy-start.88 = (s32[8]{0:T(128)S(1)}, s32[8]{0:T(128)}, u32[]{:S(2)}) copy-start(s32[8]{0:T(128)} %param.24) | copy-start | bytes 100
  7.2 56.6 %all-gather.3.cloned.1.call-start = ((), (), s32[]{:S(2)}) async-start(), calls=%async_computation.4 | async-start | bytes 1392640 | tf_op jit(solution)/shard_map/all_gather | solution.py:636
  22.0 26.4 %collective-permute-start.2 = (s32[128,2]{1,0:T(8,128)S(1)}, s32[128,2]{1,0:T(8,128)S(1)}, u32[]{:S(2)}, u32[]{:S(2)}) collective-permute-start(s32[128,2]{1,0:T(8,128)S(1)} %select_bitcast_fusion), channel_id=1, source_target_pairs={{0,64},{64,0},{1,65},{65,1},{2,66},{66,2},{3,67},{67,3},{4,68},{68... | collective-permute-start | bytes 3080 | tf_op jit(solution)/shard_map/ppermute | solution.py:664
  46.9 17.3 %collective-permute-start.1 = (bf16[16,16,768]{2,1,0:T(8,128)(2,1)S(1)}, bf16[16,16,768]{2,1,0:T(8,128)(2,1)S(1)}, u32[]{:S(2)}, u32[]{:S(2)}) collective-permute-start(bf16[16,16,768]{2,1,0:T(8,128)(2,1)S(1)} %bitcast.200), channel_id=1, source_target_pairs={{0,64},{64,0},{1,65},{65,1},{2,66},{66,2},{3,67},{67,3},{4,68},{68... | collective-permute-start | bytes 1179656 | tf_op jit(solution)/shard_map/ppermute | solution.py:622
  47.0 18.9 %collective-permute-start.4 = (bf16[768,768]{1,0:T(8,128)(2,1)}, bf16[768,768]{1,0:T(8,128)(2,1)}, u32[]{:S(2)}, u32[]{:S(2)}) collective-permute-start(bf16[768,768]{1,0:T(8,128)(2,1)} %bitcast.19), channel_id=1, source_target_pairs={{0,64},{64,0},{1,65},{65,1},{2,66},{66,2},{3,67},{67,3},{4,68},{68... | collective-permute-start | bytes 3538952 | tf_op jit(solution)/shard_map/ppermute | solution.py:622
  47.5 21.5 %collective-permute-start.3 = (bf16[768,768]{1,0:T(8,128)(2,1)}, bf16[768,768]{1,0:T(8,128)(2,1)}, u32[]{:S(2)}, u32[]{:S(2)}) collective-permute-start(bf16[768,768]{1,0:T(8,128)(2,1)} %bitcast.18), channel_id=1, source_target_pairs={{0,64},{64,0},{1,65},{65,1},{2,66},{66,2},{3,67},{67,3},{4,68},{68... | collective-permute-start | bytes 3538952 | tf_op jit(solution)/shard_map/ppermute | solution.py:622
  47.7 31.1 %copy-start.42 = (bf16[1,1,128,768]{3,2,1,0:T(8,128)(2,1)}, bf16[1,1,128,768]{3,2,1,0:T(8,128)(2,1)S(1)}, u32[]{:S(2)}) copy-start(bf16[1,1,128,768]{3,2,1,0:T(8,128)(2,1)S(1)} %get-tuple-element.125) | copy-start | bytes 589828
  48.3 30.5 %copy-start.86 = (f32[128]{0:T(128)}, f32[128]{0:T(128)S(1)}, u32[]{:S(2)}) copy-start(f32[128]{0:T(128)S(1)} %get-tuple-element.153) | copy-start | bytes 1540
  63.8 8.5 %collective-permute-start = (bf16[16,64,576]{2,1,0:T(8,128)(2,1)}, bf16[16,64,576]{2,1,0:T(8,128)(2,1)}, u32[]{:S(2)}, u32[]{:S(2)}) collective-permute-start(bf16[16,64,576]{2,1,0:T(8,128)(2,1)} %all-gather.3.cloned.1.call-done), channel_id=1, source_target_pairs={{0,64},{64,0},{1,65},{65,1},{2,66},{66,2},{3,67},{67,3},{4,68},{68... | collective-permute-start | bytes 3538952 | tf_op jit(solution)/shard_map/ppermute | solution.py:622
  125.7 56.2 %copy-start.28 = (f32[128,768]{1,0:T(8,128)}, f32[128,768]{1,0:T(8,128)S(1)}, u32[]{:S(2)}) copy-start(f32[128,768]{1,0:T(8,128)S(1)} %get-tuple-element.123) | copy-start | bytes 1179652
  125.8 55.8 %copy-start.50 = (bf16[128,768]{1,0:T(8,128)(2,1)}, bf16[128,768]{1,0:T(8,128)(2,1)S(1)}, u32[]{:S(2)}) copy-start(bf16[128,768]{1,0:T(8,128)(2,1)S(1)} %multiply_convert_fusion.1) | copy-start | bytes 589828
  127.4 54.3 %copy-start.57 = (bf16[768,16]{1,0:T(8,128)(2,1)S(1)}, bf16[768,16]{1,0:T(8,128)(2,1)}, u32[]{:S(2)}) copy-start(bf16[768,16]{1,0:T(8,128)(2,1)} %reshape.547) | copy-start | bytes 73732
  207.8 120.1 %copy-start.30 = (f32[128,768]{1,0:T(8,128)}, f32[128,768]{1,0:T(8,128)S(1)}, u32[]{:S(2)}) copy-start(f32[128,768]{1,0:T(8,128)S(1)} %get-tuple-element.119) | copy-start | bytes 1179652
  209.4 55.5 %copy-start.82 = (bf16[2,1,128,768]{3,2,1,0:T(8,128)(2,1)S(1)}, bf16[2,1,128,768]{3,2,1,0:T(8,128)(2,1)}, u32[]{:S(2)}) copy-start(bf16[2,1,128,768]{3,2,1,0:T(8,128)(2,1)} %param.22) | copy-start | bytes 1179652
  364.9 56.1 %copy-start.29 = (f32[128,768]{1,0:T(8,128)S(1)}, f32[128,768]{1,0:T(8,128)}, u32[]{:S(2)}) copy-start(f32[128,768]{1,0:T(8,128)} %copy-done.28) | copy-start | bytes 1179652
  446.7 82.1 %collective-permute-start.5 = (bf16[128,768]{1,0:T(8,128)(2,1)}, bf16[128,768]{1,0:T(8,128)(2,1)}, u32[]{:S(2)}, u32[]{:S(2)}) collective-permute-start(bf16[128,768]{1,0:T(8,128)(2,1)} %get-tuple-element.116), channel_id=1, source_target_pairs={{0,64},{64,0},{1,65},{65,1},{2,66},{66,2},{3,67},{67,3},{4,68},{68... | collective-permute-start | bytes 589832 | tf_op jit(solution)/shard_map/ppermute | solution.py:734
  476.5 25.4 %collective-permute-start.9 = (bf16[64,222]{1,0:T(8,128)(2,1)}, bf16[64,222]{1,0:T(8,128)(2,1)}, u32[]{:S(2)}, u32[]{:S(2)}) collective-permute-start(bf16[64,222]{1,0:T(8,128)(2,1)} %fusion.108), channel_id=1, source_target_pairs={{64,0},{65,1},{66,2},{67,3},{68,4},{69,5},{70,6},{71,7},{72,8},{73... | collective-permute-start | bytes 85256 | tf_op jit(solution)/shard_map/ppermute | solution.py:746
  484.3 35.4 %collective-permute-start.7 = (bf16[768,576]{0,1:T(8,128)(2,1)}, bf16[768,576]{0,1:T(8,128)(2,1)}, u32[]{:S(2)}, u32[]{:S(2)}) collective-permute-start(bf16[768,576]{0,1:T(8,128)(2,1)} %get-tuple-element.166), channel_id=1, source_target_pairs={{64,0},{65,1},{66,2},{67,3},{68,4},{69,5},{70,6},{71,7},{72,8},{73... | collective-permute-start | bytes 2654216 | tf_op jit(solution)/shard_map/ppermute | solution.py:746
  485.5 38.7 %collective-permute-start.8 = (bf16[768,576]{0,1:T(8,128)(2,1)}, bf16[768,576]{0,1:T(8,128)(2,1)}, u32[]{:S(2)}, u32[]{:S(2)}) collective-permute-start(bf16[768,576]{0,1:T(8,128)(2,1)} %get-tuple-element.164), channel_id=1, source_target_pairs={{0,64},{1,65},{2,66},{3,67},{4,68},{5,69},{6,70},{7,71},{8,72},{9,... | collective-permute-start | bytes 2654216 | tf_op jit(solution)/shard_map/ppermute | solution.py:744
  491.1 12.1 %collective-permute-start.10 = (bf16[64,222]{1,0:T(8,128)(2,1)S(1)}, bf16[64,222]{1,0:T(8,128)(2,1)S(1)}, u32[]{:S(2)}, u32[]{:S(2)}) collective-permute-start(bf16[64,222]{1,0:T(8,128)(2,1)S(1)} %fusion.107), channel_id=1, source_target_pairs={{0,64},{1,65},{2,66},{3,67},{4,68},{5,69},{6,70},{7,71},{8,72},{9,... | collective-permute-start | bytes 85256 | tf_op jit(solution)/shard_map/ppermute | solution.py:744
  501.9 4.4 collective-permute-start.12
  503.2 7.2 %collective-permute-start.11 = (bf16[192,768]{1,0:T(8,128)(2,1)S(1)}, bf16[192,768]{1,0:T(8,128)(2,1)S(1)}, u32[]{:S(2)}, u32[]{:S(2)}) collective-permute-start(bf16[192,768]{1,0:T(8,128)(2,1)S(1)} %copy-done.81), channel_id=1, source_target_pairs={{64,0},{65,1},{66,2},{67,3},{68,4},{69,5},{70,6},{71,7},{72,8},{73... | collective-permute-start | bytes 884744 | tf_op jit(solution)/shard_map/ppermute | solution.py:746
  506.3 38.3 %collective-permute-start.16 = (bf16[768,768]{1,0:T(8,128)(2,1)}, bf16[768,768]{1,0:T(8,128)(2,1)}, u32[]{:S(2)}, u32[]{:S(2)}) collective-permute-start(bf16[768,768]{1,0:T(8,128)(2,1)} %convert_element_type.348), channel_id=1, source_target_pairs={{0,64},{1,65},{2,66},{3,67},{4,68},{5,69},{6,70},{7,71},{8,72},{9,... | collective-permute-start | bytes 3538952 | tf_op jit(solution)/shard_map/ppermute | solution.py:744
  510.4 34.2 %collective-permute-start.15 = (bf16[768,768]{1,0:T(8,128)(2,1)}, bf16[768,768]{1,0:T(8,128)(2,1)}, u32[]{:S(2)}, u32[]{:S(2)}) collective-permute-start(bf16[768,768]{1,0:T(8,128)(2,1)} %convert_element_type.346), channel_id=1, source_target_pairs={{64,0},{65,1},{66,2},{67,3},{68,4},{69,5},{70,6},{71,7},{72,8},{73... | collective-permute-start | bytes 3538952 | tf_op jit(solution)/shard_map/ppermute | solution.py:746
  512.7 19.7 %all-to-all-start.3 = ((bf16[16,12,768]{2,1,0:T(8,128)(2,1)}), bf16[16,12,768]{2,1,0:T(8,128)(2,1)S(1)}, u32[]{:S(2)}, u32[]{:S(2)}) async-start(bf16[16,12,768]{2,1,0:T(8,128)(2,1)} %convert_element_type.340), calls=%async_computation.3 | async-start | bytes 786432 | tf_op jit(solution)/shard_map/all_to_all | solution.py:591
  519.7 41.5 %collective-permute-start.14 = (bf16[768,768]{1,0:T(8,128)(2,1)}, bf16[768,768]{1,0:T(8,128)(2,1)}, u32[]{:S(2)}, u32[]{:S(2)}) collective-permute-start(bf16[768,768]{1,0:T(8,128)(2,1)} %convert_element_type.344), channel_id=1, source_target_pairs={{0,64},{1,65},{2,66},{3,67},{4,68},{5,69},{6,70},{7,71},{8,72},{9,... | collective-permute-start | bytes 3538952 | tf_op jit(solution)/shard_map/ppermute | solution.py:744
  524.2 17.6 %collective-permute-start.6 = (f32[128,768]{1,0:T(8,128)}, f32[128,768]{1,0:T(8,128)}, u32[]{:S(2)}, u32[]{:S(2)}) collective-permute-start(f32[128,768]{1,0:T(8,128)} %get-tuple-element.133), channel_id=1, source_target_pairs={{0,64},{64,0},{1,65},{65,1},{2,66},{66,2},{3,67},{67,3},{4,68},{68... | collective-permute-start | bytes 1179656 | tf_op jit(solution)/shard_map/ppermute | solution.py:734
  528.8 32.4 %collective-permute-start.13 = (bf16[768,768]{1,0:T(8,128)(2,1)}, bf16[768,768]{1,0:T(8,128)(2,1)}, u32[]{:S(2)}, u32[]{:S(2)}) collective-permute-start(bf16[768,768]{1,0:T(8,128)(2,1)} %convert_element_type.342), channel_id=1, source_target_pairs={{64,0},{65,1},{66,2},{67,3},{68,4},{69,5},{70,6},{71,7},{72,8},{73... | collective-permute-start | bytes 3538952 | tf_op jit(solution)/shard_map/ppermute | solution.py:746
  532.4 23.0 %all-to-all-start.1 = ((bf16[16,4,13,576]{3,1,2,0:T(4,128)(2,1)}), bf16[16,4,13,576]{3,1,2,0:T(4,128)(2,1)}, u32[]{:S(2)}, u32[]{:S(2)}) async-start(bf16[16,4,13,576]{3,1,2,0:T(4,128)(2,1)} %copy.134), calls=%async_computation.1 | async-start | bytes 2129920 | tf_op jit(solution)/shard_map/all_to_all | solution.py:591
  557.7 10.5 %all-to-all-start.2 = ((f32[4,13,576]{2,1,0:T(8,128)}), f32[4,13,576]{2,1,0:T(8,128)S(1)}, u32[]{:S(2)}, u32[]{:S(2)}) async-start(f32[4,13,576]{2,1,0:T(8,128)} %convert_reduce_fusion), calls=%async_computation.2 | async-start | bytes 327680 | tf_op jit(solution)/shard_map/all_to_all | solution.py:757
  (80 other events, 487.1 us)
Sparse Core Ops, SparseCore 0:
  21.2 42.5 all-gather.2

commit v3 on v2

v3 whole, which is shorter than its diff:
```python
import functools
import math

import jax
import jax.numpy as jnp
import numpy as np
from jax import lax
from jax.experimental import pallas as pl
from jax.experimental.pallas import tpu as pltpu
from jax.sharding import PartitionSpec as P

HEADS = 12
HEAD_DIM = 64
BUCKETS = 32
REACH = 128
TOP = 2
EPS = 1e-06
NEG = -1e30
SPAN = 64
KINDS = 4
MESH = pl.DeviceIdType.MESH
BF16 = jnp.bfloat16
F32 = jnp.float32
GELU_C = math.sqrt(2.0 / math.pi)


def dot(a, b, dims):
    return lax.dot_general(a, b, (dims, ((), ())), preferred_element_type=F32)


def mm(a, b):
    return dot(a, b, ((1,), (0,)))


def mm_nt(a, b):
    return dot(a, b, ((1,), (1,)))


def mm_tn(a, b):
    return dot(a, b, ((0,), (0,)))


def meet_neighbours(axis, count):
    me = lax.axis_index(axis)
    right, left = lax.rem(me + 1, count), lax.rem(me + count - 1, count)
    barrier = pltpu.get_barrier_semaphore()
    for neighbour in (left, right):
        pl.semaphore_signal(barrier, inc=1, device_id={axis: neighbour}, device_id_type=MESH)
    pl.semaphore_wait(barrier, 2)
    return me, right, left


def remote(src, dst, send, recv, k, axis, to):
    return pltpu.make_async_remote_copy(
        src_ref=src,
        dst_ref=dst,
        send_sem=send.at[k],
        recv_sem=recv.at[k],
        device_id={axis: to},
        device_id_type=MESH,
    )


def halves(rows):
    first = (rows // 2 + 15) // 16 * 16
    return (pl.ds(0, first), pl.ds(first, rows - first))


def ring_copy(send, recv, k, src, dst, to):
    return remote(src, dst, send, recv, k, "ctx", to)


class RingGather:
    def __init__(self, all_ref, rows, ids, send, recv):
        me, right, left = ids
        low, high = halves(rows)

        def pass_on(k, slot, half, to):
            at = all_ref.at[slot, half]
            return ring_copy(send, recv, k, at, at, to)

        self.first = (
            pass_on(0, me, low, right),
            pass_on(1, me, high, left),
            pass_on(2, me, high, right),
            pass_on(3, me, low, left),
        )
        self.second = (pass_on(4, left, low, right), pass_on(5, right, high, left))

    def start(self):
        for c in self.first:
            c.start()

    def forward(self):
        self.first[0].wait_recv()
        self.second[0].start()
        self.first[1].wait_recv()
        self.second[1].start()

    def wait_left(self):
        self.first[2].wait_recv()

    def wait_right(self):
        self.first[3].wait_recv()

    def wait_far(self):
        for c in self.second:
            c.wait_recv()

    def wait_send(self):
        for c in self.first + self.second:
            c.wait_send()


class RingScatter:
    def __init__(self, part, rows, ids, bufs, send, recv):
        me, right, left = ids
        far = lax.rem(me + 2, 4)
        low, high = halves(rows)
        far_l, far_r, sum_l, sum_r, in_l, in_r = bufs
        self.part, self.ids, self.n_low, self.bufs = part, ids, low.size, bufs
        copy = functools.partial(ring_copy, send, recv)
        self.far = (
            copy(0, part.at[far, low], far_l, right),
            copy(1, part.at[far, high], far_r, left),
        )
        self.right = copy(2, part.at[right, high], in_l.at[high], right)
        self.left = copy(3, part.at[left, low], in_r.at[low], left)
        self.sums = (
            copy(4, sum_r, in_l.at[low], right),
            copy(5, sum_l, in_r.at[high], left),
        )

    def send_far(self):
        for c in self.far:
            c.start()

    def send_left(self):
        self.left.start()

    def send_right(self):
        self.right.start()

    def send_sums(self):
        me, right, left = self.ids
        far_l, far_r, sum_l, sum_r, in_l, in_r = self.bufs
        n = self.n_low
        self.far[0].wait_recv()
        sum_r[...] = (self.part[right, :n, :].astype(F32) + far_l[...].astype(F32)).astype(BF16)
        self.sums[0].start()
        self.far[1].wait_recv()
        sum_l[...] = (self.part[left, n:, :].astype(F32) + far_r[...].astype(F32)).astype(BF16)
        self.sums[1].start()

    def total(self):
        for c in (self.right, self.left, *self.sums):
            c.wait_recv()
        in_l, in_r = self.bufs[4:]
        return self.part[self.ids[0]].astype(F32) + in_l[...].astype(F32) + in_r[...].astype(F32)

    def wait_send(self):
        for c in (*self.far, self.right, self.left, *self.sums):
            c.wait_send()


def scatter_buffers(rows, width):
    low, high = halves(rows)
    sizes = (low.size, high.size, high.size, low.size, rows, rows)
    return [pltpu.VMEM((n, width), BF16) for n in sizes]


PAD = 32


class Exchange:
    def __init__(self, src, dst, send, recv):
        self.src, self.dst, self.send, self.recv = src, dst, send, recv
        self.me, self.count = lax.axis_index("exp"), lax.axis_size("exp")

    def copy(self, k):
        peer = lax.rem(self.me + k, self.count)
        return remote(
            self.src.at[peer], self.dst.at[self.me], self.send, self.recv, k, "exp", peer
        )

    def each(self, act):
        def body(k, carry):
            act(self.copy(k))
            return carry

        lax.fori_loop(1, self.count, body, 0)

    def start(self):
        self.each(lambda c: c.start())
        self.dst[self.me] = self.src[self.me]

    def wait_recv(self):
        self.each(lambda c: c.wait_recv())

    def wait_send(self):
        self.each(lambda c: c.wait_send())


def meet_all():
    barrier = pltpu.get_barrier_semaphore()
    me, count = lax.axis_index("exp"), lax.axis_size("exp")

    def greet(k, carry):
        peer = lax.rem(me + k, count)
        pl.semaphore_signal(barrier, inc=1, device_id={"exp": peer}, device_id_type=MESH)
        return carry

    lax.fori_loop(1, count, greet, 0)
    ctx = lax.axis_index("ctx")
    right, left = lax.rem(ctx + 1, 4), lax.rem(ctx + 3, 4)
    for neighbour in (left, right):
        pl.semaphore_signal(barrier, inc=1, device_id={"ctx": neighbour}, device_id_type=MESH)
    pl.semaphore_wait(barrier, count + 1)
    return ctx, right, left


def run_experts(
    rows, out_ref, sel_ref, all_ref, ret_ref, block, beside_one, beside_two, scratch
):
    inbox, part, res = scratch[:3]
    bufs = scratch[3:9]
    s_in, r_in, s_out, r_out, s_ag, r_ag, s_rs, r_rs = scratch[9:]
    ids = meet_all()
    me, right, left = ids
    far = lax.rem(me + 2, 4)
    flat = inbox.shape[0] * inbox.shape[1]
    width = inbox.shape[2]

    arriving = Exchange(out_ref, inbox, s_in, r_in)
    arriving.start()
    arriving.wait_recv()
    all_ref[me] = mm(sel_ref[...], inbox[...].reshape(flat, width)).astype(BF16)
    gather = RingGather(all_ref, rows, ids, s_ag, r_ag)
    scatter = RingScatter(part, rows, ids, bufs, s_rs, r_rs)
    gather.start()
    block(me, part)
    gather.forward()
    gather.wait_left()
    block(left, part)
    scatter.send_left()
    gather.wait_right()
    block(right, part)
    scatter.send_right()
    gather.wait_far()
    block(far, part)
    scatter.send_far()
    beside_one()
    scatter.send_sums()
    beside_two()
    padded = mm_tn(sel_ref[...], scatter.total().astype(BF16)).astype(BF16)
    res[...] = padded.reshape(res.shape)
    leaving = Exchange(res, ret_ref, s_out, r_out)
    leaving.start()
    leaving.wait_recv()
    gather.wait_send()
    scatter.wait_send()
    arriving.wait_send()
    leaving.wait_send()


def expert_scratch(experts, rows, width):
    v = lambda *shape: pltpu.VMEM((*shape, width), BF16)
    return [
        v(experts, PAD),
        v(4, rows),
        v(experts, PAD),
        *scatter_buffers(rows, width),
        *[pltpu.SemaphoreType.DMA((experts,))] * 4,
        *[pltpu.SemaphoreType.DMA((6,))] * 4,
    ]


def experts_kernel(rows, out_ref, sel_ref, w_in, w_back, ret_ref, all_ref, pre_ref, *scratch):
    def block(j, part):
        pre = mm(all_ref[j], w_in[...])
        pre_ref[j] = pre
        hidden = gelu_parts(pre)[0].astype(BF16)
        part[j] = mm_nt(hidden, w_back[...]).astype(BF16)

    nothing = lambda: None
    run_experts(rows, out_ref, sel_ref, all_ref, ret_ref, block, nothing, nothing, scratch)


def experts_back_kernel(
    rows, out_ref, sel_ref, w_in, w_back, ent_ref, pre_ref, ret_ref, d_in, d_back, e_in, e_back,
    all_ref, hid_ref, dpre_ref, *scratch
):
    width = w_in.shape[0]

    def block(j, part):
        hidden, slope = gelu_parts(pre_ref[j])
        hid_ref[j] = hidden.astype(BF16)
        dpre = (mm(all_ref[j], w_back[...]) * slope).astype(BF16)
        dpre_ref[j] = dpre
        part[j] = mm_nt(dpre, w_in[...]).astype(BF16)

    def flat(ref):
        return ref[...].reshape(4 * rows, ref.shape[2])

    def beside_one():
        grad = mm_tn(flat(all_ref), flat(hid_ref))
        d_back[...] = grad
        e_back[...] = grad.astype(BF16)

    def beside_two():
        grad = mm_tn(flat(ent_ref), flat(dpre_ref))
        d_in[...] = grad
        e_in[...] = grad.astype(BF16)

    run_experts(rows, out_ref, sel_ref, all_ref, ret_ref, block, beside_one, beside_two, scratch)


def selection(experts, capacity):
    sel = np.zeros((experts * capacity, experts, PAD), np.float32)
    for e in range(experts):
        for s in range(capacity):
            sel[e * capacity + s, e, s] = 1
    return jnp.asarray(sel.reshape(experts * capacity, experts * PAD), BF16)


def experts_forward(outgoing, sel, w_in, w_back):
    experts, _, width = outgoing.shape
    rows = sel.shape[0]
    vm = pl.BlockSpec(memory_space=pltpu.VMEM)
    return pl.pallas_call(
        functools.partial(experts_kernel, rows),
        out_shape=(
            jax.ShapeDtypeStruct(outgoing.shape, BF16),
            jax.ShapeDtypeStruct((4, rows, width), BF16),
            jax.ShapeDtypeStruct((4, rows, w_in.shape[1]), F32),
        ),
        in_specs=[vm] * 4,
        out_specs=(vm,) * 3,
        scratch_shapes=expert_scratch(experts, rows, width),
        compiler_params=pltpu.CompilerParams(
            collective_id=2, has_side_effects=True, vmem_limit_bytes=48 << 20
        ),
    )(outgoing, sel, w_in, w_back)


def experts_backward(outgoing, sel, w_in, w_back, entering, pre):
    experts, _, width = outgoing.shape
    rows, hid = sel.shape[0], w_in.shape[1]
    vm = pl.BlockSpec(memory_space=pltpu.VMEM)
    return pl.pallas_call(
        functools.partial(experts_back_kernel, rows),
        out_shape=(
            jax.ShapeDtypeStruct(outgoing.shape, BF16),
            jax.ShapeDtypeStruct(w_in.shape, F32),
            jax.ShapeDtypeStruct(w_back.shape, F32),
            jax.ShapeDtypeStruct(w_in.shape, BF16),
            jax.ShapeDtypeStruct(w_back.shape, BF16),
        ),
        in_specs=[vm] * 6,
        out_specs=(vm,) * 5,
        scratch_shapes=[
            pltpu.VMEM((4, rows, width), BF16),
            pltpu.VMEM((4, rows, hid), BF16),
            pltpu.VMEM((4, rows, hid), BF16),
            *expert_scratch(experts, rows, width),
        ],
        compiler_params=pltpu.CompilerParams(
            collective_id=3, has_side_effects=True, vmem_limit_bytes=48 << 20
        ),
    )(outgoing, sel, w_in, w_back, entering, pre)


def bucket_bounds():
    half = BUCKETS // 2
    powers = np.arange(1, BUCKETS - half) / (BUCKETS - half)
    return [int(m) for m in np.ceil(half * (REACH / half) ** powers)]


def tile_buckets(kind):
    row = lax.broadcasted_iota(jnp.int32, (SPAN, 2 * SPAN), 0)
    col = lax.broadcasted_iota(jnp.int32, (SPAN, 2 * SPAN), 1)
    ahead = kind * SPAN + row - lax.rem(col, SPAN)
    n = jnp.maximum(ahead, 0)
    bucket = jnp.minimum(n, BUCKETS // 2)
    for bound in bucket_bounds():
        bucket += (n >= bound).astype(jnp.int32)
    return ahead, bucket


def tile_range(kind):
    half = BUCKETS // 2
    ends = [max(kind * SPAN + r - c, 0) for r, c in ((0, SPAN - 1), (SPAN - 1, 0))]
    first, last = (min(n, half) + sum(n >= m for m in bucket_bounds()) for n in ends)
    return range(first, last + 1)


def make_tiles(table_ref, tiles_ref, heads):
    repeat = tiles_ref.shape[3] // (2 * SPAN)
    for k in range(KINDS - 1):
        ahead, bucket = tile_buckets(k)
        for h in range(heads):
            tile = jnp.full(bucket.shape, NEG, F32)
            for b in tile_range(k):
                tile = jnp.where(bucket == b, table_ref[b : b + 1, h : h + 1], tile)
            tile = jnp.where(ahead < 0, NEG, tile)
            tiles_ref[h, k] = jnp.concatenate([tile] * repeat, 1)


def bias_rows(tiles_ref, table_ref, kind_ref, head, block):
    kind = kind_ref[block : block + 1, :]
    last = table_ref[BUCKETS - 1 : BUCKETS, head : head + 1]
    rows = jnp.where(kind == 3, last, NEG)
    for k in (2, 1, 0):
        rows = jnp.where(kind == k, tiles_ref[head, k], rows)
    return rows


def head_columns(ref, group, head, heads):
    at = (group * heads + head) * HEAD_DIM
    return ref[:, at : at + HEAD_DIM]


def meet_ring(partner):
    barrier = pltpu.get_barrier_semaphore()
    ctx = lax.axis_index("ctx")
    right, left = lax.rem(ctx + 1, 4), lax.rem(ctx + 3, 4)
    for neighbour in (left, right):
        pl.semaphore_signal(barrier, inc=1, device_id={"ctx": neighbour}, device_id_type=MESH)
    if partner is not None:
        pl.semaphore_signal(barrier, inc=1, device_id={"section": partner}, device_id_type=MESH)
    pl.semaphore_wait(barrier, 2 if partner is None else 3)
    return ctx, right, left


def attend_kernel(
    heads, x_ref, gain_ref, w_qkv, w_out, table_ref, kind_ref,
    middle_ref, all_ref, proj_ref, att_ref,
    tiles_ref, s_ref, p_ref, part, *scratch
):
    bufs, (s_ag, r_ag, s_rs, r_rs) = scratch[:6], scratch[6:]
    ids = meet_ring(None)
    me, right, left = ids
    far = lax.rem(me + 2, 4)
    rows, width = x_ref.shape
    seq = 4 * rows
    all_ref[me] = norm(x_ref[...], gain_ref[...])
    gather = RingGather(all_ref, rows, ids, s_ag, r_ag)
    gather.start()
    make_tiles(table_ref, tiles_ref, heads)
    gather.forward()
    gather.wait_left()
    gather.wait_right()
    gather.wait_far()
    proj_ref[...] = mm(all_ref[...].reshape(seq, width), w_qkv[...]).astype(BF16)
    parts = []
    for h in range(heads):
        q, k, v = (head_columns(proj_ref, g, h, heads) for g in range(3))
        s_ref[...] = mm_nt(q, k)
        for b in range(seq // SPAN):
            at = slice(b * SPAN, (b + 1) * SPAN)
            s = s_ref[at, :] * HEAD_DIM**-0.5 + bias_rows(tiles_ref, table_ref, kind_ref, h, b)
            e = jnp.exp(s - jnp.max(s, -1, keepdims=True))
            p_ref[at, :] = (e * (1.0 / jnp.sum(e, -1, keepdims=True))).astype(BF16)
        parts.append(mm(p_ref[...], v).astype(BF16))
    att_ref[...] = jnp.concatenate(parts, 1).reshape(att_ref.shape)
    scatter = RingScatter(part, rows, ids, bufs, s_rs, r_rs)
    part[far] = mm(att_ref[far], w_out[...]).astype(BF16)
    scatter.send_far()
    part[right] = mm(att_ref[right], w_out[...]).astype(BF16)
    scatter.send_right()
    part[left] = mm(att_ref[left], w_out[...]).astype(BF16)
    scatter.send_left()
    part[me] = mm(att_ref[me], w_out[...]).astype(BF16)
    scatter.send_sums()
    middle_ref[...] = x_ref[...] + scatter.total()
    gather.wait_send()
    scatter.wait_send()


def attend(x, gain, w_qkv, w_out, table, kind):
    rows, width = x.shape
    seq = 4 * rows
    part = w_out.shape[0]
    heads = part // HEAD_DIM
    vm = pl.BlockSpec(memory_space=pltpu.VMEM)
    return pl.pallas_call(
        functools.partial(attend_kernel, heads),
        out_shape=(
            jax.ShapeDtypeStruct(x.shape, F32),
            jax.ShapeDtypeStruct((4, rows, width), BF16),
            jax.ShapeDtypeStruct((seq, 3 * part), BF16),
            jax.ShapeDtypeStruct((4, rows, part), BF16),
        ),
        in_specs=[vm] * 6,
        out_specs=(vm,) * 4,
        scratch_shapes=[
            pltpu.VMEM((heads, KINDS - 1, SPAN, seq), F32),
            pltpu.VMEM((seq, seq), F32),
            pltpu.VMEM((seq, seq), BF16),
            pltpu.VMEM((4, rows, width), BF16),
            *scatter_buffers(rows, width),
            *[pltpu.SemaphoreType.DMA((6,))] * 4,
        ],
        compiler_params=pltpu.CompilerParams(
            collective_id=0, has_side_effects=True, vmem_limit_bytes=48 << 20
        ),
    )(x, gain, w_qkv, w_out, table, kind)


def attend_back_kernel(
    heads, dmid_ref, all_ref, proj_ref, att_ref, w_qkv, w_out, table_ref, kind_ref,
    e_in, e_back, perm_ref, perm_out_ref,
    dnormed_ref, pq_ref, po_ref, dtable_ref, got_in, got_back, got_pq, got_po,
    tiles_ref, dtiles_ref, s_ref, dp_ref, p_ref, ds_ref, da_ref, dproj_ref, db_ref, part, *scratch
):
    bufs, (s_ag, r_ag, s_rs, r_rs, s_x, r_x) = scratch[:6], scratch[6:]
    partner = 1 - lax.axis_index("section")
    ids = meet_ring(partner)
    me, right, left = ids
    far = lax.rem(me + 2, 4)
    rows, width = dmid_ref.shape
    seq = 4 * rows
    scale = HEAD_DIM**-0.5

    def across(k, src, dst):
        return remote(src, dst, s_x, r_x, k, "section", partner)

    crossing = [
        across(0, e_in, got_in),
        across(1, e_back, got_back),
        across(2, pq_ref, got_pq),
        across(3, po_ref, got_po),
    ]
    db_ref[me] = dmid_ref[...].astype(BF16)
    gather = RingGather(db_ref, rows, ids, s_ag, r_ag)
    gather.start()
    crossing[0].start()
    crossing[1].start()
    make_tiles(table_ref, tiles_ref, heads)
    gather.forward()
    gather.wait_left()
    gather.wait_right()
    gather.wait_far()
    da_ref[...] = mm_nt(db_ref[...].reshape(seq, width), w_out[...]).astype(BF16)
    dq, dk, dv = [], [], []
    for h in range(heads):
        q, k, v = (head_columns(proj_ref, g, h, heads) for g in range(3))
        da = head_columns(da_ref, 0, h, heads)
        s_ref[...] = mm_nt(q, k)
        dp_ref[...] = mm_nt(da, v)
        dtiles_ref[...] = jnp.zeros(dtiles_ref.shape, F32)
        for b in range(seq // SPAN):
            at = slice(b * SPAN, (b + 1) * SPAN)
            s = s_ref[at, :] * scale + bias_rows(tiles_ref, table_ref, kind_ref, h, b)
            e = jnp.exp(s - jnp.max(s, -1, keepdims=True))
            p = e * (1.0 / jnp.sum(e, -1, keepdims=True))
            dp = dp_ref[at, :]
            ds = p * (dp - jnp.sum(p * dp, -1, keepdims=True))
            p_ref[at, :] = p.astype(BF16)
            ds_ref[at, :] = ds.astype(BF16)
            kind = kind_ref[b : b + 1, :]
            for n in range(KINDS):
                dtiles_ref[n] += jnp.where(kind == n, ds, 0.0)
        for n in range(KINDS):
            folded = dtiles_ref[n, :, : 2 * SPAN]
            for m in range(1, seq // (2 * SPAN)):
                folded = folded + dtiles_ref[n, :, m * 2 * SPAN : (m + 1) * 2 * SPAN]
            dtiles_ref[n, :, : 2 * SPAN] = folded
        sums = [jnp.zeros((1, 2 * SPAN), F32)] * BUCKETS
        for n in range(KINDS - 1):
            bucket = tile_buckets(n)[1]
            folded = dtiles_ref[n, :, : 2 * SPAN]
            for b in tile_range(n):
                hit = jnp.where(bucket == b, folded, 0.0)
                sums[b] = sums[b] + jnp.sum(hit, 0, keepdims=True)
        rest = dtiles_ref[KINDS - 1, :, : 2 * SPAN]
        sums[-1] = sums[-1] + jnp.sum(rest, 0, keepdims=True)
        dtable_ref[h] = jnp.concatenate(sums, 0)
        p = p_ref[...]
        ds = ds_ref[...]
        dq.append((mm(ds, k) * scale).astype(BF16))
        dk.append((mm_tn(ds, q) * scale).astype(BF16))
        dv.append(mm_tn(p, da).astype(BF16))
    dproj_ref[...] = jnp.concatenate(dq + dk + dv, 1).reshape(dproj_ref.shape)
    scatter = RingScatter(part, rows, ids, bufs, s_rs, r_rs)
    part[far] = mm_nt(dproj_ref[far], w_qkv[...]).astype(BF16)
    scatter.send_far()
    part[right] = mm_nt(dproj_ref[right], w_qkv[...]).astype(BF16)
    scatter.send_right()
    part[left] = mm_nt(dproj_ref[left], w_qkv[...]).astype(BF16)
    scatter.send_left()
    part[me] = mm_nt(dproj_ref[me], w_qkv[...]).astype(BF16)
    dproj = dproj_ref[...].reshape(seq, dproj_ref.shape[2])
    d_qkv = mm_tn(all_ref[...].reshape(seq, width), dproj).astype(BF16)
    pq_ref[...] = mm(perm_ref[...], d_qkv).astype(BF16)
    crossing[2].start()
    scatter.send_sums()
    d_out = mm_tn(att_ref[...].reshape(seq, att_ref.shape[2]), db_ref[...].reshape(seq, width))
    po_ref[...] = mm(perm_out_ref[...], d_out.astype(BF16)).astype(BF16)
    crossing[3].start()
    dnormed_ref[...] = scatter.total()
    gather.wait_send()
    scatter.wait_send()
    for c in crossing:
        c.wait()


def attend_back(dmiddle, normed, proj, att, w_qkv, w_out, table, kind, e_in, e_back, perm, perm_out):
    rows, width = dmiddle.shape
    seq = 4 * rows
    part = w_out.shape[0]
    heads = part // HEAD_DIM
    vm = pl.BlockSpec(memory_space=pltpu.VMEM)
    pq = jax.ShapeDtypeStruct((perm.shape[0], 3 * part), BF16)
    po = jax.ShapeDtypeStruct((perm_out.shape[0], width), BF16)
    return pl.pallas_call(
        functools.partial(attend_back_kernel, heads),
        out_shape=(
            jax.ShapeDtypeStruct((rows, width), F32),
            pq,
            po,
            jax.ShapeDtypeStruct((heads, BUCKETS, 2 * SPAN), F32),
            jax.ShapeDtypeStruct(e_in.shape, BF16),
            jax.ShapeDtypeStruct(e_back.shape, BF16),
            pq,
            po,
        ),
        in_specs=[vm] * 12,
        out_specs=(vm,) * 8,
        scratch_shapes=[
            pltpu.VMEM((heads, KINDS - 1, SPAN, seq), F32),
            pltpu.VMEM((KINDS, SPAN, seq), F32),
            pltpu.VMEM((seq, seq), F32),
            pltpu.VMEM((seq, seq), F32),
            pltpu.VMEM((seq, seq), BF16),
            pltpu.VMEM((seq, seq), BF16),
            pltpu.VMEM((seq, part), BF16),
            pltpu.VMEM((4, rows, 3 * part), BF16),
            pltpu.VMEM((4, rows, width), BF16),
            pltpu.VMEM((4, rows, width), BF16),
            *scatter_buffers(rows, width),
            *[pltpu.SemaphoreType.DMA((6,))] * 4,
            *[pltpu.SemaphoreType.DMA((4,))] * 2,
        ],
        compiler_params=pltpu.CompilerParams(
            collective_id=1, has_side_effects=True, vmem_limit_bytes=52 << 20
        ),
    )(dmiddle, normed, proj, att, w_qkv, w_out, table, kind, e_in, e_back, perm, perm_out)


def meet_everyone():
    barrier = pltpu.get_barrier_semaphore()
    peers = [("exp", 16), ("ctx", 4), ("section", 2)]
    for axis, count in peers:
        me = lax.axis_index(axis)

        def greet(k, carry, axis=axis, me=me, count=count):
            peer = lax.rem(me + k, count)
            pl.semaphore_signal(barrier, inc=1, device_id={axis: peer}, device_id_type=MESH)
            return carry

        lax.fori_loop(1, count, greet, 0)
    pl.semaphore_wait(barrier, sum(count - 1 for _, count in peers))


def ctx_exchange(src, dst, send, recv):
    me = lax.axis_index("ctx")
    copies = []
    for k in (1, 3, 2):
        peer = lax.rem(me + k, 4)
        copies.append(remote(src.at[peer], dst.at[me], send, recv, k, "ctx", peer))
    return copies


def weights_kernel(
    cols_ref, outp_ref, w_in, w_back, perm_ref, perm_out_ref, pick_ref,
    w_qkv, w_out, small_ref, both_in, both_back,
    zin, grid, grid_out, s_z, r_z, s_q, r_q, s_o, r_o, s_fq, r_fq, s_fo, r_fo, s_x, r_x, s_own
):
    meet_everyone()
    section, ctx, exp = (lax.axis_index(a) for a in ("section", "ctx", "exp"))
    partner = 1 - section
    count = grid.shape[1]
    turn = ctx_exchange(cols_ref, zin, s_z, r_z)
    for c in turn:
        c.start()
    zin[ctx] = cols_ref[ctx]
    grid_out[section, exp] = outp_ref[...]

    def spread(ref, send, recv, k):
        peer = lax.rem(exp + k, count)
        at = ref.at[section, exp]
        return remote(at, at, send, recv, k, "exp", peer)

    def forward(ref, send, recv, k):
        at = ref.at[section, lax.rem(exp + count - k, count)]
        return remote(at, at, send, recv, k, "section", partner)

    def each(act, first=1):
        def body(k, carry):
            act(k)
            return carry

        lax.fori_loop(first, count, body, 0)

    each(lambda k: spread(grid_out, s_o, r_o, k).start())
    for c in turn:
        c.wait_recv()
    grid[section, exp] = zin[...].reshape(grid.shape[2:])
    each(lambda k: spread(grid, s_q, r_q, k).start())
    forward(grid, s_fq, r_fq, 0).start()
    forward(grid_out, s_fo, r_fo, 0).start()
    own_in = pltpu.make_async_copy(w_in, both_in.at[section], s_own.at[0])
    own_back = pltpu.make_async_copy(w_back, both_back.at[section], s_own.at[1])
    own_in.start()
    own_back.start()
    cross_in = remote(w_in, both_in.at[section], s_x, r_x, 0, "section", partner)
    cross_back = remote(w_back, both_back.at[section], s_x, r_x, 1, "section", partner)

    def relay(ref, s, r, sf, rf, k):
        spread(ref, s, r, k).wait_recv()
        forward(ref, sf, rf, k).start()

    each(lambda k: relay(grid_out, s_o, r_o, s_fo, r_fo, k))
    each(lambda k: relay(grid, s_q, r_q, s_fq, r_fq, k))
    cross_in.start()
    cross_back.start()

    def unpack(layer):
        flat = grid[layer].reshape(perm_ref.shape[0], grid.shape[3])
        w_qkv[layer] = mm_tn(perm_ref[...], flat).astype(BF16)
        small_ref[layer] = mm(pick_ref[...], flat)
        flat = grid_out[layer].reshape(perm_out_ref.shape[0], grid_out.shape[3])
        w_out[layer] = mm_tn(perm_out_ref[...], flat).astype(BF16)

    unpack(section)
    each(lambda k: forward(grid_out, s_fo, r_fo, k).wait_recv(), 0)
    each(lambda k: forward(grid, s_fq, r_fq, k).wait_recv(), 0)
    unpack(partner)
    each(lambda k: spread(grid_out, s_o, r_o, k).wait_send())
    each(lambda k: spread(grid, s_q, r_q, k).wait_send())
    each(lambda k: forward(grid_out, s_fo, r_fo, k).wait_send(), 0)
    each(lambda k: forward(grid, s_fq, r_fq, k).wait_send(), 0)
    for c in turn:
        c.wait_send()
    own_in.wait()
    own_back.wait()
    cross_in.wait()
    cross_back.wait()


def gather_weights(cols, outp, w_in, w_back, perm, perm_out, pick):
    width, part = outp.shape[1], cols.shape[2]
    count = perm_out.shape[0] // 16
    vm = pl.BlockSpec(memory_space=pltpu.VMEM)
    dma = lambda n: pltpu.SemaphoreType.DMA((n,))
    return pl.pallas_call(
        weights_kernel,
        out_shape=(
            jax.ShapeDtypeStruct((2, width, part), BF16),
            jax.ShapeDtypeStruct((2, perm_out.shape[1], width), BF16),
            jax.ShapeDtypeStruct((2, pick.shape[0], part), F32),
            jax.ShapeDtypeStruct((2, *w_in.shape), BF16),
            jax.ShapeDtypeStruct((2, *w_back.shape), BF16),
        ),
        in_specs=[vm] * 7,
        out_specs=(vm,) * 5,
        scratch_shapes=[
            pltpu.VMEM(cols.shape, BF16),
            pltpu.VMEM((2, count, 64, part), BF16),
            pltpu.VMEM((2, count, 16, width), BF16),
            dma(4), dma(4), *[dma(count)] * 8, dma(2), dma(2), dma(2),
        ],
        compiler_params=pltpu.CompilerParams(
            collective_id=4, has_side_effects=True, vmem_limit_bytes=48 << 20
        ),
    )(cols, outp, w_in, w_back, perm, perm_out, pick)


def owners_kernel(
    pq0, pq1, gq0, gq1, po0, po1, go0, go1, small_ref, spread_ref,
    in0, in1, gin0, gin1, back0, back1, gback0, gback1,
    turned, out_grad, d_in, d_back,
    got_small, pieces, box, pieces_out, box_out, summed, s_s, r_s, s_q, r_q, s_o, r_o, s_z, r_z
):
    meet_everyone()
    section, ctx, exp = (lax.axis_index(a) for a in ("section", "ctx", "exp"))
    partner = 1 - section
    first = section == 0
    cross = remote(small_ref.at[partner], got_small, s_s, r_s, 0, "section", partner)
    cross.start()

    def chosen(a, b, c, d):
        return jnp.where(first, a[...], b[...]).astype(F32) + jnp.where(
            first, c[...], d[...]
        ).astype(F32)

    pieces_out[...] = chosen(po0, po1, go0, go1).astype(BF16).reshape(pieces_out.shape)
    swap_out = Exchange(pieces_out, box_out, s_o, r_o)
    swap_out.start()
    dense = chosen(pq0, pq1, gq0, gq1)
    cross.wait_recv()
    small = small_ref[section] + got_small[...]
    wide = mm(spread_ref[...], small.astype(BF16))
    n = wide.shape[1]
    dense = jnp.concatenate([dense[:, :n] + wide, dense[:, n:]], 1)
    pieces[...] = dense.astype(BF16).reshape(pieces.shape)
    swap = Exchange(pieces, box, s_q, r_q)
    swap.start()
    d_in[...] = chosen(in0, in1, gin0, gin1)
    d_back[...] = chosen(back0, back1, gback0, gback1)
    swap_out.wait_recv()
    total = box_out[0].astype(F32)
    for k in range(1, box_out.shape[0]):
        total = total + box_out[k].astype(F32)
    out_grad[...] = total
    swap.wait_recv()
    total = box[0].astype(F32)
    for k in range(1, box.shape[0]):
        total = total + box[k].astype(F32)
    summed[...] = total.reshape(summed.shape)
    turn = ctx_exchange(summed, turned, s_z, r_z)
    for c in turn:
        c.start()
    turned[ctx] = summed[ctx]
    for c in turn:
        c.wait()
    cross.wait_send()
    swap.wait_send()
    swap_out.wait_send()


def sum_at_owners(pq, gq, po, go, small, spread, d_in, g_in, d_back, g_back, count):
    rows, part = pq[0].shape
    out_rows, width = po[0].shape
    vm = pl.BlockSpec(memory_space=pltpu.VMEM)
    dma = lambda n: pltpu.SemaphoreType.DMA((n,))
    own = (rows // count, part)
    own_out = (out_rows // count, width)
    quarter = (4, rows // count // 4, part)
    return pl.pallas_call(
        owners_kernel,
        out_shape=(
            jax.ShapeDtypeStruct(quarter, F32),
            jax.ShapeDtypeStruct(own_out, F32),
            jax.ShapeDtypeStruct(d_in[0].shape, F32),
            jax.ShapeDtypeStruct(d_back[0].shape, F32),
        ),
        in_specs=[vm] * 18,
        out_specs=(vm,) * 4,
        scratch_shapes=[
            pltpu.VMEM(small.shape[1:], F32),
            pltpu.VMEM((count, *own), BF16),
            pltpu.VMEM((count, *own), BF16),
            pltpu.VMEM((count, *own_out), BF16),
            pltpu.VMEM((count, *own_out), BF16),
            pltpu.VMEM(quarter, F32),
            dma(1), dma(1), *[dma(count)] * 4, dma(4), dma(4),
        ],
        compiler_params=pltpu.CompilerParams(
            collective_id=5, has_side_effects=True, vmem_limit_bytes=52 << 20
        ),
    )(*pq, *gq, *po, *go, small, spread, *d_in, *g_in, *d_back, *g_back)


def packing(n_ctx, n_exp, own_rows):
    blocks = n_ctx * n_exp
    perm = np.zeros((blocks, 16, blocks, own_rows), np.float32)
    pick = np.zeros((blocks, blocks, 16), np.float32)
    perm_out = np.zeros((n_exp, 16, n_exp, own_rows), np.float32)
    for e in range(n_exp):
        for i in range(own_rows):
            perm_out[e, i, e, i] = 1
        for c in range(n_ctx):
            for i in range(own_rows):
                perm[e * n_ctx + c, i, c * n_exp + e, i] = 1
            pick[c * n_exp + e, e * n_ctx + c, own_rows] = 1
    perm = perm.reshape(blocks * 16, blocks * own_rows)
    pick = pick.reshape(blocks, blocks * 16)
    perm_out = perm_out.reshape(n_exp * 16, n_exp * own_rows)
    return tuple(jnp.asarray(m, BF16) for m in (perm, pick, pick.T.copy(), perm_out))


def norm_scale(v):
    return lax.rsqrt(jnp.mean(v * v, -1, keepdims=True) + EPS)


def norm(v, gain):
    return (v * norm_scale(v) * gain).astype(BF16)


def norm_back(v, gain, du):
    r = norm_scale(v)
    dug = du * gain
    dv = r * dug - v * (r * r * r) * jnp.mean(dug * v, -1, keepdims=True)
    return dv, jnp.sum(du * v * r, 0)


def gelu_parts(v):
    t = jnp.tanh(GELU_C * (v + 0.044715 * v * v * v))
    value = 0.5 * v * (1.0 + t)
    slope = 0.5 * (1.0 + t) + 0.5 * v * (1.0 - t * t) * GELU_C * (1.0 + 3 * 0.044715 * v * v)
    return value, slope


def slot_tables(routes, experts):
    rows = routes.shape[0]
    flat = routes.reshape(rows * TOP)
    hot = flat[:, None] == jnp.arange(experts, dtype=jnp.int32)
    before = np.tril(np.ones((rows * TOP, rows * TOP), np.float32), -1)
    earlier = mm(jnp.asarray(before, BF16), hot.astype(BF16))
    slot = jnp.sum(jnp.where(hot, earlier, 0.0), -1).astype(jnp.int32)
    target = (flat * PAD + slot).reshape(rows, TOP)
    slots = jnp.arange(experts * PAD, dtype=jnp.int32)
    slot_hot = [(target[:, c : c + 1] == slots).astype(BF16) for c in range(TOP)]
    route_hot = [(routes[:, c : c + 1] == jnp.arange(experts)).astype(F32) for c in range(TOP)]
    return route_hot, slot_hot


def on_device(
    inputs,
    cotangent,
    routes,
    block_order,
    attn_gain,
    qkv_weight,
    out_weight,
    rel_bias,
    moe_gain,
    router_weight,
    expert_in,
    expert_out,
):
    rows, width = inputs.shape[2:]
    n_ctx, n_exp = lax.axis_size("ctx"), lax.axis_size("exp")
    seq = rows * n_ctx
    own_rows = qkv_weight.shape[1]
    heads = HEADS // n_ctx
    part = heads * HEAD_DIM
    capacity = rows * TOP // n_exp + max(1, rows * TOP // (16 * n_exp))
    slots = n_exp * PAD
    sel = selection(n_exp, capacity)
    section = lax.axis_index("section")
    ctx = lax.axis_index("ctx")
    first = section == 0

    perm, pick, place, perm_out = packing(n_ctx, n_exp, own_rows)
    small = jnp.concatenate(
        [attn_gain[0], moe_gain[0], rel_bias[0], router_weight[0].reshape(-1)]
    )
    n_small = small.shape[0]
    columns = qkv_weight[0].reshape(own_rows, 3, n_ctx, part).transpose(2, 0, 1, 3)
    columns = columns.reshape(n_ctx, own_rows, 3 * part)
    small_row = jnp.pad(small, (0, 3 * part - n_small))
    small_rows = jnp.broadcast_to(small_row, (n_ctx, 1, 3 * part))
    columns = jnp.concatenate([columns, small_rows], 1)
    columns = jnp.pad(columns, ((0, 0), (0, 15 - own_rows), (0, 0)))
    out_rows = jnp.pad(out_weight[0], ((0, 16 - own_rows), (0, 0)))
    w_qkv_both, w_out_both, small_both, w_in_both, w_back_both = gather_weights(
        columns, out_rows, expert_in[0, 0], expert_out[0, 0], perm, perm_out, pick
    )
    n_bias = BUCKETS * HEADS // (n_ctx * n_exp)

    def dense(layer):
        small = small_both[layer]
        gain_one = small[:, :own_rows].reshape(1, width)
        gain_two = small[:, own_rows : 2 * own_rows].reshape(1, width)
        table = small[:, 2 * own_rows : 2 * own_rows + n_bias].reshape(BUCKETS, HEADS)
        table = lax.dynamic_slice_in_dim(table, ctx * heads, heads, 1)
        router = small[:, 2 * own_rows + n_bias : n_small].reshape(width, n_exp).astype(BF16)
        return (
            w_qkv_both[layer], w_out_both[layer], gain_one, gain_two, table, router,
            w_in_both[layer], w_back_both[layer],
        )

    weights = [dense(0), dense(1)]
    ahead = block_order[:, None] - block_order[None, :]
    kind = jnp.repeat(jnp.where(ahead < 0, -1, jnp.minimum(ahead, 3)), SPAN, 1)

    own_routes = routes[0, :, 0]
    kept = jnp.where(first, own_routes[0], own_routes[1])
    given = jnp.where(first, own_routes[1], own_routes[0])
    taken = lax.ppermute(given, "section", [(0, 1), (1, 0)])
    layer_routes = (jnp.where(first, kept, taken), jnp.where(first, taken, kept))
    tables = [slot_tables(r, n_exp) for r in layer_routes]

    def forward(x, layer):
        w_qkv, w_out, gain_one, gain_two, table, router, w_in, w_back = weights[layer]
        route_hot, slot_hot = tables[layer]
        middle, normed, proj, attended = attend(x, gain_one, w_qkv, w_out, table, kind)
        mixed = norm(middle, gain_two)
        logits = mm(mixed, router)
        chosen = [jnp.sum(h * logits, -1, keepdims=True) for h in route_hot]
        peak = jnp.maximum(chosen[0], chosen[1])
        raised = [jnp.exp(c - peak) for c in chosen]
        gates = [r / (raised[0] + raised[1]) for r in raised]
        placing = slot_hot[0] + slot_hot[1]
        outgoing = mm_tn(placing, mixed).astype(BF16).reshape(n_exp, PAD, width)
        returned, entering, pre = experts_forward(outgoing, sel, w_in, w_back)
        returned = returned.reshape(slots, width)
        picked = [mm(h, returned) for h in slot_hot]
        y = middle + gates[0] * picked[0] + gates[1] * picked[1]
        keep = (x, normed, proj, attended, middle, mixed, gates, picked, entering, pre)
        return y, keep

    def backward(g, keep, layer):
        x, normed, proj, attended, middle, mixed, gates, picked, entering, pre = keep
        w_qkv, w_out, gain_one, gain_two, table, router, w_in, w_back = weights[layer]
        route_hot, slot_hot = tables[layer]
        dreturned = mm_tn(slot_hot[0], (gates[0] * g).astype(BF16)) + mm_tn(
            slot_hot[1], (gates[1] * g).astype(BF16)
        )
        dreturned = dreturned.astype(BF16).reshape(n_exp, PAD, width)
        dleft, d_in, d_back, e_in, e_back = experts_backward(dreturned, sel, w_in, w_back, entering, pre)
        dleft = dleft.reshape(slots, width)
        dgates = [jnp.sum(g * p, -1, keepdims=True) for p in picked]
        mean = gates[0] * dgates[0] + gates[1] * dgates[1]
        dchosen = [a * (b - mean) for a, b in zip(gates, dgates)]
        dlogits = route_hot[0] * dchosen[0] + route_hot[1] * dchosen[1]
        dlogits = dlogits.astype(BF16)
        d_router = mm_tn(mixed, dlogits)
        dmixed = mm(slot_hot[0] + slot_hot[1], dleft) + mm_nt(dlogits, router)
        dnorm, d_gain_two = norm_back(middle, gain_two, dmixed)
        dmiddle = g + dnorm
        dnormed, pq, po, d_table, g_in, g_back, gq, go = attend_back(
            dmiddle, normed, proj, attended, w_qkv, w_out, table, kind, e_in, e_back, perm, perm_out
        )
        dnorm, d_gain_one = norm_back(x, gain_one, dnormed)
        d_table = jnp.repeat(jnp.sum(d_table, -1).T, 2, axis=0)
        owner = jnp.arange(n_ctx * n_exp)[:, None]
        d_table = jnp.where(owner % 2 == ctx // 2, d_table, 0.0)
        even = ctx % 2 == 0
        d_table = [jnp.where(even, d_table, 0.0), jnp.where(even, 0.0, d_table)]
        owners = (n_ctx * n_exp, -1)
        d_small = jnp.concatenate(
            [d_gain_one.reshape(owners), d_gain_two.reshape(owners), *d_table,
             d_router.reshape(owners)],
            1,
        )
        d_small = jnp.pad(d_small, ((0, 0), (0, 256 - n_small)))
        return dmiddle + dnorm, (pq, gq, po, go, d_small, d_in, g_in, d_back, g_back)

    def swap(x):
        return lax.ppermute(x, "section", [(0, 1), (1, 0)])

    x = jnp.where(first, inputs[0, 0], inputs[1, 0]).astype(F32)
    cot = jnp.where(first, cotangent[0, 0], cotangent[1, 0]).astype(F32)
    y0, keep0 = forward(x, 0)
    h = y0.astype(BF16)
    y1, keep1 = forward(h.astype(F32), 1)
    top = y1.astype(BF16)
    dh, grads1 = backward(cot, keep1, 1)
    dh = dh.astype(BF16)
    dx, grads0 = backward(dh.astype(F32), keep0, 0)
    pq, gq, po, go, d_small, d_in, g_in, d_back, g_back = zip(grads0, grads1)
    pieces, out_grad, d_in, d_back = sum_at_owners(
        pq, gq, po, go, jnp.stack(d_small), place, d_in, g_in, d_back, g_back, n_exp
    )
    qkv_grad = pieces[:, :own_rows].reshape(n_ctx, own_rows, 3, part)
    qkv_grad = qkv_grad.transpose(1, 2, 0, 3).reshape(own_rows, 3 * width)
    out_grad = out_grad[:own_rows]
    small = jnp.sum(pieces[:, own_rows, :n_small], 0)

    other = swap(jnp.where(first, top, h))
    layer_out = jnp.where(
        first, jnp.stack([h, other]), jnp.stack([other, top])
    ).reshape(1, 2, 1, rows, width)
    dh = dh.astype(F32)
    other = swap(jnp.where(first, dh, dx))
    input_grad = jnp.where(
        first, jnp.stack([dx, other]), jnp.stack([other, dh])
    ).reshape(1, 2, 1, rows, width)
    return (
        layer_out,
        input_grad,
        small[:own_rows][None],
        qkv_grad[None],
        out_grad[None],
        small[2 * own_rows : 2 * own_rows + n_bias][None],
        small[own_rows : 2 * own_rows][None],
        small[2 * own_rows + n_bias :].reshape(1, own_rows, n_exp),
        d_in[None, None],
        d_back[None, None],
    )


def solution(mesh):
    return jax.shard_map(
        on_device,
        mesh=mesh,
        in_specs=(
            P(None, "exp", "ctx", None),
            P(None, "exp", "ctx", None),
            P("section", None, "exp", "ctx", None),
            P(),
            P("section", ("ctx", "exp")),
            P("section", ("ctx", "exp"), None),
            P("section", ("ctx", "exp"), None),
            P("section", ("ctx", "exp")),
            P("section", ("ctx", "exp")),
            P("section", ("ctx", "exp"), None),
            P("section", "exp", None, "ctx"),
            P("section", "exp", None, "ctx"),
        ),
        out_specs=(
            P("section", None, "exp", "ctx", None),
            P("section", None, "exp", "ctx", None),
            P("section", ("ctx", "exp")),
            P("section", ("ctx", "exp"), None),
            P("section", ("ctx", "exp"), None),
            P("section", ("ctx", "exp")),
            P("section", ("ctx", "exp")),
            P("section", ("ctx", "exp"), None),
            P("section", "exp", None, "ctx"),
            P("section", "exp", None, "ctx"),
        ),
        check_vma=False,
    )
```

time: 587 us -> 524 us (0.89)
  Pallas kernels: 321 us -> 418 us
  starting transfers between devices: 41.9 us -> 0.5 us
  blocking collectives: 35 us -> 0 us
  other arithmetic: 49.5 us -> 19.1 us
  waiting for transfers between devices: 23.2 us -> 0.01 us
  matrix products: 28 us -> 14.5 us
  between operations: 16 us -> 2.76 us
    pallas_call x2, Pallas kernels: 9.34 us -> 61.2 us  [attend_back(): pl.pallas_call(functools.partial(attend_back_kernel, heads), out_shape=(j...]
    pallas_call x10 -> x4, Pallas kernels: 87.8 us -> 127 us  [the longest x2 44.9 us: attend(): pl.pallas_call(functools.partial(attend_kernel, heads), out_shape=(jax.Sh...]
    all_gather x1 -> x0, blocking collectives: 24 us -> none  [on_device(): lax.all_gather(jnp.pad(out_weight[0], ((0, 4), (0, 0))), 'exp', axis=0)]
    ppermute x14 -> x0, starting transfers between devices: 23.8 us -> none  [the longest x5 16.8 us: on_device(): sent1 = [lax.ppermute(p.astype(BF16), 'section', [(0, 1)]) for p in grads1]]
    all_to_all x3 -> x0, starting transfers between devices: 17.8 us -> none  [the longest x2 14.3 us: exp_swap(): return lax.all_to_all(x, 'exp', split_axis=0, concat_axis=0, tiled=True)]
    reshape x17 -> x4, local copies, waits for them, and re-layouts: 17 us -> 1.7 us  [the longest x2 1.56 us: dense(): gain_one = small[:, :own_rows].reshape(1, width)]
    all_gather x1 -> x0, waiting for transfers between devices: 14.1 us -> none  [on_device(): lax.all_gather(columns.reshape(n_ctx * 16, 3 * part), 'exp', axis=0)]
    dot_general x38 -> x20, matrix products: 28 us -> 14.5 us  [dot(): return lax.dot_general(a, b, (dims, ((), ())), preferred_element_type=F32)]
  transfers between devices with their start and end apart: 21 -> 3, of which waited for: 3 -> 0; matrix products, arithmetic and copies ran while one was open for 12% -> 7% of each run, Pallas kernels for 2% -> 12%
where the time goes in v3:
time: 524 us; the launch traced here: 515 us
  Pallas kernels  418 us (80%)
  local copies, waits for them, and re-layouts  60.1 us (11%)
  other arithmetic  19.1 us (4%)
  matrix products  14.5 us (3%)
    pallas_call x2, Pallas kernels, experts_forward(): pl.pallas_call(functools.partial(experts_kernel, rows), out_shape=(jax.Sh...  115 us
    pallas_call x2, Pallas kernels, experts_backward(): pl.pallas_call(functools.partial(experts_back_kernel, rows), out_shape=(j...  114 us
    pallas_call x2, Pallas kernels, attend_back(): pl.pallas_call(functools.partial(attend_back_kernel, heads), out_shape=(j...  61.2 us
    pallas_call x2, Pallas kernels, attend(): pl.pallas_call(functools.partial(attend_kernel, heads), out_shape=(jax.Sh...  44.9 us
    pallas_call x1, Pallas kernels, sum_at_owners(): pl.pallas_call(owners_kernel, out_shape=(jax.ShapeDtypeStruct(quarter, F3...  42.7 us
    pallas_call x1, Pallas kernels, gather_weights(): pl.pallas_call(weights_kernel, out_shape=(jax.ShapeDtypeStruct((2, width,...  39.6 us
    unnamed x253, local copies, waits for them, and re-layouts  20.5 us
    dot_general x20, matrix products, dot(): return lax.dot_general(a, b, (dims, ((), ())), preferred_element_type=F32)  14.5 us
  transfers between devices with their start and end apart: 3, of which 0 were waited for; matrix products, arithmetic and copies ran while one was open for 7% of the time, Pallas kernels for 12%

profile of v3, /device:TPU:2, one launch (start us, length us, event | category | flops | bytes accessed | tf_op | source)
XLA Modules:
  0.0 514.6 jit_solution(17472842955060921054)
XLA Ops:
  10.4 39.6 %shard_map.258 = (bf16[2,768,576]{2,1,0:T(8,128)(2,1)}, bf16[2,192,768]{2,1,0:T(8,128)(2,1)S(1)}, f32[2,64,576]{2,1,0:T(8,128)S(1)}, bf16[2,768,768]{2,1,0:T(8,128)(2,1)}, bf16[2,768,768]{2,1,0:T(8,128)(2,1)}) custom-call(bf16[4,16,576]{2,1,0:T(8,128)(2,1)S(1)} %fusion.63.cols_ref, bf16[16,768]{1,0:T(8,128)(2,1)S(1)} %pad.21.outp_ref, ...), custom_call_target="tpu_custom_call" | custom-call | tf_op jit(solution)/shard_map/pallas_call | solution.py:757
  53.8 2.7 slice_bitcast_fusion.4
  57.3 24.0 %shard_map.259 = (f32[128,768]{1,0:T(8,128)S(1)}, bf16[4,128,768]{2,1,0:T(8,128)(2,1)S(1)}, bf16[512,576]{1,0:T(8,128)(2,1)S(1)}, bf16[4,128,192]{2,1,0:T(8,128)(2,1)S(1)}) custom-call(f32[128,768]{1,0:T(8,128)S(1)} %bitcast_convert_fusion.x_ref, f32[1,768]{1,0:T(1,128)S(1)} %reshape.448.gain_ref, bf16[768,576]{1,0:T(8,128)(2,1)S(1)} %get-tuple-element.189.w_qkv, ...), custom_call_target="tpu_custom_call" | custom-call | tf_op jit(solution)/shard_map/pallas_call | solution.py:486
  85.3 3.7 slice_bitcast_fusion
  89.5 1.7 slice.207
  91.2 1.5 reshape.453.gain_ref
  92.7 1.4 mul.536
  94.1 1.4 mul.570
  95.6 1.6 slice.208
  97.2 1.4 mul.503
  98.6 1.6 convert_element_type.115
  100.2 1.6 convert_element_type.124
  101.8 1.5 bitcast_select_fusion
  103.4 1.5 eq.205
  104.9 1.5 eq.185
  106.5 1.7 slice_reduce_fusion.3
  111.5 1.4 convert_element_type.117
  113.0 1.4 convert_element_type.126
  117.3 60.6 %shard_map.260 = (bf16[16,32,768]{2,1,0:T(8,128)(2,1)S(1)}, bf16[4,272,768]{2,1,0:T(8,128)(2,1)S(1)}, f32[4,272,768]{2,1,0:T(8,128)}) custom-call(bf16[16,32,768]{2,1,0:T(8,128)(2,1)S(1)} %bitcast.123, bf16[272,512]{1,0:T(8,128)(2,1)S(1)} %copy-done.11, bf16[768,768]{1,0:T(8,128)(2,1)S(1)} %get-tuple-element.232.w_in, ...), custom_call_target="tpu_custom_call" | custom-call | tf_op jit(solution)/shard_map/pallas_call | solution.py:330
  181.8 20.9 %shard_map.261 = (f32[128,768]{1,0:T(8,128)S(1)}, bf16[4,128,768]{2,1,0:T(8,128)(2,1)S(1)}, bf16[512,576]{1,0:T(8,128)(2,1)S(1)}, bf16[4,128,192]{2,1,0:T(8,128)(2,1)S(1)}) custom-call(f32[128,768]{1,0:T(8,128)S(1)} %convert_element_type.122.x_ref, f32[1,768]{1,0:T(1,128)S(1)} %copy-done.44, bf16[768,576]{1,0:T(8,128)(2,1)S(1)} %copy-done.10, ...), custom_call_target="tpu_custom_call" | custom-call | tf_op jit(solution)/shard_map/pallas_call | solution.py:486
  205.7 54.5 %shard_map.262 = (bf16[16,32,768]{2,1,0:T(8,128)(2,1)S(1)}, bf16[4,272,768]{2,1,0:T(8,128)(2,1)S(1)}, f32[4,272,768]{2,1,0:T(8,128)}) custom-call(bf16[16,32,768]{2,1,0:T(8,128)(2,1)S(1)} %bitcast.122, bf16[272,512]{1,0:T(8,128)(2,1)S(1)} %copy-done.11, bf16[768,768]{1,0:T(8,128)(2,1)S(1)} %copy-done.3, bf16[768,768]{1,0:T(8,128)(2,1)S(1)} %get-tuple-element.184.w_back), custom_call_target="tpu_custom_call" | custom-call | tf_op jit(solution)/shard_map/pallas_call | solution.py:330
  265.3 54.3 %shard_map.263 = (bf16[16,32,768]{2,1,0:T(8,128)(2,1)S(1)}, f32[768,768]{1,0:T(8,128)}, f32[768,768]{1,0:T(8,128)}, bf16[768,768]{1,0:T(8,128)(2,1)S(1)}, bf16[768,768]{1,0:T(8,128)(2,1)S(1)}) custom-call(bf16[16,32,768]{2,1,0:T(8,128)(2,1)S(1)} %bitcast.119, bf16[272,512]{1,0:T(8,128)(2,1)S(1)} %copy-done.12, bf16[768,768]{1,0:T(8,128)(2,1)S(1)} %copy-done.3, ...), custom_call_target="tpu_custom_call" | custom-call | tf_op jit(solution)/shard_map/pallas_call | solution.py:350
  323.5 30.6 %shard_map.264 = (f32[128,768]{1,0:T(8,128)S(1)}, bf16[1024,576]{1,0:T(8,128)(2,1)}, bf16[256,768]{1,0:T(8,128)(2,1)S(1)}, f32[3,32,128]{2,1,0:T(8,128)S(1)}, bf...) custom-call(f32[128,768]{1,0:T(8,128)} %convert_add_fusion.1.dmid_re, ...), custom_call_target="tpu_custom_call" | custom-call | tf_op jit(solution)/shard_map/pallas_call | solution.py:616
  355.3 1.6 fusion.24
  357.9 2.1 add_convert_fusion
  360.1 59.8 %shard_map.265 = (bf16[16,32,768]{2,1,0:T(8,128)(2,1)S(1)}, f32[768,768]{1,0:T(8,128)}, f32[768,768]{1,0:T(8,128)}, bf16[768,768]{1,0:T(8,128)(2,1)S(1)}, bf16[768,768]{1,0:T(8,128)(2,1)S(1)}) custom-call(bf16[16,32,768]{2,1,0:T(8,128)(2,1)S(1)} %bitcast.118, bf16[272,512]{1,0:T(8,128)(2,1)S(1)} %copy-done.12, bf16[768,768]{1,0:T(8,128)(2,1)S(1)} %get-tuple-element.232.w_in, ...), custom_call_target="tpu_custom_call" | custom-call | tf_op jit(solution)/shard_map/pallas_call | solution.py:350
  423.7 30.6 %shard_map.266 = (f32[128,768]{1,0:T(8,128)S(1)}, bf16[1024,576]{1,0:T(8,128)(2,1)}, bf16[256,768]{1,0:T(8,128)(2,1)S(1)}, f32[3,32,128]{2,1,0:T(8,128)S(1)}, bf...) custom-call(f32[128,768]{1,0:T(8,128)} %convert_add_fusion.dmid_ref,, ...), custom_call_target="tpu_custom_call" | custom-call | tf_op jit(solution)/shard_map/pallas_call | solution.py:616
  455.4 42.7 %shard_map.267 = (f32[4,16,576]{2,1,0:T(8,128)S(1)}, f32[16,768]{1,0:T(8,128)S(1)}, f32[768,768]{1,0:T(8,128)}, f32[768,768]{1,0:T(8,128)}) custom-call(bf16[1024,576]{1,0:T(8,128)(2,1)} %get-tuple-element.86.pq0, bf16[1024,576]{1,0:T(8,128)(2,1)} %get-tuple-element.87.pq1, bf16[1024,576]{1,0:T(8,128)(2,1)} %get-tuple-element.88.gq0, ...), custom_call_target="tpu_custom_call" | custom-call | tf_op jit(solution)/shard_map/pallas_call | solution.py:841
  503.6 1.9 broadcast_in_dim_reshape.6
  506.1 1.9 maximum_select_fusion.1
  508.0 2.1 maximum_select_fusion
  510.1 1.4 copy.72
  (360 shorter events, 55.2 us)
Async XLA Ops:
  2.3 99.5 %collective-permute-start = (s32[128,2]{1,0:T(8,128)}, s32[128,2]{1,0:T(8,128)}, u32[]{:S(2)}, u32[]{:S(2)}) collective-permute-start(s32[128,2]{1,0:T(8,128)} %select_bitcast_fusion), channel_id=1, source_target_pairs={{0,64},{64,0},{1,65},{65,1},{2,66},{66,2},{3,67},{67,3},{4,68},{68... | collective-permute-start | bytes 3080 | tf_op jit(solution)/shard_map/ppermute | solution.py:983
  89.0 116.6 %copy-start.2 = (bf16[768,768]{1,0:T(8,128)(2,1)}, bf16[768,768]{1,0:T(8,128)(2,1)S(1)}, u32[]{:S(2)}) copy-start(bf16[768,768]{1,0:T(8,128)(2,1)S(1)} %get-tuple-element.184.w_back) | copy-start | bytes 3538948
  115.6 144.6 %copy-start.90 = (s32[128]{0:T(128)}, s32[128]{0:T(128)S(1)}, u32[]{:S(2)}) copy-start(s32[128]{0:T(128)S(1)} %get-tuple-element.163) | copy-start | bytes 1540
  115.6 145.0 %copy-start.88 = (s32[128]{0:T(128)}, s32[128]{0:T(128)S(1)}, u32[]{:S(2)}) copy-start(s32[128]{0:T(128)S(1)} %get-tuple-element.162) | copy-start | bytes 1540
  115.8 63.3 %copy-start.84 = (s32[128]{0:T(128)}, s32[128]{0:T(128)S(1)}, u32[]{:S(2)}) copy-start(s32[128]{0:T(128)S(1)} %get-tuple-element.166) | copy-start | bytes 1540
  115.8 63.9 %copy-start.86 = (s32[128]{0:T(128)}, s32[128]{0:T(128)S(1)}, u32[]{:S(2)}) copy-start(s32[128]{0:T(128)S(1)} %get-tuple-element.167) | copy-start | bytes 1540
  117.2 62.1 %copy-start.58 = (bf16[128,768]{1,0:T(8,128)(2,1)S(1)}, bf16[128,768]{1,0:T(8,128)(2,1)}, u32[]{:S(2)}) copy-start(bf16[128,768]{1,0:T(8,128)(2,1)} %multiply_convert_fusion.1) | copy-start | bytes 589828
  117.2 62.1 %copy-start.62 = (bf16[768,16]{1,0:T(8,128)(2,1)S(1)}, bf16[768,16]{1,0:T(8,128)(2,1)}, u32[]{:S(2)}) copy-start(bf16[768,16]{1,0:T(8,128)(2,1)} %convert_element_type.115) | copy-start | bytes 73732
  117.3 62.1 %copy-start.92 = (s32[128]{0:T(128)S(1)}, s32[128]{0:T(128)}, u32[]{:S(2)}) copy-start(s32[128]{0:T(128)} %get-tuple-element.228) | copy-start | bytes 1540
  117.3 62.1 %copy-start.94 = (s32[128]{0:T(128)S(1)}, s32[128]{0:T(128)}, u32[]{:S(2)}) copy-start(s32[128]{0:T(128)} %get-tuple-element.229) | copy-start | bytes 1540
  204.2 55.9 %copy-start.7 = (f32[128,768]{1,0:T(8,128)}, f32[128,768]{1,0:T(8,128)S(1)}, u32[]{:S(2)}) copy-start(f32[128,768]{1,0:T(8,128)S(1)} %get-tuple-element.66) | copy-start | bytes 1179652
  205.6 54.9 %copy-start.77 = (bf16[2,1,128,768]{3,2,1,0:T(8,128)(2,1)S(1)}, bf16[2,1,128,768]{3,2,1,0:T(8,128)(2,1)}, u32[]{:S(2)}) copy-start(bf16[2,1,128,768]{3,2,1,0:T(8,128)(2,1)} %param.20) | copy-start | bytes 1179652
  265.2 56.4 %copy-start.89 = (s32[128]{0:T(128)S(1)}, s32[128]{0:T(128)}, u32[]{:S(2)}) copy-start(s32[128]{0:T(128)} %copy-done.88) | copy-start | bytes 1540
  265.2 56.8 %copy-start.8 = (f32[128,768]{1,0:T(8,128)S(1)}, f32[128,768]{1,0:T(8,128)}, u32[]{:S(2)}) copy-start(f32[128,768]{1,0:T(8,128)} %copy-done.7) | copy-start | bytes 1179652
  265.2 56.8 %copy-start.65 = (bf16[768,16]{1,0:T(8,128)(2,1)S(1)}, bf16[768,16]{1,0:T(8,128)(2,1)}, u32[]{:S(2)}) copy-start(bf16[768,16]{1,0:T(8,128)(2,1)} %convert_element_type.124) | copy-start | bytes 73732
  265.2 56.8 %copy-start.81 = (f32[768]{0:T(1024)S(1)}, f32[768]{0:T(1024)}, u32[]{:S(2)}) copy-start(f32[768]{0:T(1024)} %mul.503) | copy-start | bytes 9220
  265.2 56.8 %copy-start.97 = (s32[128]{0:T(128)S(1)}, s32[128]{0:T(128)}, u32[]{:S(2)}) copy-start(s32[128]{0:T(128)} %get-tuple-element.160) | copy-start | bytes 1540
  265.2 56.8 %copy-start.99 = (s32[128]{0:T(128)S(1)}, s32[128]{0:T(128)}, u32[]{:S(2)}) copy-start(s32[128]{0:T(128)} %get-tuple-element.161) | copy-start | bytes 1540
  265.2 56.8 %copy-start.109 = (f32[128]{0:T(128)S(1)}, f32[128]{0:T(128)}, u32[]{:S(2)}) copy-start(f32[128]{0:T(128)} %copy-done.108) | copy-start | bytes 1540
  265.2 56.8 %copy-start.111 = (f32[128]{0:T(128)S(1)}, f32[128]{0:T(128)}, u32[]{:S(2)}) copy-start(f32[128]{0:T(128)} %copy-done.110) | copy-start | bytes 1540
  265.2 56.8 %copy-start.115 = (f32[128]{0:T(128)S(1)}, f32[128]{0:T(128)}, u32[]{:S(2)}) copy-start(f32[128]{0:T(128)} %copy-done.114) | copy-start | bytes 1540
  360.0 62.2 %copy-start.6 = (f32[128,768]{1,0:T(8,128)S(1)}, f32[128,768]{1,0:T(8,128)}, u32[]{:S(2)}) copy-start(f32[128,768]{1,0:T(8,128)} %copy-done.4) | copy-start | bytes 1179652
  360.0 62.2 %copy-start.63 = (bf16[768,16]{1,0:T(8,128)(2,1)S(1)}, bf16[768,16]{1,0:T(8,128)(2,1)}, u32[]{:S(2)}) copy-start(bf16[768,16]{1,0:T(8,128)(2,1)} %convert_element_type.115) | copy-start | bytes 73732
  360.1 62.2 %copy-start.79 = (f32[768]{0:T(1024)S(1)}, f32[768]{0:T(1024)}, u32[]{:S(2)}) copy-start(f32[768]{0:T(1024)} %copy-done.78) | copy-start | bytes 9220
  360.1 62.2 %copy-start.113 = (f32[128]{0:T(128)S(1)}, f32[128]{0:T(128)}, u32[]{:S(2)}) copy-start(f32[128]{0:T(128)} %copy-done.112) | copy-start | bytes 1540
  455.4 43.4 %copy-start.47 = (bf16[128,768]{1,0:T(8,128)(2,1)S(1)}, bf16[128,768]{1,0:T(8,128)(2,1)}, u32[]{:S(2)}) copy-start(bf16[128,768]{1,0:T(8,128)(2,1)} %copy-done.45) | copy-start | bytes 589828
  455.4 43.4 %copy-start.51 = (f32[128,768]{1,0:T(8,128)S(1)}, f32[128,768]{1,0:T(8,128)}, u32[]{:S(2)}) copy-start(f32[128,768]{1,0:T(8,128)} %copy-done.50) | copy-start | bytes 1179652
  455.4 43.4 %copy-start.66 = (f32[128,768]{1,0:T(8,128)S(1)}, f32[128,768]{1,0:T(8,128)}, u32[]{:S(2)}) copy-start(f32[128,768]{1,0:T(8,128)} %get-tuple-element.225) | copy-start | bytes 1179652
  455.4 43.4 %copy-start.101 = (f32[128]{0:T(128)S(1)}, f32[128]{0:T(128)}, u32[]{:S(2)}) copy-start(f32[128]{0:T(128)} %copy-done.100) | copy-start | bytes 1540
  455.4 43.4 %copy-start.103 = (f32[128]{0:T(128)S(1)}, f32[128]{0:T(128)}, u32[]{:S(2)}) copy-start(f32[128]{0:T(128)} %copy-done.102) | copy-start | bytes 1540
  499.8 6.3 %collective-permute-start.1 = (bf16[128,768]{1,0:T(8,128)(2,1)}, bf16[128,768]{1,0:T(8,128)(2,1)}, u32[]{:S(2)}, u32[]{:S(2)}) collective-permute-start(bf16[128,768]{1,0:T(8,128)(2,1)} %get-tuple-element.182), channel_id=1, source_target_pairs={{0,64},{64,0},{1,65},{65,1},{2,66},{66,2},{3,67},{67,3},{4,68},{68... | collective-permute-start | bytes 589832 | tf_op jit(solution)/shard_map/ppermute | solution.py:1044
  500.9 7.2 %collective-permute-start.2 = (f32[128,768]{1,0:T(8,128)}, f32[128,768]{1,0:T(8,128)}, u32[]{:S(2)}, u32[]{:S(2)}) collective-permute-start(f32[128,768]{1,0:T(8,128)} %get-tuple-element.191), channel_id=1, source_target_pairs={{0,64},{64,0},{1,65},{65,1},{2,66},{66,2},{3,67},{67,3},{4,68},{68... | collective-permute-start | bytes 1179656 | tf_op jit(solution)/shard_map/ppermute | solution.py:1044
  (95 other events, 704.9 us)

commit v4 on v3

--- a/solution.py
+++ b/solution.py
@@ -201,7 +201,7 @@
         self.each(lambda c: c.wait_send())
 
 
-def meet_all():
+def meet_all(partner=None):
     barrier = pltpu.get_barrier_semaphore()
     me, count = lax.axis_index("exp"), lax.axis_size("exp")
 
@@ -215,17 +215,18 @@
     right, left = lax.rem(ctx + 1, 4), lax.rem(ctx + 3, 4)
     for neighbour in (left, right):
         pl.semaphore_signal(barrier, inc=1, device_id={"ctx": neighbour}, device_id_type=MESH)
-    pl.semaphore_wait(barrier, count + 1)
+    if partner is not None:
+        pl.semaphore_signal(barrier, inc=1, device_id={"section": partner}, device_id_type=MESH)
+    pl.semaphore_wait(barrier, count + (1 if partner is None else 2))
     return ctx, right, left
 
 
 def run_experts(
-    rows, out_ref, sel_ref, all_ref, ret_ref, block, beside_one, beside_two, scratch
+    ids, rows, out_ref, sel_ref, all_ref, ret_ref, block, beside, scratch
 ):
     inbox, part, res = scratch[:3]
     bufs = scratch[3:9]
     s_in, r_in, s_out, r_out, s_ag, r_ag, s_rs, r_rs = scratch[9:]
-    ids = meet_all()
     me, right, left = ids
     far = lax.rem(me + 2, 4)
     flat = inbox.shape[0] * inbox.shape[1]
@@ -233,6 +234,7 @@
 
     arriving = Exchange(out_ref, inbox, s_in, r_in)
     arriving.start()
+    beside[0]()
     arriving.wait_recv()
     all_ref[me] = mm(sel_ref[...], inbox[...].reshape(flat, width)).astype(BF16)
     gather = RingGather(all_ref, rows, ids, s_ag, r_ag)
@@ -249,13 +251,14 @@
     gather.wait_far()
     block(far, part)
     scatter.send_far()
-    beside_one()
+    beside[1]()
     scatter.send_sums()
-    beside_two()
+    beside[2]()
     padded = mm_tn(sel_ref[...], scatter.total().astype(BF16)).astype(BF16)
     res[...] = padded.reshape(res.shape)
     leaving = Exchange(res, ret_ref, s_out, r_out)
     leaving.start()
+    beside[3]()
     leaving.wait_recv()
     gather.wait_send()
     scatter.wait_send()
@@ -275,44 +278,30 @@
     ]
 
 
-def experts_kernel(rows, out_ref, sel_ref, w_in, w_back, ret_ref, all_ref, pre_ref, *scratch):
-    def block(j, part):
-        pre = mm(all_ref[j], w_in[...])
-        pre_ref[j] = pre
-        hidden = gelu_parts(pre)[0].astype(BF16)
-        part[j] = mm_nt(hidden, w_back[...]).astype(BF16)
-
-    nothing = lambda: None
-    run_experts(rows, out_ref, sel_ref, all_ref, ret_ref, block, nothing, nothing, scratch)
-
-
-def experts_back_kernel(
-    rows, out_ref, sel_ref, w_in, w_back, ent_ref, pre_ref, ret_ref, d_in, d_back, e_in, e_back,
-    all_ref, hid_ref, dpre_ref, *scratch
-):
-    width = w_in.shape[0]
-
-    def block(j, part):
-        hidden, slope = gelu_parts(pre_ref[j])
-        hid_ref[j] = hidden.astype(BF16)
-        dpre = (mm(all_ref[j], w_back[...]) * slope).astype(BF16)
-        dpre_ref[j] = dpre
-        part[j] = mm_nt(dpre, w_in[...]).astype(BF16)
-
-    def flat(ref):
-        return ref[...].reshape(4 * rows, ref.shape[2])
-
-    def beside_one():
-        grad = mm_tn(flat(all_ref), flat(hid_ref))
-        d_back[...] = grad
-        e_back[...] = grad.astype(BF16)
-
-    def beside_two():
-        grad = mm_tn(flat(ent_ref), flat(dpre_ref))
-        d_in[...] = grad
-        e_in[...] = grad.astype(BF16)
-
-    run_experts(rows, out_ref, sel_ref, all_ref, ret_ref, block, beside_one, beside_two, scratch)
+def route_tables(routes_ref, experts):
+    rows = routes_ref.shape[0]
+    routes = routes_ref[...]
+    lanes = lax.broadcasted_iota(jnp.int32, (rows, experts), 1)
+    hot = [jnp.where(routes[:, c : c + 1] == lanes, 1.0, 0.0) for c in range(TOP)]
+    row = lax.broadcasted_iota(jnp.int32, (rows, rows), 0)
+    col = lax.broadcasted_iota(jnp.int32, (rows, rows), 1)
+    before = jnp.where(row > col, 1.0, 0.0).astype(BF16)
+    earlier = mm(before, (hot[0] + hot[1]).astype(BF16))
+    wide = lax.broadcasted_iota(jnp.int32, (rows, experts * PAD), 1).astype(F32)
+    slots = []
+    for c in range(TOP):
+        slot = jnp.sum(hot[c] * earlier, -1, keepdims=True)
+        target = routes[:, c : c + 1].astype(F32) * PAD + slot
+        slots.append(jnp.where(wide == target, 1.0, 0.0).astype(BF16))
+    return hot, slots
+
+
+def gates_of(logits, hot):
+    chosen = [jnp.sum(h * logits, -1, keepdims=True) for h in hot]
+    peak = jnp.maximum(chosen[0], chosen[1])
+    raised = [jnp.exp(c - peak) for c in chosen]
+    total = 1.0 / (raised[0] + raised[1])
+    return [r * total for r in raised]
 
 
 def selection(experts, capacity):
@@ -420,30 +409,17 @@
     return ref[:, at : at + HEAD_DIM]
 
 
-def meet_ring(partner):
-    barrier = pltpu.get_barrier_semaphore()
-    ctx = lax.axis_index("ctx")
-    right, left = lax.rem(ctx + 1, 4), lax.rem(ctx + 3, 4)
-    for neighbour in (left, right):
-        pl.semaphore_signal(barrier, inc=1, device_id={"ctx": neighbour}, device_id_type=MESH)
-    if partner is not None:
-        pl.semaphore_signal(barrier, inc=1, device_id={"section": partner}, device_id_type=MESH)
-    pl.semaphore_wait(barrier, 2 if partner is None else 3)
-    return ctx, right, left
-
-
-def attend_kernel(
-    heads, x_ref, gain_ref, w_qkv, w_out, table_ref, kind_ref,
-    middle_ref, all_ref, proj_ref, att_ref,
-    tiles_ref, s_ref, p_ref, part, *scratch
+def attend(
+    ids, x, gain_ref, w_qkv, w_out, table_ref, kind_ref, all_ref, proj_ref, att_ref,
+    tiles_ref, s_ref, p_ref, part, scratch
 ):
     bufs, (s_ag, r_ag, s_rs, r_rs) = scratch[:6], scratch[6:]
-    ids = meet_ring(None)
     me, right, left = ids
     far = lax.rem(me + 2, 4)
-    rows, width = x_ref.shape
+    rows, width = x.shape
     seq = 4 * rows
-    all_ref[me] = norm(x_ref[...], gain_ref[...])
+    heads = w_out.shape[0] // HEAD_DIM
+    all_ref[me] = norm(x, gain_ref[...])
     gather = RingGather(all_ref, rows, ids, s_ag, r_ag)
     gather.start()
     make_tiles(table_ref, tiles_ref, heads)
@@ -472,70 +448,27 @@
     scatter.send_left()
     part[me] = mm(att_ref[me], w_out[...]).astype(BF16)
     scatter.send_sums()
-    middle_ref[...] = x_ref[...] + scatter.total()
+    total = scatter.total()
     gather.wait_send()
     scatter.wait_send()
-
-
-def attend(x, gain, w_qkv, w_out, table, kind):
-    rows, width = x.shape
-    seq = 4 * rows
-    part = w_out.shape[0]
-    heads = part // HEAD_DIM
-    vm = pl.BlockSpec(memory_space=pltpu.VMEM)
-    return pl.pallas_call(
-        functools.partial(attend_kernel, heads),
-        out_shape=(
-            jax.ShapeDtypeStruct(x.shape, F32),
-            jax.ShapeDtypeStruct((4, rows, width), BF16),
-            jax.ShapeDtypeStruct((seq, 3 * part), BF16),
-            jax.ShapeDtypeStruct((4, rows, part), BF16),
-        ),
-        in_specs=[vm] * 6,
-        out_specs=(vm,) * 4,
-        scratch_shapes=[
-            pltpu.VMEM((heads, KINDS - 1, SPAN, seq), F32),
-            pltpu.VMEM((seq, seq), F32),
-            pltpu.VMEM((seq, seq), BF16),
-            pltpu.VMEM((4, rows, width), BF16),
-            *scatter_buffers(rows, width),
-            *[pltpu.SemaphoreType.DMA((6,))] * 4,
-        ],
-        compiler_params=pltpu.CompilerParams(
-            collective_id=0, has_side_effects=True, vmem_limit_bytes=48 << 20
-        ),
-    )(x, gain, w_qkv, w_out, table, kind)
-
-
-def attend_back_kernel(
-    heads, dmid_ref, all_ref, proj_ref, att_ref, w_qkv, w_out, table_ref, kind_ref,
-    e_in, e_back, perm_ref, perm_out_ref,
-    dnormed_ref, pq_ref, po_ref, dtable_ref, got_in, got_back, got_pq, got_po,
-    tiles_ref, dtiles_ref, s_ref, dp_ref, p_ref, ds_ref, da_ref, dproj_ref, db_ref, part, *scratch
+    return total
+
+
+def attend_back(
+    ids, dmiddle, all_ref, proj_ref, att_ref, w_qkv, w_out, table_ref, kind_ref,
+    perm_ref, perm_out_ref, pq_ref, po_ref, dtable_ref, ready,
+    tiles_ref, dtiles_ref, s_ref, dp_ref, p_ref, ds_ref, da_ref, dproj_ref, db_ref, part, scratch
 ):
-    bufs, (s_ag, r_ag, s_rs, r_rs, s_x, r_x) = scratch[:6], scratch[6:]
-    partner = 1 - lax.axis_index("section")
-    ids = meet_ring(partner)
+    bufs, (s_ag, r_ag, s_rs, r_rs) = scratch[:6], scratch[6:]
     me, right, left = ids
     far = lax.rem(me + 2, 4)
-    rows, width = dmid_ref.shape
+    rows, width = dmiddle.shape
     seq = 4 * rows
+    heads = w_out.shape[0] // HEAD_DIM
     scale = HEAD_DIM**-0.5
-
-    def across(k, src, dst):
-        return remote(src, dst, s_x, r_x, k, "section", partner)
-
-    crossing = [
-        across(0, e_in, got_in),
-        across(1, e_back, got_back),
-        across(2, pq_ref, got_pq),
-        across(3, po_ref, got_po),
-    ]
-    db_ref[me] = dmid_ref[...].astype(BF16)
+    db_ref[me] = dmiddle.astype(BF16)
     gather = RingGather(db_ref, rows, ids, s_ag, r_ag)
     gather.start()
-    crossing[0].start()
-    crossing[1].start()
     make_tiles(table_ref, tiles_ref, heads)
     gather.forward()
     gather.wait_left()
@@ -593,40 +526,222 @@
     dproj = dproj_ref[...].reshape(seq, dproj_ref.shape[2])
     d_qkv = mm_tn(all_ref[...].reshape(seq, width), dproj).astype(BF16)
     pq_ref[...] = mm(perm_ref[...], d_qkv).astype(BF16)
-    crossing[2].start()
+    ready(0)
     scatter.send_sums()
     d_out = mm_tn(att_ref[...].reshape(seq, att_ref.shape[2]), db_ref[...].reshape(seq, width))
     po_ref[...] = mm(perm_out_ref[...], d_out.astype(BF16)).astype(BF16)
-    crossing[3].start()
-    dnormed_ref[...] = scatter.total()
+    ready(1)
+    total = scatter.total()
     gather.wait_send()
     scatter.wait_send()
+    return total
+
+
+def layer_kernel(
+    x_ref, gain_one, gain_two, w_qkv, w_out, table_ref, kind_ref, router_ref, routes_ref,
+    sel_ref, w_in, w_back,
+    h_ref, all_ref, proj_ref, att_ref, middle_ref, mixed_ref, logits_ref, picked_ref,
+    ent_ref, pre_ref, *scratch
+):
+    tiles_ref, s_ref, p_ref, part, out_ref, ret_ref = scratch[:6]
+    ids = meet_all()
+    rows, width = x_ref.shape
+    x = x_ref[...].astype(F32)
+    branch = attend(
+        ids, x, gain_one, w_qkv, w_out, table_ref, kind_ref, all_ref, proj_ref, att_ref,
+        tiles_ref, s_ref, p_ref, part, scratch[6:16]
+    )
+    middle = x + branch
+    middle_ref[...] = middle
+    mixed = norm(middle, gain_two[...])
+    mixed_ref[...] = mixed
+    hot, slots = route_tables(routes_ref, out_ref.shape[0])
+    out_ref[...] = mm_tn(slots[0] + slots[1], mixed).astype(BF16).reshape(out_ref.shape)
+
+    def block(j, part):
+        pre = mm(ent_ref[j], w_in[...])
+        pre_ref[j] = pre
+        hidden = gelu_parts(pre)[0].astype(BF16)
+        part[j] = mm_nt(hidden, w_back[...]).astype(BF16)
+
+    def find_logits():
+        logits_ref[...] = mm(mixed_ref[...], router_ref[...])
+
+    nothing = lambda: None
+    run_experts(
+        ids, sel_ref.shape[0], out_ref, sel_ref, ent_ref, ret_ref, block,
+        (find_logits, nothing, nothing, nothing), scratch[16:]
+    )
+    gates = gates_of(logits_ref[...], hot)
+    returned = ret_ref[...].reshape(slots[0].shape[1], width)
+    y = middle_ref[...]
+    for c in range(TOP):
+        picked = mm(slots[c], returned)
+        picked_ref[c] = picked.astype(BF16)
+        y = y + gates[c] * picked
+    h_ref[...] = y.astype(BF16)
+
+
+def layer_forward(x, weights, kind, routes, sel):
+    w_qkv, w_out, gain_one, gain_two, table, router, w_in, w_back = weights
+    rows, width = x.shape
+    seq, part, experts = 4 * rows, w_out.shape[0], router.shape[1]
+    heads, slots = part // HEAD_DIM, sel.shape[0]
+    vm = pl.BlockSpec(memory_space=pltpu.VMEM)
+    shape = jax.ShapeDtypeStruct
+    return pl.pallas_call(
+        layer_kernel,
+        out_shape=(
+            shape(x.shape, BF16),
+            shape((4, rows, width), BF16),
+            shape((seq, 3 * part), BF16),
+            shape((4, rows, part), BF16),
+            shape(x.shape, F32),
+            shape(x.shape, BF16),
+            shape((rows, experts), F32),
+            shape((TOP, rows, width), BF16),
+            shape((4, slots, width), BF16),
+            shape((4, slots, w_in.shape[1]), F32),
+        ),
+        in_specs=[vm] * 12,
+        out_specs=(vm,) * 10,
+        scratch_shapes=[
+            pltpu.VMEM((heads, KINDS - 1, SPAN, seq), F32),
+            pltpu.VMEM((seq, seq), F32),
+            pltpu.VMEM((seq, seq), BF16),
+            pltpu.VMEM((4, rows, width), BF16),
+            pltpu.VMEM((experts, PAD, width), BF16),
+            pltpu.VMEM((experts, PAD, width), BF16),
+            *scatter_buffers(rows, width),
+            *[pltpu.SemaphoreType.DMA((6,))] * 4,
+            *expert_scratch(experts, slots, width),
+        ],
+        compiler_params=pltpu.CompilerParams(
+            collective_id=0, has_side_effects=True, vmem_limit_bytes=56 << 20
+        ),
+    )(x, gain_one, gain_two, w_qkv, w_out, table, kind, router, routes, sel, w_in, w_back)
+
+
+def layer_back_kernel(
+    g_ref, x_ref, gain_one, gain_two, w_qkv, w_out, table_ref, kind_ref, router_ref, routes_ref,
+    sel_ref, w_in, w_back, perm_ref, perm_out_ref,
+    all_ref, proj_ref, att_ref, middle_ref, mixed_ref, logits_ref, picked_ref, ent_ref, pre_ref,
+    dx_ref, dxb_ref, dgain_one, dgain_two, drouter_ref, pq_ref, po_ref, dtable_ref,
+    d_in, d_back, got_in, got_back, got_pq, got_po, *scratch
+):
+    (
+        tiles_ref, dtiles_ref, s_ref, dp_ref, p_ref, ds_ref, da_ref, dproj_ref, db_ref, part,
+        out_ref, ret_ref, darr_ref, hid_ref, dpre_ref, e_in, e_back, s_x, r_x
+    ) = scratch[:19]
+    partner = 1 - lax.axis_index("section")
+    ids = meet_all(partner)
+    rows, width = x_ref.shape
+
+    def across(k, src, dst):
+        return remote(src, dst, s_x, r_x, k, "section", partner)
+
+    crossing = [
+        across(0, e_back, got_back),
+        across(1, e_in, got_in),
+        across(2, pq_ref, got_pq),
+        across(3, po_ref, got_po),
+    ]
+    g = g_ref[...].astype(F32)
+    hot, slots = route_tables(routes_ref, out_ref.shape[0])
+    gates = gates_of(logits_ref[...], hot)
+    dreturned = mm_tn(slots[0], (gates[0] * g).astype(BF16)) + mm_tn(
+        slots[1], (gates[1] * g).astype(BF16)
+    )
+    out_ref[...] = dreturned.astype(BF16).reshape(out_ref.shape)
+
+    def logits_back():
+        g = g_ref[...].astype(F32)
+        dgates = [
+            jnp.sum(g * picked_ref[c].astype(F32), -1, keepdims=True) for c in range(TOP)
+        ]
+        mean = gates[0] * dgates[0] + gates[1] * dgates[1]
+        dchosen = [a * (b - mean) for a, b in zip(gates, dgates)]
+        dlogits = (hot[0] * dchosen[0] + hot[1] * dchosen[1]).astype(BF16)
+        drouter_ref[...] = mm_tn(mixed_ref[...], dlogits)
+        dx_ref[...] = mm_nt(dlogits, router_ref[...])
+
+    def block(j, part):
+        hidden, slope = gelu_parts(pre_ref[j])
+        hid_ref[j] = hidden.astype(BF16)
+        dpre = (mm(darr_ref[j], w_back[...]) * slope).astype(BF16)
+        dpre_ref[j] = dpre
+        part[j] = mm_nt(dpre, w_in[...]).astype(BF16)
+
+    def flat(ref):
+        return ref[...].reshape(ref.shape[0] * ref.shape[1], ref.shape[2])
+
+    def back_grad():
+        grad = mm_tn(flat(darr_ref), flat(hid_ref))
+        d_back[...] = grad
+        e_back[...] = grad.astype(BF16)
+        crossing[0].start()
+
+    def in_grad():
+        grad = mm_tn(flat(ent_ref), flat(dpre_ref))
+        d_in[...] = grad
+        e_in[...] = grad.astype(BF16)
+        crossing[1].start()
+
+    run_experts(
+        ids, sel_ref.shape[0], out_ref, sel_ref, darr_ref, ret_ref, block,
+        (logits_back, back_grad, lambda: None, in_grad), scratch[29:]
+    )
+    dleft = ret_ref[...].reshape(slots[0].shape[1], width)
+    dmixed = mm(slots[0] + slots[1], dleft) + dx_ref[...]
+    dnorm, dgain = norm_back(middle_ref[...], gain_two[...], dmixed)
+    dgain_two[...] = dgain
+    dmiddle = g_ref[...].astype(F32) + dnorm
+    dx_ref[...] = dmiddle
+    dnormed = attend_back(
+        ids, dmiddle, all_ref, proj_ref, att_ref, w_qkv, w_out, table_ref, kind_ref,
+        perm_ref, perm_out_ref, pq_ref, po_ref, dtable_ref, lambda k: crossing[2 + k].start(),
+        tiles_ref, dtiles_ref, s_ref, dp_ref, p_ref, ds_ref, da_ref, dproj_ref, db_ref, part,
+        scratch[19:29]
+    )
+    dnorm, dgain = norm_back(x_ref[...].astype(F32), gain_one[...], dnormed)
+    dgain_one[...] = dgain
+    dx = dx_ref[...] + dnorm
+    dx_ref[...] = dx
+    dxb_ref[...] = dx.astype(BF16)
     for c in crossing:
         c.wait()
 
 
-def attend_back(dmiddle, normed, proj, att, w_qkv, w_out, table, kind, e_in, e_back, perm, perm_out):
-    rows, width = dmiddle.shape
-    seq = 4 * rows
-    part = w_out.shape[0]
-    heads = part // HEAD_DIM
+def layer_backward(g, keep, weights, kind, routes, sel, perm, perm_out):
+    x, *saved = keep
+    w_qkv, w_out, gain_one, gain_two, table, router, w_in, w_back = weights
+    rows, width = x.shape
+    seq, part, experts = 4 * rows, w_out.shape[0], router.shape[1]
+    heads, slots, hid = part // HEAD_DIM, sel.shape[0], w_in.shape[1]
     vm = pl.BlockSpec(memory_space=pltpu.VMEM)
-    pq = jax.ShapeDtypeStruct((perm.shape[0], 3 * part), BF16)
-    po = jax.ShapeDtypeStruct((perm_out.shape[0], width), BF16)
+    shape = jax.ShapeDtypeStruct
+    pq = shape((perm.shape[0], 3 * part), BF16)
+    po = shape((perm_out.shape[0], width), BF16)
     return pl.pallas_call(
-        functools.partial(attend_back_kernel, heads),
+        layer_back_kernel,
         out_shape=(
-            jax.ShapeDtypeStruct((rows, width), F32),
+            shape(x.shape, F32),
+            shape(x.shape, BF16),
+            shape((1, width), F32),
+            shape((1, width), F32),
+            shape((width, experts), F32),
             pq,
             po,
-            jax.ShapeDtypeStruct((heads, BUCKETS, 2 * SPAN), F32),
-            jax.ShapeDtypeStruct(e_in.shape, BF16),
-            jax.ShapeDtypeStruct(e_back.shape, BF16),
+            shape((heads, BUCKETS, 2 * SPAN), F32),
+            shape(w_in.shape, F32),
+            shape(w_back.shape, F32),
+            shape(w_in.shape, BF16),
+            shape(w_back.shape, BF16),
             pq,
             po,
         ),
-        in_specs=[vm] * 12,
-        out_specs=(vm,) * 8,
+        in_specs=[vm] * 24,
+        out_specs=(vm,) * 14,
         scratch_shapes=[
             pltpu.VMEM((heads, KINDS - 1, SPAN, seq), F32),
             pltpu.VMEM((KINDS, SPAN, seq), F32),
@@ -638,14 +753,25 @@
             pltpu.VMEM((4, rows, 3 * part), BF16),
             pltpu.VMEM((4, rows, width), BF16),
             pltpu.VMEM((4, rows, width), BF16),
+            pltpu.VMEM((experts, PAD, width), BF16),
+            pltpu.VMEM((experts, PAD, width), BF16),
+            pltpu.VMEM((4, slots, width), BF16),
+            pltpu.VMEM((4, slots, hid), BF16),
+            pltpu.VMEM((4, slots, hid), BF16),
+            pltpu.VMEM(w_in.shape, BF16),
+            pltpu.VMEM(w_back.shape, BF16),
+            *[pltpu.SemaphoreType.DMA((4,))] * 2,
             *scatter_buffers(rows, width),
             *[pltpu.SemaphoreType.DMA((6,))] * 4,
-            *[pltpu.SemaphoreType.DMA((4,))] * 2,
+            *expert_scratch(experts, slots, width),
         ],
         compiler_params=pltpu.CompilerParams(
-            collective_id=1, has_side_effects=True, vmem_limit_bytes=52 << 20
-        ),
-    )(dmiddle, normed, proj, att, w_qkv, w_out, table, kind, e_in, e_back, perm, perm_out)
+            collective_id=1, has_side_effects=True, vmem_limit_bytes=60 << 20
+        ),
+    )(
+        g, x, gain_one, gain_two, w_qkv, w_out, table, kind, router, routes, sel, w_in, w_back,
+        perm, perm_out, *saved
+    )
 
 
 def meet_everyone():
@@ -893,7 +1019,7 @@
     r = norm_scale(v)
     dug = du * gain
     dv = r * dug - v * (r * r * r) * jnp.mean(dug * v, -1, keepdims=True)
-    return dv, jnp.sum(du * v * r, 0)
+    return dv, jnp.sum(du * v * r, 0, keepdims=True)
 
 
 def gelu_parts(v):
@@ -901,20 +1027,6 @@
     value = 0.5 * v * (1.0 + t)
     slope = 0.5 * (1.0 + t) + 0.5 * v * (1.0 - t * t) * GELU_C * (1.0 + 3 * 0.044715 * v * v)
     return value, slope
-
-
-def slot_tables(routes, experts):
-    rows = routes.shape[0]
-    flat = routes.reshape(rows * TOP)
-    hot = flat[:, None] == jnp.arange(experts, dtype=jnp.int32)
-    before = np.tril(np.ones((rows * TOP, rows * TOP), np.float32), -1)
-    earlier = mm(jnp.asarray(before, BF16), hot.astype(BF16))
-    slot = jnp.sum(jnp.where(hot, earlier, 0.0), -1).astype(jnp.int32)
-    target = (flat * PAD + slot).reshape(rows, TOP)
-    slots = jnp.arange(experts * PAD, dtype=jnp.int32)
-    slot_hot = [(target[:, c : c + 1] == slots).astype(BF16) for c in range(TOP)]
-    route_hot = [(routes[:, c : c + 1] == jnp.arange(experts)).astype(F32) for c in range(TOP)]
-    return route_hot, slot_hot
 
 
 def on_device(
@@ -938,7 +1050,6 @@
     heads = HEADS // n_ctx
     part = heads * HEAD_DIM
     capacity = rows * TOP // n_exp + max(1, rows * TOP // (16 * n_exp))
-    slots = n_exp * PAD
     sel = selection(n_exp, capacity)
     section = lax.axis_index("section")
     ctx = lax.axis_index("ctx")
@@ -982,50 +1093,17 @@
     given = jnp.where(first, own_routes[1], own_routes[0])
     taken = lax.ppermute(given, "section", [(0, 1), (1, 0)])
     layer_routes = (jnp.where(first, kept, taken), jnp.where(first, taken, kept))
-    tables = [slot_tables(r, n_exp) for r in layer_routes]
-
     def forward(x, layer):
-        w_qkv, w_out, gain_one, gain_two, table, router, w_in, w_back = weights[layer]
-        route_hot, slot_hot = tables[layer]
-        middle, normed, proj, attended = attend(x, gain_one, w_qkv, w_out, table, kind)
-        mixed = norm(middle, gain_two)
-        logits = mm(mixed, router)
-        chosen = [jnp.sum(h * logits, -1, keepdims=True) for h in route_hot]
-        peak = jnp.maximum(chosen[0], chosen[1])
-        raised = [jnp.exp(c - peak) for c in chosen]
-        gates = [r / (raised[0] + raised[1]) for r in raised]
-        placing = slot_hot[0] + slot_hot[1]
-        outgoing = mm_tn(placing, mixed).astype(BF16).reshape(n_exp, PAD, width)
-        returned, entering, pre = experts_forward(outgoing, sel, w_in, w_back)
-        returned = returned.reshape(slots, width)
-        picked = [mm(h, returned) for h in slot_hot]
-        y = middle + gates[0] * picked[0] + gates[1] * picked[1]
-        keep = (x, normed, proj, attended, middle, mixed, gates, picked, entering, pre)
-        return y, keep
+        h, *saved = layer_forward(x, weights[layer], kind, layer_routes[layer], sel)
+        return h, (x, *saved)
 
     def backward(g, keep, layer):
-        x, normed, proj, attended, middle, mixed, gates, picked, entering, pre = keep
-        w_qkv, w_out, gain_one, gain_two, table, router, w_in, w_back = weights[layer]
-        route_hot, slot_hot = tables[layer]
-        dreturned = mm_tn(slot_hot[0], (gates[0] * g).astype(BF16)) + mm_tn(
-            slot_hot[1], (gates[1] * g).astype(BF16)
+        (
+            dx, dxb, d_gain_one, d_gain_two, d_router, pq, po, d_table,
+            d_in, d_back, g_in, g_back, gq, go
+        ) = layer_backward(
+            g, keep, weights[layer], kind, layer_routes[layer], sel, perm, perm_out
         )
-        dreturned = dreturned.astype(BF16).reshape(n_exp, PAD, width)
-        dleft, d_in, d_back, e_in, e_back = experts_backward(dreturned, sel, w_in, w_back, entering, pre)
-        dleft = dleft.reshape(slots, width)
-        dgates = [jnp.sum(g * p, -1, keepdims=True) for p in picked]
-        mean = gates[0] * dgates[0] + gates[1] * dgates[1]
-        dchosen = [a * (b - mean) for a, b in zip(gates, dgates)]
-        dlogits = route_hot[0] * dchosen[0] + route_hot[1] * dchosen[1]
-        dlogits = dlogits.astype(BF16)
-        d_router = mm_tn(mixed, dlogits)
-        dmixed = mm(slot_hot[0] + slot_hot[1], dleft) + mm_nt(dlogits, router)
-        dnorm, d_gain_two = norm_back(middle, gain_two, dmixed)
-        dmiddle = g + dnorm
-        dnormed, pq, po, d_table, g_in, g_back, gq, go = attend_back(
-            dmiddle, normed, proj, attended, w_qkv, w_out, table, kind, e_in, e_back, perm, perm_out
-        )
-        dnorm, d_gain_one = norm_back(x, gain_one, dnormed)
         d_table = jnp.repeat(jnp.sum(d_table, -1).T, 2, axis=0)
         owner = jnp.arange(n_ctx * n_exp)[:, None]
         d_table = jnp.where(owner % 2 == ctx // 2, d_table, 0.0)
@@ -1038,20 +1116,17 @@
             1,
         )
         d_small = jnp.pad(d_small, ((0, 0), (0, 256 - n_small)))
-        return dmiddle + dnorm, (pq, gq, po, go, d_small, d_in, g_in, d_back, g_back)
+        return dx, dxb, (pq, gq, po, go, d_small, d_in, g_in, d_back, g_back)
 
     def swap(x):
         return lax.ppermute(x, "section", [(0, 1), (1, 0)])
 
-    x = jnp.where(first, inputs[0, 0], inputs[1, 0]).astype(F32)
-    cot = jnp.where(first, cotangent[0, 0], cotangent[1, 0]).astype(F32)
-    y0, keep0 = forward(x, 0)
-    h = y0.astype(BF16)
-    y1, keep1 = forward(h.astype(F32), 1)
-    top = y1.astype(BF16)
-    dh, grads1 = backward(cot, keep1, 1)
-    dh = dh.astype(BF16)
-    dx, grads0 = backward(dh.astype(F32), keep0, 0)
+    x = jnp.where(first, inputs[0, 0], inputs[1, 0])
+    cot = jnp.where(first, cotangent[0, 0], cotangent[1, 0])
+    h, keep0 = forward(x, 0)
+    top, keep1 = forward(h, 1)
+    _, dh, grads1 = backward(cot, keep1, 1)
+    dx, _, grads0 = backward(dh, keep0, 0)
     pq, gq, po, go, d_small, d_in, g_in, d_back, g_back = zip(grads0, grads1)
     pieces, out_grad, d_in, d_back = sum_at_owners(
         pq, gq, po, go, jnp.stack(d_small), place, d_in, g_in, d_back, g_back, n_exp

time: 524 us -> 480 us (0.916)
  local copies, waits for them, and re-layouts: 60.1 us -> 33.7 us
  matrix products: 14.5 us -> 0 us
  other arithmetic: 19.1 us -> 8.34 us
  Pallas kernels: 418 us -> 427 us
    dot_general x20 -> x0, matrix products: 14.5 us -> none  [dot(): return lax.dot_general(a, b, (dims, ((), ())), preferred_element_type=F32)]
    unnamed x253 -> x47, local copies, waits for them, and re-layouts: 20.5 us -> 10.2 us
    pallas_call x8 -> x4, Pallas kernels: 335 us -> 345 us  [the longest x2 179 us: layer_backward(): pl.pallas_call(layer_back_kernel, out_shape=(shape(x.shape, F32), shape(x...]
  transfers between devices with their start and end apart: 3 -> 3, of which waited for: 0 -> 1; matrix products, arithmetic and copies ran while one was open for 7% -> 5% of each run, Pallas kernels for 12% -> 8%
where the time goes in v4:
time: 480 us; the launch traced here: 471 us
  Pallas kernels  427 us (89%)
  local copies, waits for them, and re-layouts  33.7 us (7%)
  other arithmetic  8.34 us (2%)
    pallas_call x2, Pallas kernels, layer_backward(): pl.pallas_call(layer_back_kernel, out_shape=(shape(x.shape, F32), shape(x...  179 us
    pallas_call x2, Pallas kernels, layer_forward(): pl.pallas_call(layer_kernel, out_shape=(shape(x.shape, BF16), shape((4, r...  166 us
    pallas_call x1, Pallas kernels, sum_at_owners(): pl.pallas_call(owners_kernel, out_shape=(jax.ShapeDtypeStruct(quarter, F3...  42.2 us
    pallas_call x1, Pallas kernels, gather_weights(): pl.pallas_call(weights_kernel, out_shape=(jax.ShapeDtypeStruct((2, width,...  39.5 us
    unnamed x47, local copies, waits for them, and re-layouts  10.2 us
  transfers between devices with their start and end apart: 3, of which 1 were waited for; matrix products, arithmetic and copies ran while one was open for 5% of the time, Pallas kernels for 8%

profile of v4, /device:TPU:2, one launch (start us, length us, event | category | flops | bytes accessed | tf_op | source)
XLA Modules:
  0.0 471.4 jit_solution(55578833144037293)
XLA Ops:
  0.7 0.8 fusion.14
  1.8 1.0 reshape_squeeze.6
  3.0 0.8 reshape_squeeze.7
  3.8 0.8 fusion.10
  4.6 0.7 pad.21.outp_ref
  5.3 1.4 copy-done
  6.7 0.9 copy-done.1
  7.6 1.3 copy-done.3
  8.9 0.9 copy-done.8
  9.8 39.5 %shard_map.240 = (bf16[2,768,576]{2,1,0:T(8,128)(2,1)}, bf16[2,192,768]{2,1,0:T(8,128)(2,1)S(1)}, f32[2,64,576]{2,1,0:T(8,128)S(1)}, bf16[2,768,768]{2,1,0:T(8,128)(2,1)}, bf16[2,768,768]{2,1,0:T(8,128)(2,1)}) custom-call(bf16[4,16,576]{2,1,0:T(8,128)(2,1)S(1)} %fusion.2.cols_ref, bf16[16,768]{1,0:T(8,128)(2,1)S(1)} %pad.21.outp_ref, ...), custom_call_target="tpu_custom_call" | custom-call | tf_op jit(solution)/shard_map/pallas_call | solution.py:883
  49.8 0.7 select_bitcast_fusion.1.x_ref
  50.5 3.0 slice_bitcast_fusion.4
  53.5 0.8 slice_bitcast_fusion.6
  54.4 0.7 select_bitcast_fusion.g_ref
  55.1 4.6 slice_bitcast_fusion
  61.2 0.7 reshape.231.gain_two
  61.9 0.8 convert_element_type.18.router_ref
  64.9 0.9 convert_element_type.19.router_ref
  66.4 86.5 %shard_map.241 = (bf16[128,768]{1,0:T(8,128)(2,1)}, bf16[4,128,768]{2,1,0:T(8,128)(2,1)}, bf16[512,576]{1,0:T(8,128)(2,1)}, bf16[4,128,192]{2,1,0:T(8,128)(2,1)}...) custom-call(bf16[128,768]{1,0:T(8,128)(2,1)} %select_bitcast_fusion., ...), custom_call_target="tpu_custom_call" | custom-call | tf_op jit(solution)/shard_map/pallas_call | solution.py:592
  153.0 79.6 %shard_map.242 = (bf16[128,768]{1,0:T(8,128)(2,1)}, bf16[4,128,768]{2,1,0:T(8,128)(2,1)}, bf16[512,576]{1,0:T(8,128)(2,1)}, bf16[4,128,192]{2,1,0:T(8,128)(2,1)}...) custom-call(bf16[128,768]{1,0:T(8,128)(2,1)} %get-tuple-element.70.x, ...), custom_call_target="tpu_custom_call" | custom-call | tf_op jit(solution)/shard_map/pallas_call | solution.py:592
  232.6 87.7 %shard_map.243 = (f32[128,768]{1,0:T(8,128)}, bf16[128,768]{1,0:T(8,128)(2,1)}, f32[1,768]{1,0:T(1,128)}, f32[1,768]{1,0:T(1,128)}, f32[768,16]{1,0:T(8,128)}, /...) custom-call(bf16[128,768]{1,0:T(8,128)(2,1)} %select_bitcast_fusion., ...), custom_call_target="tpu_custom_call" | custom-call | tf_op jit(solution)/shard_map/pallas_call | solution.py:725
  320.2 1.0 convert_bitcast_fusion
  321.2 91.0 %shard_map.244 = (f32[128,768]{1,0:T(8,128)}, bf16[128,768]{1,0:T(8,128)(2,1)}, f32[1,768]{1,0:T(1,128)}, f32[1,768]{1,0:T(1,128)}, f32[768,16]{1,0:T(8,128)}, /...) custom-call(bf16[128,768]{1,0:T(8,128)(2,1)} %get-tuple-element.81.g, ...), custom_call_target="tpu_custom_call" | custom-call | tf_op jit(solution)/shard_map/pallas_call | solution.py:725
  412.3 1.0 reduce_sum.27
  413.6 1.2 reshape.240
  414.7 0.7 reduce.1
  417.3 42.2 %shard_map.245 = (f32[4,16,576]{2,1,0:T(8,128)S(1)}, f32[16,768]{1,0:T(8,128)S(1)}, f32[768,768]{1,0:T(8,128)}, f32[768,768]{1,0:T(8,128)}) custom-call(bf16[1024,576]{1,0:T(8,128)(2,1)} %get-tuple-element.92.pq0, bf16[1024,576]{1,0:T(8,128)(2,1)} %get-tuple-element.93.pq1, bf16[1024,576]{1,0:T(8,128)(2,1)} %get-tuple-element.94.gq0, ...), custom_call_target="tpu_custom_call" | custom-call | tf_op jit(solution)/shard_map/pallas_call | solution.py:967
  460.6 0.9 broadcast_in_dim_reshape.4
  464.3 0.8 maximum_select_fusion.1
  465.1 0.9 maximum_select_fusion
  466.1 3.4 copy.62
  469.5 1.4 copy.63
  (100 shorter events, 11.2 us)
Async XLA Ops:
  0.6 4.7 copy-start.2
  1.7 64.1 %collective-permute-start = (s32[128,2]{1,0:T(8,128)S(1)}, s32[128,2]{1,0:T(8,128)S(1)}, u32[]{:S(2)}, u32[]{:S(2)}) collective-permute-start(s32[128,2]{1,0:T(8,128)S(1)} %select_bitcast_fusion.2), channel_id=1, source_target_pairs={{0,64},{64,0},{1,65},{65,1},{2,66},{66,2},{3,67},{67,3},{4,68},{68... | collective-permute-start | bytes 3080 | tf_op jit(solution)/shard_map/ppermute | solution.py:1094
  5.3 1.4 copy-start
  6.7 0.9 copy-start.1
  7.6 1.3 copy-start.3
  8.9 0.9 copy-start.8
  9.8 39.9 %copy-start.15 = (bf16[2,1,128,768]{3,2,1,0:T(8,128)(2,1)S(1)}, bf16[2,1,128,768]{3,2,1,0:T(8,128)(2,1)}, u32[]{:S(2)}) copy-start(bf16[2,1,128,768]{3,2,1,0:T(8,128)(2,1)} %param.17) | copy-start | bytes 1179652
  50.5 3.8 copy-start.20
  50.5 3.9 copy-start.16
  321.2 92.2 %copy-start.17 = (f32[3,32,128]{2,1,0:T(8,128)S(1)}, f32[3,32,128]{2,1,0:T(8,128)}, u32[]{:S(2)}) copy-start(f32[3,32,128]{2,1,0:T(8,128)} %get-tuple-element.106) | copy-start | bytes 147460
  321.2 95.4 %copy-start.14 = (f32[768,16]{1,0:T(8,128)S(1)}, f32[768,16]{1,0:T(8,128)}, u32[]{:S(2)}) copy-start(f32[768,16]{1,0:T(8,128)} %get-tuple-element.107) | copy-start | bytes 147460
  412.2 4.5 copy-start.19
  412.2 4.6 copy-start.18
  412.3 4.9 %copy-start.4 = (bf16[256,768]{1,0:T(8,128)(2,1)S(1)}, bf16[256,768]{1,0:T(8,128)(2,1)}, u32[]{:S(2)}) copy-start(bf16[256,768]{1,0:T(8,128)(2,1)} %get-tuple-element.97.po1) | copy-start | bytes 1179652
  412.3 4.9 %copy-start.5 = (bf16[256,768]{1,0:T(8,128)(2,1)S(1)}, bf16[256,768]{1,0:T(8,128)(2,1)}, u32[]{:S(2)}) copy-start(bf16[256,768]{1,0:T(8,128)(2,1)} %get-tuple-element.96.po0) | copy-start | bytes 1179652
  412.3 4.9 %copy-start.6 = (bf16[256,768]{1,0:T(8,128)(2,1)S(1)}, bf16[256,768]{1,0:T(8,128)(2,1)}, u32[]{:S(2)}) copy-start(bf16[256,768]{1,0:T(8,128)(2,1)} %get-tuple-element.98.go0) | copy-start | bytes 1179652
  412.3 4.9 %copy-start.7 = (bf16[1024,64]{1,0:T(8,128)(2,1)S(1)}, bf16[1024,64]{1,0:T(8,128)(2,1)}, u32[]{:S(2)}) copy-start(bf16[1024,64]{1,0:T(8,128)(2,1)} %constant.78.clone.spread_ref) | copy-start | bytes 393220
  417.2 42.3 %copy-start.11 = (bf16[128,768]{1,0:T(8,128)(2,1)S(1)}, bf16[128,768]{1,0:T(8,128)(2,1)}, u32[]{:S(2)}) copy-start(bf16[128,768]{1,0:T(8,128)(2,1)} %get-tuple-element.81.g_ref) | copy-start | bytes 589828
  417.2 42.3 %copy-start.12 = (f32[128,768]{1,0:T(8,128)S(1)}, f32[128,768]{1,0:T(8,128)}, u32[]{:S(2)}) copy-start(f32[128,768]{1,0:T(8,128)} %get-tuple-element.91) | copy-start | bytes 1179652
  417.2 42.4 %copy-start.9 = (bf16[128,768]{1,0:T(8,128)(2,1)S(1)}, bf16[128,768]{1,0:T(8,128)(2,1)}, u32[]{:S(2)}) copy-start(bf16[128,768]{1,0:T(8,128)(2,1)} %get-tuple-element.70.x_ref) | copy-start | bytes 589828
  417.3 42.4 %copy-start.13 = (bf16[128,768]{1,0:T(8,128)(2,1)S(1)}, bf16[128,768]{1,0:T(8,128)(2,1)}, u32[]{:S(2)}) copy-start(bf16[128,768]{1,0:T(8,128)(2,1)} %get-tuple-element.71) | copy-start | bytes 589828
  459.6 5.6 %collective-permute-start.2 = (f32[128,768]{1,0:T(8,128)S(1)}, f32[128,768]{1,0:T(8,128)S(1)}, u32[]{:S(2)}, u32[]{:S(2)}) collective-permute-start(f32[128,768]{1,0:T(8,128)S(1)} %convert_select_fusion), channel_id=1, source_target_pairs={{0,64},{64,0},{1,65},{65,1},{2,66},{66,2},{3,67},{67,3},{4,68},{68... | collective-permute-start | bytes 1179656 | tf_op jit(solution)/shard_map/ppermute | solution.py:1122
  462.8 1.5 collective-permute-start.1
  466.1 3.4 copy-start.10

commit v5 on v4

--- a/solution.py
+++ b/solution.py
@@ -169,36 +169,80 @@
     return [pltpu.VMEM((n, width), BF16) for n in sizes]
 
 
-PAD = 32
+TILE = 16
+PARTS = 2
+
+
+class Loads:
+    def __init__(self, sems):
+        self.sems, self.copies = sems, []
+
+    def start(self, src, dst):
+        copy = pltpu.make_async_copy(src, dst, self.sems.at[len(self.copies)])
+        copy.start()
+        self.copies.append(copy)
+
+    def wait(self, *which):
+        for k in which:
+            self.copies[k].wait()
+
+    def wait_all(self):
+        self.wait(*range(len(self.copies)))
+
+
+def set_slots(main, extra, values):
+    count = extra.shape[0]
+    main[...] = values[: count * TILE].astype(BF16).reshape(main.shape)
+    for e in range(count):
+        extra[e] = values[count * TILE + e : count * TILE + e + 1]
+
+
+def get_slots(main, extra):
+    count = extra.shape[0]
+    rows = [extra[e] for e in range(count)]
+    first = main[...].reshape(count * TILE, main.shape[2])
+    return jnp.concatenate([first, jnp.concatenate(rows, 0).astype(BF16)], 0)
 
 
 class Exchange:
-    def __init__(self, src, dst, send, recv):
-        self.src, self.dst, self.send, self.recv = src, dst, send, recv
+    def __init__(self, copy, send, recv):
+        self.copy, self.send, self.recv = copy, send, recv
         self.me, self.count = lax.axis_index("exp"), lax.axis_size("exp")
 
-    def copy(self, k):
-        peer = lax.rem(self.me + k, self.count)
-        return remote(
-            self.src.at[peer], self.dst.at[self.me], self.send, self.recv, k, "exp", peer
-        )
-
-    def each(self, act):
+    def each(self, act, first=1, last=None):
         def body(k, carry):
-            act(self.copy(k))
+            act(self.copy(self, k))
             return carry
 
-        lax.fori_loop(1, self.count, body, 0)
-
-    def start(self):
-        self.each(lambda c: c.start())
-        self.dst[self.me] = self.src[self.me]
-
-    def wait_recv(self):
-        self.each(lambda c: c.wait_recv())
+        lax.fori_loop(first, self.count if last is None else last, body, 0)
+
+    def start(self, *span):
+        self.each(lambda c: c.start(), *span)
+
+    def wait_recv(self, *span):
+        self.each(lambda c: c.wait_recv(), *span)
 
     def wait_send(self):
         self.each(lambda c: c.wait_send())
+
+    def to(self, src, dst, k, peer):
+        return remote(src, dst, self.send, self.recv, k, "exp", peer)
+
+
+def exchange_out(src, dst, send, recv):
+    def copy(x, k):
+        peer = lax.rem(x.me + k, x.count)
+        return x.to(src.at[peer], dst.at[k], k, peer)
+
+    return Exchange(copy, send, recv)
+
+
+def exchange_home(src, dst, send, recv):
+    def copy(x, k):
+        peer = lax.rem(x.me + x.count - k, x.count)
+        return x.to(src.at[k], dst.at[x.me], k, peer)
+
+    return Exchange(copy, send, recv)
 
 
 def meet_all(partner=None):
@@ -221,60 +265,87 @@
     return ctx, right, left
 
 
-def run_experts(
-    ids, rows, out_ref, sel_ref, all_ref, ret_ref, block, beside, scratch
-):
-    inbox, part, res = scratch[:3]
-    bufs = scratch[3:9]
-    s_in, r_in, s_out, r_out, s_ag, r_ag, s_rs, r_rs = scratch[9:]
+def run_experts(ids, outs, all_ref, rets, block, done, beside, scratch):
+    part = scratch[0]
+    inbox, res = scratch[1:3], scratch[3:5]
+    s_in, r_in, s_out, r_out = scratch[5:7], scratch[7:9], scratch[9:11], scratch[11:13]
+    rest = scratch[13:]
     me, right, left = ids
     far = lax.rem(me + 2, 4)
-    flat = inbox.shape[0] * inbox.shape[1]
-    width = inbox.shape[2]
-
-    arriving = Exchange(out_ref, inbox, s_in, r_in)
-    arriving.start()
+    parts, _, rows, width = all_ref.shape
+    near = inbox[0].shape[0] // parts
+    filled = near * TILE
+    exp = lax.axis_index("exp")
+    arriving = [exchange_out(outs[m], inbox[m], s_in[m], r_in[m]) for m in range(2)]
+    leaving = [exchange_home(res[m], rets[m], s_out[m], r_out[m]) for m in range(2)]
+    gathers = [RingGather(all_ref.at[n], rows, ids, *rest[10 * n : 10 * n + 2]) for n in range(parts)]
+    scatters = [
+        RingScatter(
+            part.at[n], rows, ids, rest[10 * n + 4 : 10 * n + 10], *rest[10 * n + 2 : 10 * n + 4]
+        )
+        for n in range(parts)
+    ]
+    for n in range(parts):
+        for x in arriving:
+            x.start(max(1, n * near), (n + 1) * near)
+    for m in range(2):
+        inbox[m][0] = outs[m][exp]
     beside[0]()
-    arriving.wait_recv()
-    all_ref[me] = mm(sel_ref[...], inbox[...].reshape(flat, width)).astype(BF16)
-    gather = RingGather(all_ref, rows, ids, s_ag, r_ag)
-    scatter = RingScatter(part, rows, ids, bufs, s_rs, r_rs)
-    gather.start()
-    block(me, part)
-    gather.forward()
-    gather.wait_left()
-    block(left, part)
-    scatter.send_left()
-    gather.wait_right()
-    block(right, part)
-    scatter.send_right()
-    gather.wait_far()
-    block(far, part)
-    scatter.send_far()
+    for n in range(parts):
+        for x in arriving:
+            x.wait_recv(max(1, n * near), (n + 1) * near)
+        all_ref[n, me, :filled] = inbox[0][n * near : (n + 1) * near].reshape(filled, width)
+        last = [inbox[1][n * near + k] for k in range(near)]
+        last.append(jnp.zeros((rows - filled - near, width), F32))
+        all_ref[n, me, filled:] = jnp.concatenate(last, 0).astype(BF16)
+        gathers[n].start()
+    for n in range(parts):
+        block(n, me, part)
+    for g in gathers:
+        g.forward()
+    for n in range(parts):
+        gathers[n].wait_left()
+        block(n, left, part)
+        scatters[n].send_left()
+        gathers[n].wait_right()
+        block(n, right, part)
+        scatters[n].send_right()
+        gathers[n].wait_far()
+        block(n, far, part)
+        scatters[n].send_far()
+        done(n)
     beside[1]()
-    scatter.send_sums()
+    for n in range(parts):
+        scatters[n].send_sums()
     beside[2]()
-    padded = mm_tn(sel_ref[...], scatter.total().astype(BF16)).astype(BF16)
-    res[...] = padded.reshape(res.shape)
-    leaving = Exchange(res, ret_ref, s_out, r_out)
-    leaving.start()
+    for n in range(parts):
+        total = scatters[n].total().astype(BF16)
+        res[0][n * near : (n + 1) * near] = total[:filled].reshape(near, TILE, width)
+        last = total[filled:].astype(F32)
+        for k in range(near):
+            res[1][n * near + k] = last[k : k + 1]
+        for x in leaving:
+            x.start(max(1, n * near), (n + 1) * near)
+    for m in range(2):
+        rets[m][exp] = res[m][0]
     beside[3]()
-    leaving.wait_recv()
-    gather.wait_send()
-    scatter.wait_send()
-    arriving.wait_send()
-    leaving.wait_send()
+    for x in leaving:
+        x.wait_recv()
+    for x in (*gathers, *scatters, *arriving, *leaving):
+        x.wait_send()
+
+
+def slot_buffers(experts, width):
+    return [pltpu.VMEM((experts, TILE, width), BF16), pltpu.VMEM((experts, 1, width), F32)]
 
 
 def expert_scratch(experts, rows, width):
-    v = lambda *shape: pltpu.VMEM((*shape, width), BF16)
+    ring = [*[pltpu.SemaphoreType.DMA((6,))] * 4, *scatter_buffers(rows, width)]
     return [
-        v(experts, PAD),
-        v(4, rows),
-        v(experts, PAD),
-        *scatter_buffers(rows, width),
-        *[pltpu.SemaphoreType.DMA((experts,))] * 4,
-        *[pltpu.SemaphoreType.DMA((6,))] * 4,
+        pltpu.VMEM((PARTS, 4, rows, width), BF16),
+        *slot_buffers(experts, width) * 2,
+        *[pltpu.SemaphoreType.DMA((experts,))] * 8,
+        *ring * PARTS,
     ]
 
 
@@ -287,11 +358,12 @@
     col = lax.broadcasted_iota(jnp.int32, (rows, rows), 1)
     before = jnp.where(row > col, 1.0, 0.0).astype(BF16)
     earlier = mm(before, (hot[0] + hot[1]).astype(BF16))
-    wide = lax.broadcasted_iota(jnp.int32, (rows, experts * PAD), 1).astype(F32)
+    wide = lax.broadcasted_iota(jnp.int32, (rows, experts * (TILE + 1)), 1).astype(F32)
     slots = []
     for c in range(TOP):
         slot = jnp.sum(hot[c] * earlier, -1, keepdims=True)
-        target = routes[:, c : c + 1].astype(F32) * PAD + slot
+        expert = routes[:, c : c + 1].astype(F32)
+        target = jnp.where(slot < TILE, expert * TILE + slot, experts * TILE + expert)
         slots.append(jnp.where(wide == target, 1.0, 0.0).astype(BF16))
     return hot, slots
 
@@ -304,59 +376,8 @@
     return [r * total for r in raised]
 
 
-def selection(experts, capacity):
-    sel = np.zeros((experts * capacity, experts, PAD), np.float32)
-    for e in range(experts):
-        for s in range(capacity):
-            sel[e * capacity + s, e, s] = 1
-    return jnp.asarray(sel.reshape(experts * capacity, experts * PAD), BF16)
-
-
-def experts_forward(outgoing, sel, w_in, w_back):
-    experts, _, width = outgoing.shape
-    rows = sel.shape[0]
-    vm = pl.BlockSpec(memory_space=pltpu.VMEM)
-    return pl.pallas_call(
-        functools.partial(experts_kernel, rows),
-        out_shape=(
-            jax.ShapeDtypeStruct(outgoing.shape, BF16),
-            jax.ShapeDtypeStruct((4, rows, width), BF16),
-            jax.ShapeDtypeStruct((4, rows, w_in.shape[1]), F32),
-        ),
-        in_specs=[vm] * 4,
-        out_specs=(vm,) * 3,
-        scratch_shapes=expert_scratch(experts, rows, width),
-        compiler_params=pltpu.CompilerParams(
-            collective_id=2, has_side_effects=True, vmem_limit_bytes=48 << 20
-        ),
-    )(outgoing, sel, w_in, w_back)
-
-
-def experts_backward(outgoing, sel, w_in, w_back, entering, pre):
-    experts, _, width = outgoing.shape
-    rows, hid = sel.shape[0], w_in.shape[1]
-    vm = pl.BlockSpec(memory_space=pltpu.VMEM)
-    return pl.pallas_call(
-        functools.partial(experts_back_kernel, rows),
-        out_shape=(
-            jax.ShapeDtypeStruct(outgoing.shape, BF16),
-            jax.ShapeDtypeStruct(w_in.shape, F32),
-            jax.ShapeDtypeStruct(w_back.shape, F32),
-            jax.ShapeDtypeStruct(w_in.shape, BF16),
-            jax.ShapeDtypeStruct(w_back.shape, BF16),
-        ),
-        in_specs=[vm] * 6,
-        out_specs=(vm,) * 5,
-        scratch_shapes=[
-            pltpu.VMEM((4, rows, width), BF16),
-            pltpu.VMEM((4, rows, hid), BF16),
-            pltpu.VMEM((4, rows, hid), BF16),
-            *expert_scratch(experts, rows, width),
-        ],
-        compiler_params=pltpu.CompilerParams(
-            collective_id=3, has_side_effects=True, vmem_limit_bytes=48 << 20
-        ),
-    )(outgoing, sel, w_in, w_back, entering, pre)
+def part_rows(experts, capacity):
+    return -(-(experts // PARTS) * capacity // TILE) * TILE
 
 
 def bucket_bounds():
@@ -538,59 +559,72 @@
 
 
 def layer_kernel(
-    x_ref, gain_one, gain_two, w_qkv, w_out, table_ref, kind_ref, router_ref, routes_ref,
-    sel_ref, w_in, w_back,
+    layer, x_ref, gains, w_qkv_both, w_out_both, tables, kind_ref, routers, routes_ref,
+    w_in_both, w_back_both,
     h_ref, all_ref, proj_ref, att_ref, middle_ref, mixed_ref, logits_ref, picked_ref,
-    ent_ref, pre_ref, *scratch
+    ent_out, pre_out, *scratch
 ):
-    tiles_ref, s_ref, p_ref, part, out_ref, ret_ref = scratch[:6]
+    tiles_ref, s_ref, p_ref, part, w_in, w_back, ent_ref, pre_ref, sems, save_sems = scratch[:10]
+    outs, rets = scratch[10:12], scratch[12:14]
+    loads, saves = Loads(sems), Loads(save_sems)
+    loads.start(w_in_both.at[layer], w_in)
+    loads.start(w_back_both.at[layer], w_back)
+    gain_one, gain_two = gains.at[2 * layer], gains.at[2 * layer + 1]
+    w_qkv, w_out = w_qkv_both.at[layer], w_out_both.at[layer]
+    table_ref, router_ref = tables.at[layer], routers.at[layer]
     ids = meet_all()
     rows, width = x_ref.shape
     x = x_ref[...].astype(F32)
     branch = attend(
         ids, x, gain_one, w_qkv, w_out, table_ref, kind_ref, all_ref, proj_ref, att_ref,
-        tiles_ref, s_ref, p_ref, part, scratch[6:16]
+        tiles_ref, s_ref, p_ref, part, scratch[14:24]
     )
     middle = x + branch
     middle_ref[...] = middle
     mixed = norm(middle, gain_two[...])
     mixed_ref[...] = mixed
-    hot, slots = route_tables(routes_ref, out_ref.shape[0])
-    out_ref[...] = mm_tn(slots[0] + slots[1], mixed).astype(BF16).reshape(out_ref.shape)
-
-    def block(j, part):
-        pre = mm(ent_ref[j], w_in[...])
-        pre_ref[j] = pre
+    hot, slots = route_tables(routes_ref, logits_ref.shape[1])
+    set_slots(*outs, mm_tn(slots[0] + slots[1], mixed))
+
+    def block(n, j, part):
+        pre = mm(ent_ref[n, j], w_in[...])
+        pre_ref[n, j] = pre
         hidden = gelu_parts(pre)[0].astype(BF16)
-        part[j] = mm_nt(hidden, w_back[...]).astype(BF16)
+        part[n, j] = mm_nt(hidden, w_back[...]).astype(BF16)
 
     def find_logits():
         logits_ref[...] = mm(mixed_ref[...], router_ref[...])
+        loads.wait_all()
+
+    def save(n):
+        saves.start(ent_ref.at[n], ent_out.at[n])
+        saves.start(pre_ref.at[n], pre_out.at[n])
 
     nothing = lambda: None
     run_experts(
-        ids, sel_ref.shape[0], out_ref, sel_ref, ent_ref, ret_ref, block,
-        (find_logits, nothing, nothing, nothing), scratch[16:]
+        ids, outs, ent_ref, rets, block, save,
+        (find_logits, nothing, nothing, nothing), scratch[24:]
     )
     gates = gates_of(logits_ref[...], hot)
-    returned = ret_ref[...].reshape(slots[0].shape[1], width)
+    returned = get_slots(*rets)
     y = middle_ref[...]
     for c in range(TOP):
         picked = mm(slots[c], returned)
         picked_ref[c] = picked.astype(BF16)
         y = y + gates[c] * picked
     h_ref[...] = y.astype(BF16)
-
-
-def layer_forward(x, weights, kind, routes, sel):
-    w_qkv, w_out, gain_one, gain_two, table, router, w_in, w_back = weights
+    saves.wait_all()
+
+
+def layer_forward(x, layer, weights, kind, routes, slots):
+    gains, w_qkv, w_out, table, router, w_in, w_back = weights
     rows, width = x.shape
-    seq, part, experts = 4 * rows, w_out.shape[0], router.shape[1]
-    heads, slots = part // HEAD_DIM, sel.shape[0]
-    vm = pl.BlockSpec(memory_space=pltpu.VMEM)
+    seq, part, experts = 4 * rows, w_out.shape[1], router.shape[2]
+    heads = part // HEAD_DIM
+    vm, far = pl.BlockSpec(memory_space=pltpu.VMEM), pl.BlockSpec(memory_space=pl.ANY)
     shape = jax.ShapeDtypeStruct
     return pl.pallas_call(
-        layer_kernel,
+        functools.partial(layer_kernel, layer),
         out_shape=(
             shape(x.shape, BF16),
             shape((4, rows, width), BF16),
@@ -600,39 +634,60 @@
             shape(x.shape, BF16),
             shape((rows, experts), F32),
             shape((TOP, rows, width), BF16),
-            shape((4, slots, width), BF16),
-            shape((4, slots, w_in.shape[1]), F32),
+            shape((PARTS, 4, slots, width), BF16),
+            shape((PARTS, 4, slots, w_in.shape[2]), F32),
         ),
-        in_specs=[vm] * 12,
-        out_specs=(vm,) * 10,
+        in_specs=[vm] * 8 + [far] * 2,
+        out_specs=(vm,) * 8 + (far,) * 2,
         scratch_shapes=[
             pltpu.VMEM((heads, KINDS - 1, SPAN, seq), F32),
             pltpu.VMEM((seq, seq), F32),
             pltpu.VMEM((seq, seq), BF16),
             pltpu.VMEM((4, rows, width), BF16),
-            pltpu.VMEM((experts, PAD, width), BF16),
-            pltpu.VMEM((experts, PAD, width), BF16),
+            pltpu.VMEM(w_in.shape[1:], BF16),
+            pltpu.VMEM(w_back.shape[1:], BF16),
+            pltpu.VMEM((PARTS, 4, slots, width), BF16),
+            pltpu.VMEM((PARTS, 4, slots, w_in.shape[2]), F32),
+            pltpu.SemaphoreType.DMA((2,)),
+            pltpu.SemaphoreType.DMA((2 * PARTS,)),
+            *slot_buffers(experts, width) * 2,
             *scatter_buffers(rows, width),
             *[pltpu.SemaphoreType.DMA((6,))] * 4,
             *expert_scratch(experts, slots, width),
         ],
         compiler_params=pltpu.CompilerParams(
-            collective_id=0, has_side_effects=True, vmem_limit_bytes=56 << 20
+            collective_id=layer, has_side_effects=True, vmem_limit_bytes=56 << 20
         ),
-    )(x, gain_one, gain_two, w_qkv, w_out, table, kind, router, routes, sel, w_in, w_back)
+    )(x, gains, w_qkv, w_out, table, kind, router, routes, w_in, w_back)
 
 
 def layer_back_kernel(
-    g_ref, x_ref, gain_one, gain_two, w_qkv, w_out, table_ref, kind_ref, router_ref, routes_ref,
-    sel_ref, w_in, w_back, perm_ref, perm_out_ref,
-    all_ref, proj_ref, att_ref, middle_ref, mixed_ref, logits_ref, picked_ref, ent_ref, pre_ref,
-    dx_ref, dxb_ref, dgain_one, dgain_two, drouter_ref, pq_ref, po_ref, dtable_ref,
-    d_in, d_back, got_in, got_back, got_pq, got_po, *scratch
+    layer, g_ref, x_ref, gains, w_qkv_both, w_out_both, tables, kind_ref, routers, routes_ref,
+    middle_ref, mixed_ref, logits_ref, picked_ref,
+    w_in_both, w_back_both, perm_in, perm_out_in, all_in, proj_in, att_in, ent_in, pre_in,
+    dx_ref, dxb_ref, small_ref, pq_ref, po_ref,
+    d_in_out, d_back_out, got_in, got_back, got_pq, got_po, *scratch
 ):
     (
         tiles_ref, dtiles_ref, s_ref, dp_ref, p_ref, ds_ref, da_ref, dproj_ref, db_ref, part,
-        out_ref, ret_ref, darr_ref, hid_ref, dpre_ref, e_in, e_back, s_x, r_x
-    ) = scratch[:19]
+        darr_ref, hid_ref, dpre_ref, e_in, e_back, drouter_ref, dtable_ref, s_x, r_x,
+        d_in, d_back, w_in, w_back, perm_ref, perm_out_ref, all_ref, proj_ref, att_ref,
+        ent_ref, pre_ref, sems, save_sems
+    ) = scratch[:32]
+    outs, rets = scratch[32:34], scratch[34:36]
+    loads, saves = Loads(sems), Loads(save_sems)
+    loads.start(w_back_both.at[layer], w_back)
+    loads.start(w_in_both.at[layer], w_in)
+    loads.start(pre_in, pre_ref)
+    loads.start(ent_in, ent_ref)
+    loads.start(all_in, all_ref)
+    loads.start(proj_in, proj_ref)
+    loads.start(att_in, att_ref)
+    loads.start(perm_in, perm_ref)
+    loads.start(perm_out_in, perm_out_ref)
+    gain_one, gain_two = gains.at[2 * layer], gains.at[2 * layer + 1]
+    w_qkv, w_out = w_qkv_both.at[layer], w_out_both.at[layer]
+    table_ref, router_ref = tables.at[layer], routers.at[layer]
     partner = 1 - lax.axis_index("section")
     ids = meet_all(partner)
     rows, width = x_ref.shape
@@ -647,12 +702,12 @@
         across(3, po_ref, got_po),
     ]
     g = g_ref[...].astype(F32)
-    hot, slots = route_tables(routes_ref, out_ref.shape[0])
+    hot, slots = route_tables(routes_ref, logits_ref.shape[1])
     gates = gates_of(logits_ref[...], hot)
     dreturned = mm_tn(slots[0], (gates[0] * g).astype(BF16)) + mm_tn(
         slots[1], (gates[1] * g).astype(BF16)
     )
-    out_ref[...] = dreturned.astype(BF16).reshape(out_ref.shape)
+    set_slots(*outs, dreturned)
 
     def logits_back():
         g = g_ref[...].astype(F32)
@@ -664,84 +719,93 @@
         dlogits = (hot[0] * dchosen[0] + hot[1] * dchosen[1]).astype(BF16)
         drouter_ref[...] = mm_tn(mixed_ref[...], dlogits)
         dx_ref[...] = mm_nt(dlogits, router_ref[...])
-
-    def block(j, part):
-        hidden, slope = gelu_parts(pre_ref[j])
-        hid_ref[j] = hidden.astype(BF16)
-        dpre = (mm(darr_ref[j], w_back[...]) * slope).astype(BF16)
-        dpre_ref[j] = dpre
-        part[j] = mm_nt(dpre, w_in[...]).astype(BF16)
+        loads.wait(0, 1, 2)
+
+    def block(n, j, expert_part):
+        hidden, slope = gelu_parts(pre_ref[n, j])
+        hid_ref[n, j] = hidden.astype(BF16)
+        dpre = (mm(darr_ref[n, j], w_back[...]) * slope).astype(BF16)
+        dpre_ref[n, j] = dpre
+        expert_part[n, j] = mm_nt(dpre, w_in[...]).astype(BF16)
 
     def flat(ref):
-        return ref[...].reshape(ref.shape[0] * ref.shape[1], ref.shape[2])
+        return ref[...].reshape(math.prod(ref.shape[:3]), ref.shape[3])
 
     def back_grad():
         grad = mm_tn(flat(darr_ref), flat(hid_ref))
         d_back[...] = grad
+        saves.start(d_back, d_back_out)
         e_back[...] = grad.astype(BF16)
         crossing[0].start()
 
     def in_grad():
+        loads.wait(3)
         grad = mm_tn(flat(ent_ref), flat(dpre_ref))
         d_in[...] = grad
+        saves.start(d_in, d_in_out)
         e_in[...] = grad.astype(BF16)
         crossing[1].start()
 
     run_experts(
-        ids, sel_ref.shape[0], out_ref, sel_ref, darr_ref, ret_ref, block,
-        (logits_back, back_grad, lambda: None, in_grad), scratch[29:]
-    )
-    dleft = ret_ref[...].reshape(slots[0].shape[1], width)
+        ids, outs, darr_ref, rets, block, lambda n: None,
+        (logits_back, back_grad, lambda: None, in_grad), scratch[46:]
+    )
+    dleft = get_slots(*rets)
+    loads.wait(*range(4, 9))
     dmixed = mm(slots[0] + slots[1], dleft) + dx_ref[...]
     dnorm, dgain = norm_back(middle_ref[...], gain_two[...], dmixed)
-    dgain_two[...] = dgain
+    small_ref[...] = pack_gain(dgain, 1, small_ref.shape) + pack_router(
+        drouter_ref[...], small_ref.shape
+    )
     dmiddle = g_ref[...].astype(F32) + dnorm
     dx_ref[...] = dmiddle
     dnormed = attend_back(
         ids, dmiddle, all_ref, proj_ref, att_ref, w_qkv, w_out, table_ref, kind_ref,
         perm_ref, perm_out_ref, pq_ref, po_ref, dtable_ref, lambda k: crossing[2 + k].start(),
         tiles_ref, dtiles_ref, s_ref, dp_ref, p_ref, ds_ref, da_ref, dproj_ref, db_ref, part,
-        scratch[19:29]
+        scratch[36:46]
     )
     dnorm, dgain = norm_back(x_ref[...].astype(F32), gain_one[...], dnormed)
-    dgain_one[...] = dgain
+    small_ref[...] += pack_gain(dgain, 0, small_ref.shape) + pack_table(
+        dtable_ref, small_ref.shape
+    )
     dx = dx_ref[...] + dnorm
     dx_ref[...] = dx
     dxb_ref[...] = dx.astype(BF16)
+    saves.wait_all()
     for c in crossing:
         c.wait()
 
 
-def layer_backward(g, keep, weights, kind, routes, sel, perm, perm_out):
-    x, *saved = keep
-    w_qkv, w_out, gain_one, gain_two, table, router, w_in, w_back = weights
+def layer_backward(g, keep, layer, weights, kind, routes, slots, perm, perm_out):
+    x, normed, proj, attended, middle, mixed, logits, picked, entering, pre = keep
+    gains, w_qkv, w_out, table, router, w_in, w_back = weights
     rows, width = x.shape
-    seq, part, experts = 4 * rows, w_out.shape[0], router.shape[1]
-    heads, slots, hid = part // HEAD_DIM, sel.shape[0], w_in.shape[1]
-    vm = pl.BlockSpec(memory_space=pltpu.VMEM)
+    seq, part, experts = 4 * rows, w_out.shape[1], router.shape[2]
+    heads, hid = part // HEAD_DIM, w_in.shape[2]
+    w_shape = w_in.shape[1:]
+    vm, far = pl.BlockSpec(memory_space=pltpu.VMEM), pl.BlockSpec(memory_space=pl.ANY)
     shape = jax.ShapeDtypeStruct
     pq = shape((perm.shape[0], 3 * part), BF16)
     po = shape((perm_out.shape[0], width), BF16)
+    loaded = (normed, proj, attended, entering, pre)
     return pl.pallas_call(
-        layer_back_kernel,
+        functools.partial(layer_back_kernel, layer),
         out_shape=(
             shape(x.shape, F32),
             shape(x.shape, BF16),
-            shape((1, width), F32),
-            shape((1, width), F32),
-            shape((width, experts), F32),
+            shape((perm.shape[0] // 16, SMALL), F32),
             pq,
             po,
-            shape((heads, BUCKETS, 2 * SPAN), F32),
-            shape(w_in.shape, F32),
-            shape(w_back.shape, F32),
-            shape(w_in.shape, BF16),
-            shape(w_back.shape, BF16),
+            shape(w_shape, F32),
+            shape(w_shape, F32),
+            shape(w_shape, BF16),
+            shape(w_shape, BF16),
             pq,
             po,
         ),
-        in_specs=[vm] * 24,
-        out_specs=(vm,) * 14,
+        in_specs=[vm] * 13 + [far] * 9,
+        out_specs=(vm,) * 5 + (far,) * 6,
         scratch_shapes=[
             pltpu.VMEM((heads, KINDS - 1, SPAN, seq), F32),
             pltpu.VMEM((KINDS, SPAN, seq), F32),
@@ -753,25 +817,117 @@
             pltpu.VMEM((4, rows, 3 * part), BF16),
             pltpu.VMEM((4, rows, width), BF16),
             pltpu.VMEM((4, rows, width), BF16),
-            pltpu.VMEM((experts, PAD, width), BF16),
-            pltpu.VMEM((experts, PAD, width), BF16),
-            pltpu.VMEM((4, slots, width), BF16),
-            pltpu.VMEM((4, slots, hid), BF16),
-            pltpu.VMEM((4, slots, hid), BF16),
-            pltpu.VMEM(w_in.shape, BF16),
-            pltpu.VMEM(w_back.shape, BF16),
+            pltpu.VMEM((PARTS, 4, slots, width), BF16),
+            pltpu.VMEM((PARTS, 4, slots, hid), BF16),
+            pltpu.VMEM((PARTS, 4, slots, hid), BF16),
+            pltpu.VMEM(w_shape, BF16),
+            pltpu.VMEM(w_shape, BF16),
+            pltpu.VMEM((width, experts), F32),
+            pltpu.VMEM((heads, BUCKETS, 2 * SPAN), F32),
             *[pltpu.SemaphoreType.DMA((4,))] * 2,
+            *[pltpu.VMEM(w_shape, F32)] * 2,
+            *[pltpu.VMEM(w_shape, BF16)] * 2,
+            *[pltpu.VMEM(a.shape, a.dtype) for a in (perm, perm_out, *loaded)],
+            pltpu.SemaphoreType.DMA((9,)),
+            pltpu.SemaphoreType.DMA((2,)),
+            *slot_buffers(experts, width) * 2,
             *scatter_buffers(rows, width),
             *[pltpu.SemaphoreType.DMA((6,))] * 4,
             *expert_scratch(experts, slots, width),
         ],
         compiler_params=pltpu.CompilerParams(
-            collective_id=1, has_side_effects=True, vmem_limit_bytes=60 << 20
+            collective_id=2 + layer, has_side_effects=True, vmem_limit_bytes=60 << 20
         ),
     )(
-        g, x, gain_one, gain_two, w_qkv, w_out, table, kind, router, routes, sel, w_in, w_back,
-        perm, perm_out, *saved
-    )
+        g, x, gains, w_qkv, w_out, table, kind, router, routes, middle, mixed, logits, picked,
+        w_in, w_back, perm, perm_out, *loaded
+    )
+
+
+SMALL = 256
+OWN = 12
+AT_TABLE = 2 * OWN
+
+
+def grid_of(shape):
+    return tuple(lax.broadcasted_iota(jnp.int32, shape, d) for d in (0, 1))
+
+
+def one_hot(where):
+    return jnp.where(where, 1.0, 0.0).astype(BF16)
+
+
+def owner_rows(owners, width):
+    row, col = grid_of((owners, width))
+    return one_hot((col >= OWN * row) & (col < OWN * row + OWN))
+
+
+def table_rows(owners):
+    row, col = grid_of((BUCKETS, owners))
+    return one_hot(col == 2 * row + lax.axis_index("ctx") // 2)
+
+
+def table_column(head):
+    return AT_TABLE + HEADS // 4 * lax.rem(lax.axis_index("ctx"), 2) + head
+
+
+def at_router(experts):
+    return AT_TABLE + BUCKETS * HEADS // 64
+
+
+def router_mask(width, experts):
+    row, col = grid_of((width, SMALL))
+    first = at_router(experts) + experts * lax.rem(row, OWN)
+    return (col >= first) & (col < first + experts)
+
+
+def unpack_small(small, width, experts, heads):
+    owners = small.shape[0]
+    small = small.astype(BF16)
+    own = owner_rows(owners, width)
+    spread = mm_tn(small[:, :128], own)
+    row, col = grid_of(spread.shape)
+    gains = [
+        jnp.sum(jnp.where(row == lax.rem(col, OWN) + n * OWN, spread, 0.0), 0, keepdims=True)
+        for n in range(2)
+    ]
+    wide = mm_tn(own, small)
+    wide = jnp.where(router_mask(width, experts), wide, 0.0).astype(BF16)
+    row, col = grid_of((SMALL, experts))
+    first = at_router(experts)
+    inside = (row >= first) & (row < first + OWN * experts)
+    router = mm(wide, one_hot(inside & (lax.rem(row + experts - first % experts, experts) == col)))
+    table = mm(table_rows(owners), small[:, :128]).astype(BF16)
+    row, col = grid_of((128, heads))
+    table = mm(table, one_hot(row == table_column(col)))
+    return gains, router.astype(BF16), table
+
+
+def pack_gain(dgain, n, shape):
+    width = dgain.shape[1]
+    row, col = grid_of((width, shape[1]))
+    own = owner_rows(shape[0], width).astype(F32) * dgain
+    return mm(own.astype(BF16), one_hot(col == lax.rem(row, OWN) + n * OWN))
+
+
+def pack_router(drouter, shape):
+    width, experts = drouter.shape
+    row, col = grid_of((experts, shape[1]))
+    first = at_router(experts)
+    wide = mm(
+        drouter.astype(BF16), one_hot(lax.rem(col + experts - first % experts, experts) == row)
+    )
+    wide = jnp.where(router_mask(width, experts), wide, 0.0).astype(BF16)
+    return mm(owner_rows(shape[0], width), wide)
+
+
+def pack_table(dtable_ref, shape):
+    total = jnp.zeros((BUCKETS, shape[1]), F32)
+    col = grid_of(total.shape)[1]
+    for h in range(dtable_ref.shape[0]):
+        column = jnp.sum(dtable_ref[h], -1, keepdims=True)
+        total = total + jnp.where(col == table_column(h), column, 0.0)
+    return mm_tn(table_rows(shape[0]), total.astype(BF16))
 
 
 def meet_everyone():
@@ -800,7 +956,7 @@
 
 def weights_kernel(
     cols_ref, outp_ref, w_in, w_back, perm_ref, perm_out_ref, pick_ref,
-    w_qkv, w_out, small_ref, both_in, both_back,
+    w_qkv, w_out, gains, routers, tables, both_in, both_back,
     zin, grid, grid_out, s_z, r_z, s_q, r_q, s_o, r_o, s_fq, r_fq, s_fo, r_fo, s_x, r_x, s_own
 ):
     meet_everyone()
@@ -810,6 +966,10 @@
     turn = ctx_exchange(cols_ref, zin, s_z, r_z)
     for c in turn:
         c.start()
+    cross_in = remote(w_in, both_in.at[section], s_x, r_x, 0, "section", partner)
+    cross_back = remote(w_back, both_back.at[section], s_x, r_x, 1, "section", partner)
+    cross_in.start()
+    cross_back.start()
     zin[ctx] = cols_ref[ctx]
     grid_out[section, exp] = outp_ref[...]
 
@@ -840,8 +1000,6 @@
     own_back = pltpu.make_async_copy(w_back, both_back.at[section], s_own.at[1])
     own_in.start()
     own_back.start()
-    cross_in = remote(w_in, both_in.at[section], s_x, r_x, 0, "section", partner)
-    cross_back = remote(w_back, both_back.at[section], s_x, r_x, 1, "section", partner)
 
     def relay(ref, s, r, sf, rf, k):
         spread(ref, s, r, k).wait_recv()
@@ -849,13 +1007,15 @@
 
     each(lambda k: relay(grid_out, s_o, r_o, s_fo, r_fo, k))
     each(lambda k: relay(grid, s_q, r_q, s_fq, r_fq, k))
-    cross_in.start()
-    cross_back.start()
 
     def unpack(layer):
         flat = grid[layer].reshape(perm_ref.shape[0], grid.shape[3])
         w_qkv[layer] = mm_tn(perm_ref[...], flat).astype(BF16)
-        small_ref[layer] = mm(pick_ref[...], flat)
+        small = mm(pick_ref[...], flat[:, :SMALL])
+        two, routers[layer], tables[layer] = unpack_small(
+            small, routers.shape[1], routers.shape[2], tables.shape[2]
+        )
+        gains[2 * layer], gains[2 * layer + 1] = two
         flat = grid_out[layer].reshape(perm_out_ref.shape[0], grid_out.shape[3])
         w_out[layer] = mm_tn(perm_out_ref[...], flat).astype(BF16)
 
@@ -878,19 +1038,21 @@
 def gather_weights(cols, outp, w_in, w_back, perm, perm_out, pick):
     width, part = outp.shape[1], cols.shape[2]
     count = perm_out.shape[0] // 16
-    vm = pl.BlockSpec(memory_space=pltpu.VMEM)
+    vm, far = pl.BlockSpec(memory_space=pltpu.VMEM), pl.BlockSpec(memory_space=pl.ANY)
     dma = lambda n: pltpu.SemaphoreType.DMA((n,))
     return pl.pallas_call(
         weights_kernel,
         out_shape=(
             jax.ShapeDtypeStruct((2, width, part), BF16),
             jax.ShapeDtypeStruct((2, perm_out.shape[1], width), BF16),
-            jax.ShapeDtypeStruct((2, pick.shape[0], part), F32),
+            jax.ShapeDtypeStruct((4, 1, width), F32),
+            jax.ShapeDtypeStruct((2, width, count), BF16),
+            jax.ShapeDtypeStruct((2, BUCKETS, part // (3 * HEAD_DIM)), F32),
             jax.ShapeDtypeStruct((2, *w_in.shape), BF16),
             jax.ShapeDtypeStruct((2, *w_back.shape), BF16),
         ),
-        in_specs=[vm] * 7,
-        out_specs=(vm,) * 5,
+        in_specs=[vm] * 2 + [far] * 2 + [vm] * 3,
+        out_specs=(vm,) * 5 + (far,) * 2,
         scratch_shapes=[
             pltpu.VMEM(cols.shape, BF16),
             pltpu.VMEM((2, count, 64, part), BF16),
@@ -904,42 +1066,77 @@
 
 
 def owners_kernel(
-    pq0, pq1, gq0, gq1, po0, po1, go0, go1, small_ref, spread_ref,
-    in0, in1, gin0, gin1, back0, back1, gback0, gback1,
-    turned, out_grad, d_in, d_back,
-    got_small, pieces, box, pieces_out, box_out, summed, s_s, r_s, s_q, r_q, s_o, r_o, s_z, r_z
+    small0, small1, spread_ref, y0, y1, dx0, dx1,
+    pq0, pq1, gq0, gq1, po0, po1, go0, go1, in0, in1, gin0, gin1, back0, back1, gback0, gback1,
+    turned, out_grad, d_in_out, d_back_out, layer_out, input_grad,
+    pq, gq, po, go, d_in, gin, d_back, gback,
+    sent_small, got_small, sent_y, sent_dx, pieces, box, pieces_out, box_out, summed,
+    s_s, r_s, s_q, r_q, s_o, r_o, s_z, r_z, sems, save_sems
 ):
-    meet_everyone()
     section, ctx, exp = (lax.axis_index(a) for a in ("section", "ctx", "exp"))
     partner = 1 - section
     first = section == 0
-    cross = remote(small_ref.at[partner], got_small, s_s, r_s, 0, "section", partner)
-    cross.start()
-
-    def chosen(a, b, c, d):
-        return jnp.where(first, a[...], b[...]).astype(F32) + jnp.where(
-            first, c[...], d[...]
-        ).astype(F32)
-
-    pieces_out[...] = chosen(po0, po1, go0, go1).astype(BF16).reshape(pieces_out.shape)
-    swap_out = Exchange(pieces_out, box_out, s_o, r_o)
-    swap_out.start()
-    dense = chosen(pq0, pq1, gq0, gq1)
-    cross.wait_recv()
-    small = small_ref[section] + got_small[...]
+    of_first = (po0, go0, pq0, gq0, in0, gin0, back0, gback0)
+    of_second = (po1, go1, pq1, gq1, in1, gin1, back1, gback1)
+    held = (po, go, pq, gq, d_in, gin, d_back, gback)
+
+    def load(sources):
+        for k, (src, dst) in enumerate(zip(sources, held)):
+            pltpu.make_async_copy(src, dst, sems.at[k]).start()
+
+    @pl.when(first)
+    def _():
+        load(of_first)
+
+    @pl.when(jnp.logical_not(first))
+    def _():
+        load(of_second)
+
+    def loaded(*which):
+        for k in which:
+            pltpu.make_async_copy(of_first[k], held[k], sems.at[k]).wait()
+
+    meet_everyone()
+    sent_small[...] = jnp.where(first, small1[...], small0[...])
+    cross = [
+        remote(sent_small, got_small, s_s, r_s, 0, "section", partner),
+        remote(sent_y, layer_out.at[section], s_s, r_s, 1, "section", partner),
+        remote(sent_dx, input_grad.at[section], s_s, r_s, 2, "section", partner),
+    ]
+    cross[0].start()
+
+    def both(a, b):
+        return a[...].astype(F32) + b[...].astype(F32)
+
+    loaded(2, 3)
+    dense = both(pq, gq)
+    cross[0].wait_recv()
+    small = jnp.where(first, small0[...], small1[...]) + got_small[...]
     wide = mm(spread_ref[...], small.astype(BF16))
     n = wide.shape[1]
     dense = jnp.concatenate([dense[:, :n] + wide, dense[:, n:]], 1)
     pieces[...] = dense.astype(BF16).reshape(pieces.shape)
-    swap = Exchange(pieces, box, s_q, r_q)
+    swap = exchange_out(pieces, box, s_q, r_q)
     swap.start()
-    d_in[...] = chosen(in0, in1, gin0, gin1)
-    d_back[...] = chosen(back0, back1, gback0, gback1)
-    swap_out.wait_recv()
-    total = box_out[0].astype(F32)
-    for k in range(1, box_out.shape[0]):
-        total = total + box_out[k].astype(F32)
-    out_grad[...] = total
+    loaded(0, 1)
+    pieces_out[...] = both(po, go).astype(BF16).reshape(pieces_out.shape)
+    swap_out = exchange_out(pieces_out, box_out, s_o, r_o)
+    swap_out.start()
+    box[0] = pieces[exp]
+    box_out[0] = pieces_out[exp]
+    sent_y[...] = jnp.where(first, y1[...], y0[...])
+    cross[1].start()
+    sent_dx[...] = jnp.where(first, dx1[...], dx0[...])
+    cross[2].start()
+    layer_out[section] = jnp.where(first, y0[...], y1[...])
+    input_grad[section] = jnp.where(first, dx0[...], dx1[...])
+    saves = Loads(save_sems)
+    loaded(4, 5)
+    d_in[...] += gin[...].astype(F32)
+    saves.start(d_in, d_in_out)
+    loaded(6, 7)
+    d_back[...] += gback[...].astype(F32)
+    saves.start(d_back, d_back_out)
     swap.wait_recv()
     total = box[0].astype(F32)
     for k in range(1, box.shape[0]):
@@ -949,21 +1146,30 @@
     for c in turn:
         c.start()
     turned[ctx] = summed[ctx]
+    swap_out.wait_recv()
+    total = box_out[0].astype(F32)
+    for k in range(1, box_out.shape[0]):
+        total = total + box_out[k].astype(F32)
+    out_grad[...] = total
     for c in turn:
         c.wait()
-    cross.wait_send()
+    cross[0].wait_send()
+    cross[1].wait()
+    cross[2].wait()
     swap.wait_send()
     swap_out.wait_send()
-
-
-def sum_at_owners(pq, gq, po, go, small, spread, d_in, g_in, d_back, g_back, count):
+    saves.wait_all()
+
+
+def sum_at_owners(pq, gq, po, go, small, spread, d_in, g_in, d_back, g_back, y, dx, count):
     rows, part = pq[0].shape
     out_rows, width = po[0].shape
-    vm = pl.BlockSpec(memory_space=pltpu.VMEM)
+    vm, far = pl.BlockSpec(memory_space=pltpu.VMEM), pl.BlockSpec(memory_space=pl.ANY)
     dma = lambda n: pltpu.SemaphoreType.DMA((n,))
     own = (rows // count, part)
     own_out = (out_rows // count, width)
     quarter = (4, rows // count // 4, part)
+    held = [a[0] for a in (pq, gq, po, go, d_in, g_in, d_back, g_back)]
     return pl.pallas_call(
         owners_kernel,
         out_shape=(
@@ -971,22 +1177,28 @@
             jax.ShapeDtypeStruct(own_out, F32),
             jax.ShapeDtypeStruct(d_in[0].shape, F32),
             jax.ShapeDtypeStruct(d_back[0].shape, F32),
+            jax.ShapeDtypeStruct((2, *y[0].shape), BF16),
+            jax.ShapeDtypeStruct((2, *dx[0].shape), F32),
         ),
-        in_specs=[vm] * 18,
-        out_specs=(vm,) * 4,
+        in_specs=[vm] * 7 + [far] * 16,
+        out_specs=(vm, vm, far, far, vm, vm),
         scratch_shapes=[
-            pltpu.VMEM(small.shape[1:], F32),
+            *[pltpu.VMEM(a.shape, a.dtype) for a in held],
+            pltpu.VMEM(small[0].shape, F32),
+            pltpu.VMEM(small[0].shape, F32),
+            pltpu.VMEM(y[0].shape, BF16),
+            pltpu.VMEM(dx[0].shape, F32),
             pltpu.VMEM((count, *own), BF16),
             pltpu.VMEM((count, *own), BF16),
             pltpu.VMEM((count, *own_out), BF16),
             pltpu.VMEM((count, *own_out), BF16),
             pltpu.VMEM(quarter, F32),
-            dma(1), dma(1), *[dma(count)] * 4, dma(4), dma(4),
+            dma(3), dma(3), *[dma(count)] * 4, dma(4), dma(4), dma(8), dma(2),
         ],
         compiler_params=pltpu.CompilerParams(
             collective_id=5, has_side_effects=True, vmem_limit_bytes=52 << 20
         ),
-    )(*pq, *gq, *po, *go, small, spread, *d_in, *g_in, *d_back, *g_back)
+    )(*small, spread, *y, *dx, *pq, *gq, *po, *go, *d_in, *g_in, *d_back, *g_back)
 
 
 def packing(n_ctx, n_exp, own_rows):
@@ -1050,7 +1262,7 @@
     heads = HEADS // n_ctx
     part = heads * HEAD_DIM
     capacity = rows * TOP // n_exp + max(1, rows * TOP // (16 * n_exp))
-    sel = selection(n_exp, capacity)
+    slots = part_rows(n_exp, capacity)
     section = lax.axis_index("section")
     ctx = lax.axis_index("ctx")
     first = section == 0
@@ -1067,24 +1279,11 @@
     columns = jnp.concatenate([columns, small_rows], 1)
     columns = jnp.pad(columns, ((0, 0), (0, 15 - own_rows), (0, 0)))
     out_rows = jnp.pad(out_weight[0], ((0, 16 - own_rows), (0, 0)))
-    w_qkv_both, w_out_both, small_both, w_in_both, w_back_both = gather_weights(
+    w_qkv, w_out, gains, routers, tables, w_in, w_back = gather_weights(
         columns, out_rows, expert_in[0, 0], expert_out[0, 0], perm, perm_out, pick
     )
+    weights = (gains, w_qkv, w_out, tables, routers, w_in, w_back)
     n_bias = BUCKETS * HEADS // (n_ctx * n_exp)
-
-    def dense(layer):
-        small = small_both[layer]
-        gain_one = small[:, :own_rows].reshape(1, width)
-        gain_two = small[:, own_rows : 2 * own_rows].reshape(1, width)
-        table = small[:, 2 * own_rows : 2 * own_rows + n_bias].reshape(BUCKETS, HEADS)
-        table = lax.dynamic_slice_in_dim(table, ctx * heads, heads, 1)
-        router = small[:, 2 * own_rows + n_bias : n_small].reshape(width, n_exp).astype(BF16)
-        return (
-            w_qkv_both[layer], w_out_both[layer], gain_one, gain_two, table, router,
-            w_in_both[layer], w_back_both[layer],
-        )
-
-    weights = [dense(0), dense(1)]
     ahead = block_order[:, None] - block_order[None, :]
     kind = jnp.repeat(jnp.where(ahead < 0, -1, jnp.minimum(ahead, 3)), SPAN, 1)
 
@@ -1094,32 +1293,14 @@
     taken = lax.ppermute(given, "section", [(0, 1), (1, 0)])
     layer_routes = (jnp.where(first, kept, taken), jnp.where(first, taken, kept))
     def forward(x, layer):
-        h, *saved = layer_forward(x, weights[layer], kind, layer_routes[layer], sel)
+        h, *saved = layer_forward(x, layer, weights, kind, layer_routes[layer], slots)
         return h, (x, *saved)
 
     def backward(g, keep, layer):
-        (
-            dx, dxb, d_gain_one, d_gain_two, d_router, pq, po, d_table,
-            d_in, d_back, g_in, g_back, gq, go
-        ) = layer_backward(
-            g, keep, weights[layer], kind, layer_routes[layer], sel, perm, perm_out
+        dx, dxb, d_small, pq, po, d_in, d_back, g_in, g_back, gq, go = layer_backward(
+            g, keep, layer, weights, kind, layer_routes[layer], slots, perm, perm_out
         )
-        d_table = jnp.repeat(jnp.sum(d_table, -1).T, 2, axis=0)
-        owner = jnp.arange(n_ctx * n_exp)[:, None]
-        d_table = jnp.where(owner % 2 == ctx // 2, d_table, 0.0)
-        even = ctx % 2 == 0
-        d_table = [jnp.where(even, d_table, 0.0), jnp.where(even, 0.0, d_table)]
-        owners = (n_ctx * n_exp, -1)
-        d_small = jnp.concatenate(
-            [d_gain_one.reshape(owners), d_gain_two.reshape(owners), *d_table,
-             d_router.reshape(owners)],
-            1,
-        )
-        d_small = jnp.pad(d_small, ((0, 0), (0, 256 - n_small)))
         return dx, dxb, (pq, gq, po, go, d_small, d_in, g_in, d_back, g_back)
-
-    def swap(x):
-        return lax.ppermute(x, "section", [(0, 1), (1, 0)])
 
     x = jnp.where(first, inputs[0, 0], inputs[1, 0])
     cot = jnp.where(first, cotangent[0, 0], cotangent[1, 0])
@@ -1128,23 +1309,17 @@
     _, dh, grads1 = backward(cot, keep1, 1)
     dx, _, grads0 = backward(dh, keep0, 0)
     pq, gq, po, go, d_small, d_in, g_in, d_back, g_back = zip(grads0, grads1)
-    pieces, out_grad, d_in, d_back = sum_at_owners(
-        pq, gq, po, go, jnp.stack(d_small), place, d_in, g_in, d_back, g_back, n_exp
+    pieces, out_grad, d_in, d_back, layer_out, input_grad = sum_at_owners(
+        pq, gq, po, go, d_small, place, d_in, g_in, d_back, g_back,
+        (h, top), (dx, dh.astype(F32)), n_exp
     )
     qkv_grad = pieces[:, :own_rows].reshape(n_ctx, own_rows, 3, part)
     qkv_grad = qkv_grad.transpose(1, 2, 0, 3).reshape(own_rows, 3 * width)
     out_grad = out_grad[:own_rows]
     small = jnp.sum(pieces[:, own_rows, :n_small], 0)
 
-    other = swap(jnp.where(first, top, h))
-    layer_out = jnp.where(
-        first, jnp.stack([h, other]), jnp.stack([other, top])
-    ).reshape(1, 2, 1, rows, width)
-    dh = dh.astype(F32)
-    other = swap(jnp.where(first, dh, dx))
-    input_grad = jnp.where(
-        first, jnp.stack([dx, other]), jnp.stack([other, dh])
-    ).reshape(1, 2, 1, rows, width)
+    layer_out = layer_out.reshape(1, 2, 1, rows, width)
+    input_grad = input_grad.reshape(1, 2, 1, rows, width)
     return (
         layer_out,
         input_grad,

time: 480 us -> 417 us (0.87)
  the two profiles are of different devices: /device:TPU:2 before, /device:TPU:5 now
where the time goes in v5:
time: 417 us; the launch traced here: 409 us
  Pallas kernels  380 us (91%)
  local copies, waits for them, and re-layouts  21.3 us (5%)
  other arithmetic  5.31 us (1%)
    pallas_call x2, Pallas kernels, layer_backward(): pl.pallas_call(functools.partial(layer_back_kernel, layer), out_shape=(sh...  168 us
    pallas_call x2, Pallas kernels, layer_forward(): pl.pallas_call(functools.partial(layer_kernel, layer), out_shape=(shape(x...  136 us
    pallas_call x1, Pallas kernels, sum_at_owners(): pl.pallas_call(owners_kernel, out_shape=(jax.ShapeDtypeStruct(quarter, F3...  39.7 us
    pallas_call x1, Pallas kernels, gather_weights(): pl.pallas_call(weights_kernel, out_shape=(jax.ShapeDtypeStruct((2, width,...  36.6 us
    unnamed x49, local copies, waits for them, and re-layouts  14.8 us
  transfers between devices with their start and end apart: 1, of which 0 were waited for; matrix products, arithmetic and copies ran while one was open for 1% of the time, Pallas kernels for 9%

profile of v5, /device:TPU:5, one launch (start us, length us, event | category | flops | bytes accessed | tf_op | source)
XLA Modules:
  0.0 409.2 jit_solution(18127248682571890368)
XLA Ops:
  0.7 0.8 fusion.11
  1.8 0.8 collective-permute-start
  2.5 0.8 reshape_squeeze.7
  3.3 0.8 fusion.3
  4.1 1.0 reshape_squeeze.6
  5.3 2.0 select_bitcast_fusion
  7.5 0.7 reshape.53.kind_ref
  8.3 1.3 copy-done.5
  9.5 1.3 copy-done.6
  10.8 36.6 %shard_map.231 = (bf16[2,768,576]{2,1,0:T(8,128)(2,1)}, bf16[2,192,768]{2,1,0:T(8,128)(2,1)S(1)}, f32[4,1,768]{2,1,0:T(1,128)S(1)}, bf16[2,768,16]{2,1,0:T(8,128...) custom-call(bf16[4,16,576]{2,1,0:T(8,128)(2,1)S(1)} %fusion.2.cols_ref, ...), custom_call_target="tpu_custom_call" | custom-call | tf_op jit(solution)/shard_map/pallas_call | solution.py:1043
  47.4 0.8 copy-done.1
  48.2 0.7 copy-done.2
  49.0 0.6 copy-done.7
  49.6 0.6 copy-done.11
  50.2 0.7 bitcast_select_fusion
  50.9 75.0 %shard_map.232 = (bf16[128,768]{1,0:T(8,128)(2,1)}, bf16[4,128,768]{2,1,0:T(8,128)(2,1)}, bf16[512,576]{1,0:T(8,128)(2,1)}, bf16[4,128,192]{2,1,0:T(8,128)(2,1)}...) custom-call(bf16[128,768]{1,0:T(8,128)(2,1)} %get-tuple-element.152., ...), custom_call_target="tpu_custom_call" | custom-call | tf_op jit(solution)/shard_map/pallas_call | solution.py:626
  125.8 60.8 %shard_map.233 = (bf16[128,768]{1,0:T(8,128)(2,1)}, bf16[4,128,768]{2,1,0:T(8,128)(2,1)}, bf16[512,576]{1,0:T(8,128)(2,1)}, bf16[4,128,192]{2,1,0:T(8,128)(2,1)}...) custom-call(bf16[128,768]{1,0:T(8,128)(2,1)} %get-tuple-element.70.x, ...), custom_call_target="tpu_custom_call" | custom-call | tf_op jit(solution)/shard_map/pallas_call | solution.py:626
  186.7 90.3 %shard_map.234 = (f32[128,768]{1,0:T(8,128)}, bf16[128,768]{1,0:T(8,128)(2,1)}, f32[64,256]{1,0:T(8,128)}, bf16[1024,576]{1,0:T(8,128)(2,1)}, bf16[256,768]{1,0:...) custom-call(bf16[128,768]{1,0:T(8,128)(2,1)} %get-tuple-element.153., ...), custom_call_target="tpu_custom_call" | custom-call | tf_op jit(solution)/shard_map/pallas_call | solution.py:792
  276.9 1.7 convert_element_type.9.dx1
  278.6 78.0 %shard_map.235 = (f32[128,768]{1,0:T(8,128)}, bf16[128,768]{1,0:T(8,128)(2,1)}, f32[64,256]{1,0:T(8,128)}, bf16[1024,576]{1,0:T(8,128)(2,1)}, bf16[256,768]{1,0:...) custom-call(bf16[128,768]{1,0:T(8,128)(2,1)} %get-tuple-element.80.g, ...), custom_call_target="tpu_custom_call" | custom-call | tf_op jit(solution)/shard_map/pallas_call | solution.py:792
  356.7 1.0 copy-done.8
  357.7 0.8 copy-done.14
  358.6 39.7 %shard_map.236 = (f32[4,16,576]{2,1,0:T(8,128)S(1)}, f32[16,768]{1,0:T(8,128)S(1)}, f32[768,768]{1,0:T(8,128)}, f32[768,768]{1,0:T(8,128)}, bf16[2,128,768]{2,1,0:T(8,128)(2,1)S(1)}, /*index=5*/f32[2,128,768]{2,1,0:T(8,128)}) custom-call(f32[64,256]{1,0:T(8,128)S(1)} %copy-done.14, f32[64,256]{1,0:T(8,128)S(1)} %copy-done.13, ...), custom_call_target="tpu_custom_call" | custom-call | tf_op jit(solution)/shard_map/pallas_call | solution.py:1173
  398.3 0.6 slice_bitcast_fusion.2
  399.6 0.7 reshape.57
  400.3 0.7 copy.50
  401.1 0.9 broadcast_in_dim_reshape.4
  402.0 0.7 copy.59
  402.7 2.1 copy.60
  404.8 1.4 copy.61
  406.2 1.1 copy-done.15
  407.3 1.4 copy.62
  (52 shorter events, 1.6 us)
Async XLA Ops:
  0.6 7.6 %copy-start.4 = (bf16[256,192]{1,0:T(8,128)(2,1)S(1)}, bf16[256,192]{1,0:T(8,128)(2,1)}, u32[]{:S(2)}) copy-start(bf16[256,192]{1,0:T(8,128)(2,1)} %constant.28.clone.perm_out_ref.perm_out_in) | copy-start | bytes 294916
  0.7 7.6 %copy-start = (bf16[1024,768]{1,0:T(8,128)(2,1)S(1)}, bf16[1024,768]{1,0:T(8,128)(2,1)}, u32[]{:S(2)}) copy-start(bf16[1024,768]{1,0:T(8,128)(2,1)} %constant.25.clone.perm_ref.perm_in) | copy-start | bytes 4718596
  0.7 7.6 %copy-start.12 = (bf16[64,1024]{1,0:T(8,128)(2,1)S(1)}, bf16[64,1024]{1,0:T(8,128)(2,1)}, u32[]{:S(2)}) copy-start(bf16[64,1024]{1,0:T(8,128)(2,1)} %constant.26.clone.pick_ref) | copy-start | bytes 393220
  0.7 6.6 %copy-start.19 = (bf16[1,12]{1,0:T(2,128)(2,1)S(1)}, bf16[1,12]{1,0:T(2,128)(2,1)}, u32[]{:S(2)}) copy-start(bf16[1,12]{1,0:T(2,128)(2,1)} %param.24) | copy-start | bytes 76
  0.7 6.6 %copy-start.18 = (bf16[1,6]{1,0:T(2,128)(2,1)S(1)}, bf16[1,6]{1,0:T(2,128)(2,1)}, u32[]{:S(2)}) copy-start(bf16[1,6]{1,0:T(2,128)(2,1)} %param.23) | copy-start | bytes 40
  0.7 6.6 %copy-start.20 = (bf16[1,12]{1,0:T(2,128)(2,1)S(1)}, bf16[1,12]{1,0:T(2,128)(2,1)}, u32[]{:S(2)}) copy-start(bf16[1,12]{1,0:T(2,128)(2,1)} %param.20) | copy-start | bytes 76
  0.7 7.5 %copy-start.17 = (bf16[1,12,768]{2,1,0:T(8,128)(2,1)S(1)}, bf16[1,12,768]{2,1,0:T(8,128)(2,1)}, u32[]{:S(2)}) copy-start(bf16[1,12,768]{2,1,0:T(8,128)(2,1)} %param.22) | copy-start | bytes 55300
  1.8 48.4 %collective-permute-start = (s32[128,2]{1,0:T(8,128)S(1)}, s32[128,2]{1,0:T(8,128)S(1)}, u32[]{:S(2)}, u32[]{:S(2)}) collective-permute-start(s32[128,2]{1,0:T(8,128)S(1)} %select_bitcast_fusion.2), channel_id=1, source_target_pairs={{0,64},{64,0},{1,65},{65,1},{2,66},{66,2},{3,67},{67,3},{4,68},{68... | collective-permute-start | bytes 3080 | tf_op jit(solution)/shard_map/ppermute | solution.py:1293
  8.3 1.3 copy-start.5
  9.5 1.3 copy-start.6
  47.4 0.8 copy-start.1
  48.2 0.7 copy-start.2
  49.0 0.6 copy-start.7
  49.6 0.6 copy-start.11
  278.6 78.1 %copy-start.3 = (bf16[128,768]{1,0:T(8,128)(2,1)S(1)}, bf16[128,768]{1,0:T(8,128)(2,1)}, u32[]{:S(2)}) copy-start(bf16[128,768]{1,0:T(8,128)(2,1)} %get-tuple-element.70.x_ref.y0) | copy-start | bytes 589828
  278.6 78.1 %copy-start.9 = (bf16[1024,64]{1,0:T(8,128)(2,1)S(1)}, bf16[1024,64]{1,0:T(8,128)(2,1)}, u32[]{:S(2)}) copy-start(bf16[1024,64]{1,0:T(8,128)(2,1)} %constant.27.clone.spread_ref) | copy-start | bytes 393220
  278.6 78.1 %copy-start.10 = (bf16[128,768]{1,0:T(8,128)(2,1)S(1)}, bf16[128,768]{1,0:T(8,128)(2,1)}, u32[]{:S(2)}) copy-start(bf16[128,768]{1,0:T(8,128)(2,1)} %get-tuple-element.92.y1) | copy-start | bytes 589828
  278.6 78.1 %copy-start.13 = (f32[64,256]{1,0:T(8,128)S(1)}, f32[64,256]{1,0:T(8,128)}, u32[]{:S(2)}) copy-start(f32[64,256]{1,0:T(8,128)} %get-tuple-element.91.small1) | copy-start | bytes 196612
  356.7 1.0 copy-start.8
  357.7 0.8 copy-start.14
  398.3 6.5 %copy-start.16 = (f32[768,768]{1,0:T(8,128)S(1)}, f32[768,768]{1,0:T(8,128)}, u32[]{:S(2)}) copy-start(f32[768,768]{1,0:T(8,128)} %get-tuple-element.114) | copy-start | bytes 7077892
  404.8 2.5 copy-start.15

commit v6 on v5

--- a/solution.py
+++ b/solution.py
@@ -261,8 +261,8 @@
         pl.semaphore_signal(barrier, inc=1, device_id={"ctx": neighbour}, device_id_type=MESH)
     if partner is not None:
         pl.semaphore_signal(barrier, inc=1, device_id={"section": partner}, device_id_type=MESH)
-    pl.semaphore_wait(barrier, count + (1 if partner is None else 2))
-    return ctx, right, left
+    greeted = count + (1 if partner is None else 2)
+    return (ctx, right, left), lambda: pl.semaphore_wait(barrier, greeted)
 
 
 def run_experts(ids, outs, all_ref, rets, block, done, beside, scratch):
@@ -431,7 +431,7 @@
 
 
 def attend(
-    ids, x, gain_ref, w_qkv, w_out, table_ref, kind_ref, all_ref, proj_ref, att_ref,
+    ids, wait_all_here, x, gain_ref, w_qkv, w_out, table_ref, kind_ref, all_ref, proj_ref, att_ref,
     tiles_ref, s_ref, p_ref, part, scratch
 ):
     bufs, (s_ag, r_ag, s_rs, r_rs) = scratch[:6], scratch[6:]
@@ -442,6 +442,7 @@
     heads = w_out.shape[0] // HEAD_DIM
     all_ref[me] = norm(x, gain_ref[...])
     gather = RingGather(all_ref, rows, ids, s_ag, r_ag)
+    wait_all_here()
     gather.start()
     make_tiles(table_ref, tiles_ref, heads)
     gather.forward()
@@ -572,11 +573,11 @@
     gain_one, gain_two = gains.at[2 * layer], gains.at[2 * layer + 1]
     w_qkv, w_out = w_qkv_both.at[layer], w_out_both.at[layer]
     table_ref, router_ref = tables.at[layer], routers.at[layer]
-    ids = meet_all()
+    ids, wait_all_here = meet_all()
     rows, width = x_ref.shape
     x = x_ref[...].astype(F32)
     branch = attend(
-        ids, x, gain_one, w_qkv, w_out, table_ref, kind_ref, all_ref, proj_ref, att_ref,
+        ids, wait_all_here, x, gain_one, w_qkv, w_out, table_ref, kind_ref, all_ref, proj_ref, att_ref,
         tiles_ref, s_ref, p_ref, part, scratch[14:24]
     )
     middle = x + branch
@@ -689,7 +690,7 @@
     w_qkv, w_out = w_qkv_both.at[layer], w_out_both.at[layer]
     table_ref, router_ref = tables.at[layer], routers.at[layer]
     partner = 1 - lax.axis_index("section")
-    ids = meet_all(partner)
+    ids, wait_all_here = meet_all(partner)
     rows, width = x_ref.shape
 
     def across(k, src, dst):
@@ -708,6 +709,7 @@
         slots[1], (gates[1] * g).astype(BF16)
     )
     set_slots(*outs, dreturned)
+    wait_all_here()
 
     def logits_back():
         g = g_ref[...].astype(F32)
@@ -794,7 +796,7 @@
         out_shape=(
             shape(x.shape, F32),
             shape(x.shape, BF16),
-            shape((perm.shape[0] // 16, SMALL), F32),
+            shape((perm.shape[0] // OWN, SMALL), F32),
             pq,
             po,
             shape(w_shape, F32),
@@ -955,7 +957,7 @@
 
 
 def weights_kernel(
-    cols_ref, outp_ref, w_in, w_back, perm_ref, perm_out_ref, pick_ref,
+    cols_ref, outp_ref, w_in, w_back, perm_ref, perm_out_ref, pick_ref, fill_ref, fill_small_ref,
     w_qkv, w_out, gains, routers, tables, both_in, both_back,
     zin, grid, grid_out, s_z, r_z, s_q, r_q, s_o, r_o, s_fq, r_fq, s_fo, r_fo, s_x, r_x, s_own
 ):
@@ -966,12 +968,12 @@
     turn = ctx_exchange(cols_ref, zin, s_z, r_z)
     for c in turn:
         c.start()
+    w_in, w_back = w_in.at[0, 0], w_back.at[0, 0]
     cross_in = remote(w_in, both_in.at[section], s_x, r_x, 0, "section", partner)
     cross_back = remote(w_back, both_back.at[section], s_x, r_x, 1, "section", partner)
     cross_in.start()
     cross_back.start()
     zin[ctx] = cols_ref[ctx]
-    grid_out[section, exp] = outp_ref[...]
 
     def spread(ref, send, recv, k):
         peer = lax.rem(exp + k, count)
@@ -989,13 +991,17 @@
 
         lax.fori_loop(first, count, body, 0)
 
-    each(lambda k: spread(grid_out, s_o, r_o, k).start())
     for c in turn:
         c.wait_recv()
-    grid[section, exp] = zin[...].reshape(grid.shape[2:])
+    came = zin[...].reshape(zin.shape[0] * zin.shape[1], zin.shape[2])
+    small = mm(fill_small_ref[...], came[:, :SMALL]).astype(BF16)
+    outp = outp_ref[...]
+    grid_out[section, exp] = jnp.concatenate([outp[:, :SMALL] + small, outp[:, SMALL:]], 1)
+    each(lambda k: spread(grid_out, s_o, r_o, k).start())
+    grid[section, exp] = mm(fill_ref[...], came).astype(BF16)
     each(lambda k: spread(grid, s_q, r_q, k).start())
+    forward(grid_out, s_fo, r_fo, 0).start()
     forward(grid, s_fq, r_fq, 0).start()
-    forward(grid_out, s_fo, r_fo, 0).start()
     own_in = pltpu.make_async_copy(w_in, both_in.at[section], s_own.at[0])
     own_back = pltpu.make_async_copy(w_back, both_back.at[section], s_own.at[1])
     own_in.start()
@@ -1009,15 +1015,15 @@
     each(lambda k: relay(grid, s_q, r_q, s_fq, r_fq, k))
 
     def unpack(layer):
-        flat = grid[layer].reshape(perm_ref.shape[0], grid.shape[3])
-        w_qkv[layer] = mm_tn(perm_ref[...], flat).astype(BF16)
+        flat = grid[layer].reshape(perm_ref.shape[1], grid.shape[3])
+        w_qkv[layer] = mm(perm_ref[...], flat).astype(BF16)
+        flat = grid_out[layer].reshape(perm_out_ref.shape[1], grid_out.shape[3])
+        w_out[layer] = mm(perm_out_ref[...], flat).astype(BF16)
         small = mm(pick_ref[...], flat[:, :SMALL])
         two, routers[layer], tables[layer] = unpack_small(
             small, routers.shape[1], routers.shape[2], tables.shape[2]
         )
         gains[2 * layer], gains[2 * layer + 1] = two
-        flat = grid_out[layer].reshape(perm_out_ref.shape[0], grid_out.shape[3])
-        w_out[layer] = mm_tn(perm_out_ref[...], flat).astype(BF16)
 
     unpack(section)
     each(lambda k: forward(grid_out, s_fo, r_fo, k).wait_recv(), 0)
@@ -1035,34 +1041,34 @@
     cross_back.wait()
 
 
-def gather_weights(cols, outp, w_in, w_back, perm, perm_out, pick):
+def gather_weights(cols, outp, w_in, w_back, perm, perm_out, pick, fill, fill_small):
     width, part = outp.shape[1], cols.shape[2]
-    count = perm_out.shape[0] // 16
+    count = perm_out.shape[1] // TILE
     vm, far = pl.BlockSpec(memory_space=pltpu.VMEM), pl.BlockSpec(memory_space=pl.ANY)
     dma = lambda n: pltpu.SemaphoreType.DMA((n,))
     return pl.pallas_call(
         weights_kernel,
         out_shape=(
             jax.ShapeDtypeStruct((2, width, part), BF16),
-            jax.ShapeDtypeStruct((2, perm_out.shape[1], width), BF16),
+            jax.ShapeDtypeStruct((2, perm_out.shape[0], width), BF16),
             jax.ShapeDtypeStruct((4, 1, width), F32),
             jax.ShapeDtypeStruct((2, width, count), BF16),
             jax.ShapeDtypeStruct((2, BUCKETS, part // (3 * HEAD_DIM)), F32),
-            jax.ShapeDtypeStruct((2, *w_in.shape), BF16),
-            jax.ShapeDtypeStruct((2, *w_back.shape), BF16),
+            jax.ShapeDtypeStruct((2, *w_in.shape[2:]), BF16),
+            jax.ShapeDtypeStruct((2, *w_back.shape[2:]), BF16),
         ),
-        in_specs=[vm] * 2 + [far] * 2 + [vm] * 3,
+        in_specs=[vm] * 2 + [far] * 2 + [vm] * 5,
         out_specs=(vm,) * 5 + (far,) * 2,
         scratch_shapes=[
             pltpu.VMEM(cols.shape, BF16),
-            pltpu.VMEM((2, count, 64, part), BF16),
+            pltpu.VMEM((2, count, fill.shape[0], part), BF16),
             pltpu.VMEM((2, count, 16, width), BF16),
             dma(4), dma(4), *[dma(count)] * 8, dma(2), dma(2), dma(2),
         ],
         compiler_params=pltpu.CompilerParams(
             collective_id=4, has_side_effects=True, vmem_limit_bytes=48 << 20
         ),
-    )(cols, outp, w_in, w_back, perm, perm_out, pick)
+    )(cols, outp, w_in, w_back, perm, perm_out, pick, fill, fill_small)
 
 
 def owners_kernel(
@@ -1109,17 +1115,16 @@
         return a[...].astype(F32) + b[...].astype(F32)
 
     loaded(2, 3)
-    dense = both(pq, gq)
+    pieces[...] = both(pq, gq).astype(BF16).reshape(pieces.shape)
+    swap = exchange_out(pieces, box, s_q, r_q)
+    swap.start()
+    loaded(0, 1)
+    dense = both(po, go)
     cross[0].wait_recv()
     small = jnp.where(first, small0[...], small1[...]) + got_small[...]
     wide = mm(spread_ref[...], small.astype(BF16))
-    n = wide.shape[1]
-    dense = jnp.concatenate([dense[:, :n] + wide, dense[:, n:]], 1)
-    pieces[...] = dense.astype(BF16).reshape(pieces.shape)
-    swap = exchange_out(pieces, box, s_q, r_q)
-    swap.start()
-    loaded(0, 1)
-    pieces_out[...] = both(po, go).astype(BF16).reshape(pieces_out.shape)
+    dense = jnp.concatenate([dense[:, :SMALL] + wide, dense[:, SMALL:]], 1)
+    pieces_out[...] = dense.astype(BF16).reshape(pieces_out.shape)
     swap_out = exchange_out(pieces_out, box_out, s_o, r_o)
     swap_out.start()
     box[0] = pieces[exp]
@@ -1133,24 +1138,28 @@
     saves = Loads(save_sems)
     loaded(4, 5)
     d_in[...] += gin[...].astype(F32)
-    saves.start(d_in, d_in_out)
+    saves.start(d_in, d_in_out.at[0, 0])
     loaded(6, 7)
     d_back[...] += gback[...].astype(F32)
-    saves.start(d_back, d_back_out)
+    saves.start(d_back, d_back_out.at[0, 0])
     swap.wait_recv()
     total = box[0].astype(F32)
     for k in range(1, box.shape[0]):
         total = total + box[k].astype(F32)
-    summed[...] = total.reshape(summed.shape)
-    turn = ctx_exchange(summed, turned, s_z, r_z)
-    for c in turn:
-        c.start()
-    turned[ctx] = summed[ctx]
+    summed[...] = jnp.zeros(summed.shape, F32)
+    for c in range(4):
+        summed[c, :OWN, :] = total[c * OWN : (c + 1) * OWN]
     swap_out.wait_recv()
     total = box_out[0].astype(F32)
     for k in range(1, box_out.shape[0]):
         total = total + box_out[k].astype(F32)
     out_grad[...] = total
+    for c in range(4):
+        summed[c, OWN : OWN + 1, :SMALL] = total[OWN + c : OWN + c + 1, :SMALL]
+    turn = ctx_exchange(summed, turned, s_z, r_z)
+    for c in turn:
+        c.start()
+    turned[ctx] = summed[ctx]
     for c in turn:
         c.wait()
     cross[0].wait_send()
@@ -1168,15 +1177,15 @@
     dma = lambda n: pltpu.SemaphoreType.DMA((n,))
     own = (rows // count, part)
     own_out = (out_rows // count, width)
-    quarter = (4, rows // count // 4, part)
+    quarter = (4, TILE, part)
     held = [a[0] for a in (pq, gq, po, go, d_in, g_in, d_back, g_back)]
     return pl.pallas_call(
         owners_kernel,
         out_shape=(
             jax.ShapeDtypeStruct(quarter, F32),
             jax.ShapeDtypeStruct(own_out, F32),
-            jax.ShapeDtypeStruct(d_in[0].shape, F32),
-            jax.ShapeDtypeStruct(d_back[0].shape, F32),
+            jax.ShapeDtypeStruct((1, 1, *d_in[0].shape), F32),
+            jax.ShapeDtypeStruct((1, 1, *d_back[0].shape), F32),
             jax.ShapeDtypeStruct((2, *y[0].shape), BF16),
             jax.ShapeDtypeStruct((2, *dx[0].shape), F32),
         ),
@@ -1203,20 +1212,30 @@
 
 def packing(n_ctx, n_exp, own_rows):
     blocks = n_ctx * n_exp
-    perm = np.zeros((blocks, 16, blocks, own_rows), np.float32)
-    pick = np.zeros((blocks, blocks, 16), np.float32)
-    perm_out = np.zeros((n_exp, 16, n_exp, own_rows), np.float32)
+    perm = np.zeros((blocks, own_rows, blocks, own_rows), np.float32)
+    pick = np.zeros((blocks, n_exp, TILE), np.float32)
+    perm_out = np.zeros((n_exp, TILE, n_exp, own_rows), np.float32)
+    fill = np.zeros((n_ctx, own_rows, n_ctx, TILE), np.float32)
+    fill_small = np.zeros((TILE, n_ctx, TILE), np.float32)
+    for c in range(n_ctx):
+        fill_small[own_rows + c, c, own_rows] = 1
+        for i in range(own_rows):
+            fill[c, i, c, i] = 1
     for e in range(n_exp):
         for i in range(own_rows):
             perm_out[e, i, e, i] = 1
         for c in range(n_ctx):
             for i in range(own_rows):
                 perm[e * n_ctx + c, i, c * n_exp + e, i] = 1
-            pick[c * n_exp + e, e * n_ctx + c, own_rows] = 1
-    perm = perm.reshape(blocks * 16, blocks * own_rows)
-    pick = pick.reshape(blocks, blocks * 16)
-    perm_out = perm_out.reshape(n_exp * 16, n_exp * own_rows)
-    return tuple(jnp.asarray(m, BF16) for m in (perm, pick, pick.T.copy(), perm_out))
+            pick[c * n_exp + e, e, own_rows + c] = 1
+    perm = perm.reshape(blocks * own_rows, blocks * own_rows)
+    pick = pick.reshape(blocks, n_exp * TILE)
+    perm_out = perm_out.reshape(n_exp * TILE, n_exp * own_rows)
+    fill = fill.reshape(n_ctx * own_rows, n_ctx * TILE)
+    fill_small = fill_small.reshape(TILE, n_ctx * TILE)
+    pack = (perm, perm_out, pick.T.copy())
+    unpack = (perm.T.copy(), perm_out.T.copy(), pick, fill, fill_small)
+    return tuple(tuple(jnp.asarray(m, BF16) for m in ms) for ms in (pack, unpack))
 
 
 def norm_scale(v):
@@ -1267,7 +1286,7 @@
     ctx = lax.axis_index("ctx")
     first = section == 0
 
-    perm, pick, place, perm_out = packing(n_ctx, n_exp, own_rows)
+    (perm, perm_out, place), unpack = packing(n_ctx, n_exp, own_rows)
     small = jnp.concatenate(
         [attn_gain[0], moe_gain[0], rel_bias[0], router_weight[0].reshape(-1)]
     )
@@ -1280,7 +1299,7 @@
     columns = jnp.pad(columns, ((0, 0), (0, 15 - own_rows), (0, 0)))
     out_rows = jnp.pad(out_weight[0], ((0, 16 - own_rows), (0, 0)))
     w_qkv, w_out, gains, routers, tables, w_in, w_back = gather_weights(
-        columns, out_rows, expert_in[0, 0], expert_out[0, 0], perm, perm_out, pick
+        columns, out_rows, expert_in, expert_out, *unpack
     )
     weights = (gains, w_qkv, w_out, tables, routers, w_in, w_back)
     n_bias = BUCKETS * HEADS // (n_ctx * n_exp)
@@ -1329,8 +1348,8 @@
         small[2 * own_rows : 2 * own_rows + n_bias][None],
         small[own_rows : 2 * own_rows][None],
         small[2 * own_rows + n_bias :].reshape(1, own_rows, n_exp),
-        d_in[None, None],
-        d_back[None, None],
+        d_in,
+        d_back,
     )
 
 

time: 417 us -> 394 us (0.945)
  the two profiles are of different devices: /device:TPU:5 before, /device:TPU:2 now
where the time goes in v6:
time: 394 us; the launch traced here: 386 us
  Pallas kernels  359 us (91%)
  local copies, waits for them, and re-layouts  20.8 us (5%)
  other arithmetic  5.26 us (1%)
    pallas_call x2, Pallas kernels, layer_backward(): pl.pallas_call(functools.partial(layer_back_kernel, layer), out_shape=(sh...  154 us
    pallas_call x2, Pallas kernels, layer_forward(): pl.pallas_call(functools.partial(layer_kernel, layer), out_shape=(shape(x...  142 us
    pallas_call x1, Pallas kernels, gather_weights(): pl.pallas_call(weights_kernel, out_shape=(jax.ShapeDtypeStruct((2, width,...  36.3 us
    pallas_call x1, Pallas kernels, sum_at_owners(): pl.pallas_call(owners_kernel, out_shape=(jax.ShapeDtypeStruct(quarter, F3...  26.7 us
    unnamed x45, local copies, waits for them, and re-layouts  13.5 us
  transfers between devices with their start and end apart: 1, of which 0 were waited for; matrix products, arithmetic and copies ran while one was open for 2% of the time, Pallas kernels for 9%

profile of v6, /device:TPU:2, one launch (start us, length us, event | category | flops | bytes accessed | tf_op | source)
XLA Modules:
  0.0 386.5 jit_solution(13104382002008225897)
XLA Ops:
  0.7 0.8 fusion.11
  1.9 0.8 reshape_squeeze.7
  2.7 0.8 fusion.3
  3.5 1.0 reshape_squeeze.6
  4.7 2.0 select_bitcast_fusion
  6.7 0.8 fusion.10
  7.6 0.7 reshape.53.kind_ref
  8.3 0.7 pad.14.outp_ref
  9.1 1.3 copy-done.5
  10.3 36.3 %shard_map.267 = (bf16[2,768,576]{2,1,0:T(8,128)(2,1)}, bf16[2,192,768]{2,1,0:T(8,128)(2,1)S(1)}, f32[4,1,768]{2,1,0:T(1,128)S(1)}, bf16[2,768,16]{2,1,0:T(8,128...) custom-call(bf16[4,16,576]{2,1,0:T(8,128)(2,1)S(1)} %fusion.2.cols_ref, ...), custom_call_target="tpu_custom_call" | custom-call | tf_op jit(solution)/shard_map/pallas_call | solution.py:1049
  46.7 0.8 copy-done
  47.5 0.7 copy-done.1
  48.2 0.6 copy-done.6
  48.8 0.6 copy-done.9
  49.4 0.7 bitcast_select_fusion
  50.1 72.4 %shard_map.268 = (bf16[128,768]{1,0:T(8,128)(2,1)}, bf16[4,128,768]{2,1,0:T(8,128)(2,1)}, bf16[512,576]{1,0:T(8,128)(2,1)}, bf16[4,128,192]{2,1,0:T(8,128)(2,1)}...) custom-call(bf16[128,768]{1,0:T(8,128)(2,1)} %get-tuple-element.152., ...), custom_call_target="tpu_custom_call" | custom-call | tf_op jit(solution)/shard_map/pallas_call | solution.py:627
  122.5 69.5 %shard_map.269 = (bf16[128,768]{1,0:T(8,128)(2,1)}, bf16[4,128,768]{2,1,0:T(8,128)(2,1)}, bf16[512,576]{1,0:T(8,128)(2,1)}, bf16[4,128,192]{2,1,0:T(8,128)(2,1)}...) custom-call(bf16[128,768]{1,0:T(8,128)(2,1)} %get-tuple-element.70.x, ...), custom_call_target="tpu_custom_call" | custom-call | tf_op jit(solution)/shard_map/pallas_call | solution.py:627
  192.0 76.8 %shard_map.270 = (f32[128,768]{1,0:T(8,128)}, bf16[128,768]{1,0:T(8,128)(2,1)}, f32[64,256]{1,0:T(8,128)}, bf16[768,576]{1,0:T(8,128)(2,1)}, bf16[256,768]{1,0:T...) custom-call(bf16[128,768]{1,0:T(8,128)(2,1)} %get-tuple-element.153., ...), custom_call_target="tpu_custom_call" | custom-call | tf_op jit(solution)/shard_map/pallas_call | solution.py:794
  268.9 1.0 convert_element_type.9.dx1
  269.9 77.1 %shard_map.271 = (f32[128,768]{1,0:T(8,128)}, bf16[128,768]{1,0:T(8,128)(2,1)}, f32[64,256]{1,0:T(8,128)}, bf16[768,576]{1,0:T(8,128)(2,1)}, bf16[256,768]{1,0:T...) custom-call(bf16[128,768]{1,0:T(8,128)(2,1)} %get-tuple-element.80.g, ...), custom_call_target="tpu_custom_call" | custom-call | tf_op jit(solution)/shard_map/pallas_call | solution.py:794
  347.0 1.0 copy-done.7
  348.0 0.8 copy-done.13
  348.8 26.7 %shard_map.272 = (f32[4,16,576]{2,1,0:T(8,128)S(1)}, f32[16,768]{1,0:T(8,128)S(1)}, f32[1,1,768,768]{3,2,1,0:T(8,128)}, f32[1,1,768,768]{3,2,1,0:T(8,128)}, bf16...) custom-call(f32[64,256]{1,0:T(8,128)S(1)} %copy-done.13, f32[64,256]{1,0:T(8,128)S(1)} %copy-done.12, ...), custom_call_target="tpu_custom_call" | custom-call | tf_op jit(solution)/shard_map/pallas_call | solution.py:1182
  375.6 0.6 slice_bitcast_fusion.2
  376.8 0.7 reshape.57
  377.5 0.7 copy.54
  378.4 0.9 broadcast_in_dim_reshape.4
  379.3 0.7 copy.63
  380.0 2.1 copy.64
  382.1 1.4 copy.65
  383.5 1.1 copy-done.17
  384.6 1.4 copy.66
  (48 shorter events, 1.6 us)
Async XLA Ops:
  0.6 8.4 %copy-start.16 = (bf16[16,64]{1,0:T(8,128)(2,1)S(1)}, bf16[16,64]{1,0:T(8,128)(2,1)}, u32[]{:S(2)}) copy-start(bf16[16,64]{1,0:T(8,128)(2,1)} %constant.40.clone.fill_small_ref) | copy-start | bytes 6148
  0.7 8.3 %copy-start.15 = (bf16[48,64]{1,0:T(8,128)(2,1)S(1)}, bf16[48,64]{1,0:T(8,128)(2,1)}, u32[]{:S(2)}) copy-start(bf16[48,64]{1,0:T(8,128)(2,1)} %constant.39.clone.fill_ref) | copy-start | bytes 18436
  0.7 8.3 %copy-start.14 = (bf16[64,256]{1,0:T(8,128)(2,1)S(1)}, bf16[64,256]{1,0:T(8,128)(2,1)}, u32[]{:S(2)}) copy-start(bf16[64,256]{1,0:T(8,128)(2,1)} %constant.38.clone.pick_ref) | copy-start | bytes 98308
  0.7 8.3 %copy-start.10 = (bf16[192,256]{1,0:T(8,128)(2,1)S(1)}, bf16[192,256]{1,0:T(8,128)(2,1)}, u32[]{:S(2)}) copy-start(bf16[192,256]{1,0:T(8,128)(2,1)} %constant.37.clone.perm_out_ref) | copy-start | bytes 294916
  0.7 8.3 %copy-start.4 = (bf16[1,1,768,768]{3,2,1,0:T(8,128)(2,1)S(1)}, bf16[1,1,768,768]{3,2,1,0:T(8,128)(2,1)}, u32[]{:S(2)}) copy-start(bf16[1,1,768,768]{3,2,1,0:T(8,128)(2,1)} %w_back.1) | copy-start | bytes 3538948
  0.7 8.3 %copy-start.3 = (bf16[1,1,768,768]{3,2,1,0:T(8,128)(2,1)S(1)}, bf16[1,1,768,768]{3,2,1,0:T(8,128)(2,1)}, u32[]{:S(2)}) copy-start(bf16[1,1,768,768]{3,2,1,0:T(8,128)(2,1)} %w_in.1) | copy-start | bytes 3538948
  1.8 47.6 %collective-permute-start = (s32[128,2]{1,0:T(8,128)S(1)}, s32[128,2]{1,0:T(8,128)S(1)}, u32[]{:S(2)}, u32[]{:S(2)}) collective-permute-start(s32[128,2]{1,0:T(8,128)S(1)} %select_bitcast_fusion.2), channel_id=1, source_target_pairs={{0,64},{64,0},{1,65},{65,1},{2,66},{66,2},{3,67},{67,3},{4,68},{68... | collective-permute-start | bytes 3080 | tf_op jit(solution)/shard_map/ppermute | solution.py:1312
  9.0 1.3 copy-start.5
  46.6 0.8 copy-start
  47.5 0.7 copy-start.1
  48.2 0.6 copy-start.6
  48.8 0.6 copy-start.9
  269.8 77.1 %copy-start.2 = (bf16[128,768]{1,0:T(8,128)(2,1)S(1)}, bf16[128,768]{1,0:T(8,128)(2,1)}, u32[]{:S(2)}) copy-start(bf16[128,768]{1,0:T(8,128)(2,1)} %get-tuple-element.70.x_ref.y0) | copy-start | bytes 589828
  269.8 77.1 %copy-start.8 = (bf16[128,768]{1,0:T(8,128)(2,1)S(1)}, bf16[128,768]{1,0:T(8,128)(2,1)}, u32[]{:S(2)}) copy-start(bf16[128,768]{1,0:T(8,128)(2,1)} %get-tuple-element.92.y1) | copy-start | bytes 589828
  269.8 77.1 %copy-start.11 = (bf16[256,64]{1,0:T(8,128)(2,1)S(1)}, bf16[256,64]{1,0:T(8,128)(2,1)}, u32[]{:S(2)}) copy-start(bf16[256,64]{1,0:T(8,128)(2,1)} %constant.35.clone.spread_ref) | copy-start | bytes 98308
  269.8 77.1 %copy-start.12 = (f32[64,256]{1,0:T(8,128)S(1)}, f32[64,256]{1,0:T(8,128)}, u32[]{:S(2)}) copy-start(f32[64,256]{1,0:T(8,128)} %get-tuple-element.91.small1) | copy-start | bytes 196612
  347.0 1.0 copy-start.7
  348.0 0.8 copy-start.13
  375.6 6.5 %copy-start.18 = (f32[1,1,768,768]{3,2,1,0:T(8,128)S(1)}, f32[1,1,768,768]{3,2,1,0:T(8,128)}, u32[]{:S(2)}) copy-start(f32[1,1,768,768]{3,2,1,0:T(8,128)} %get-tuple-element.172) | copy-start | bytes 7077892
  382.1 2.5 copy-start.17

commit v7 on v6

--- a/solution.py
+++ b/solution.py
@@ -314,9 +314,10 @@
         block(n, far, part)
         scatters[n].send_far()
         done(n)
+        if n:
+            scatters[n - 1].send_sums()
     beside[1]()
-    for n in range(parts):
-        scatters[n].send_sums()
+    scatters[-1].send_sums()
     beside[2]()
     for n in range(parts):
         total = scatters[n].total().astype(BF16)
@@ -432,7 +433,7 @@
 
 def attend(
     ids, wait_all_here, x, gain_ref, w_qkv, w_out, table_ref, kind_ref, all_ref, proj_ref, att_ref,
-    tiles_ref, s_ref, p_ref, part, scratch
+    tiles_ref, s_ref, p_ref, part, scratch, weights_here
 ):
     bufs, (s_ag, r_ag, s_rs, r_rs) = scratch[:6], scratch[6:]
     me, right, left = ids
@@ -449,6 +450,7 @@
     gather.wait_left()
     gather.wait_right()
     gather.wait_far()
+    weights_here()
     proj_ref[...] = mm(all_ref[...].reshape(seq, width), w_qkv[...]).astype(BF16)
     parts = []
     for h in range(heads):
@@ -559,27 +561,39 @@
     return total
 
 
+def own_stream(ref):
+    return ref.at[lax.axis_index("section"), 0] if len(ref.shape) == 4 else ref
+
+
 def layer_kernel(
-    layer, x_ref, gains, w_qkv_both, w_out_both, tables, kind_ref, routers, routes_ref,
-    w_in_both, w_back_both,
-    h_ref, all_ref, proj_ref, att_ref, middle_ref, mixed_ref, logits_ref, picked_ref,
-    ent_out, pre_out, *scratch
+    layer, gains, tables, kind_ref, routers, routes_ref,
+    x_in, w_qkv_both, w_out_both, w_in_both, w_back_both,
+    h_ref, middle_ref, mixed_ref, logits_ref, picked_ref,
+    all_out, proj_out, att_out, ent_out, pre_out, *scratch
 ):
     tiles_ref, s_ref, p_ref, part, w_in, w_back, ent_ref, pre_ref, sems, save_sems = scratch[:10]
     outs, rets = scratch[10:12], scratch[12:14]
+    w_qkv, w_out, all_ref, proj_ref, att_ref, x_ref = scratch[14:20]
+    scratch = scratch[:14] + scratch[20:]
     loads, saves = Loads(sems), Loads(save_sems)
+    loads.start(own_stream(x_in), x_ref)
+    loads.start(w_qkv_both.at[layer], w_qkv)
+    loads.start(w_out_both.at[layer], w_out)
     loads.start(w_in_both.at[layer], w_in)
     loads.start(w_back_both.at[layer], w_back)
     gain_one, gain_two = gains.at[2 * layer], gains.at[2 * layer + 1]
-    w_qkv, w_out = w_qkv_both.at[layer], w_out_both.at[layer]
     table_ref, router_ref = tables.at[layer], routers.at[layer]
     ids, wait_all_here = meet_all()
     rows, width = x_ref.shape
+    loads.wait(0)
     x = x_ref[...].astype(F32)
     branch = attend(
         ids, wait_all_here, x, gain_one, w_qkv, w_out, table_ref, kind_ref, all_ref, proj_ref, att_ref,
-        tiles_ref, s_ref, p_ref, part, scratch[14:24]
+        tiles_ref, s_ref, p_ref, part, scratch[14:24], lambda: loads.wait(1, 2)
     )
+    saves.start(all_ref, all_out)
+    saves.start(proj_ref, proj_out)
+    saves.start(att_ref, att_out)
     middle = x + branch
     middle_ref[...] = middle
     mixed = norm(middle, gain_two[...])
@@ -595,7 +609,7 @@
 
     def find_logits():
         logits_ref[...] = mm(mixed_ref[...], router_ref[...])
-        loads.wait_all()
+        loads.wait(3, 4)
 
     def save(n):
         saves.start(ent_ref.at[n], ent_out.at[n])
@@ -619,7 +633,7 @@
 
 def layer_forward(x, layer, weights, kind, routes, slots):
     gains, w_qkv, w_out, table, router, w_in, w_back = weights
-    rows, width = x.shape
+    rows, width = x.shape[-2:]
     seq, part, experts = 4 * rows, w_out.shape[1], router.shape[2]
     heads = part // HEAD_DIM
     vm, far = pl.BlockSpec(memory_space=pltpu.VMEM), pl.BlockSpec(memory_space=pl.ANY)
@@ -627,19 +641,19 @@
     return pl.pallas_call(
         functools.partial(layer_kernel, layer),
         out_shape=(
-            shape(x.shape, BF16),
+            shape((rows, width), BF16),
+            shape((rows, width), F32),
+            shape((rows, width), BF16),
+            shape((rows, experts), F32),
+            shape((TOP, rows, width), BF16),
             shape((4, rows, width), BF16),
             shape((seq, 3 * part), BF16),
             shape((4, rows, part), BF16),
-            shape(x.shape, F32),
-            shape(x.shape, BF16),
-            shape((rows, experts), F32),
-            shape((TOP, rows, width), BF16),
             shape((PARTS, 4, slots, width), BF16),
             shape((PARTS, 4, slots, w_in.shape[2]), F32),
         ),
-        in_specs=[vm] * 8 + [far] * 2,
-        out_specs=(vm,) * 8 + (far,) * 2,
+        in_specs=[vm] * 5 + [far] * 5,
+        out_specs=(vm,) * 5 + (far,) * 5,
         scratch_shapes=[
             pltpu.VMEM((heads, KINDS - 1, SPAN, seq), F32),
             pltpu.VMEM((seq, seq), F32),
@@ -649,9 +663,15 @@
             pltpu.VMEM(w_back.shape[1:], BF16),
             pltpu.VMEM((PARTS, 4, slots, width), BF16),
             pltpu.VMEM((PARTS, 4, slots, w_in.shape[2]), F32),
-            pltpu.SemaphoreType.DMA((2,)),
-            pltpu.SemaphoreType.DMA((2 * PARTS,)),
+            pltpu.SemaphoreType.DMA((5,)),
+            pltpu.SemaphoreType.DMA((3 + 2 * PARTS,)),
             *slot_buffers(experts, width) * 2,
+            pltpu.VMEM(w_qkv.shape[1:], BF16),
+            pltpu.VMEM(w_out.shape[1:], BF16),
+            pltpu.VMEM((4, rows, width), BF16),
+            pltpu.VMEM((seq, 3 * part), BF16),
+            pltpu.VMEM((4, rows, part), BF16),
+            pltpu.VMEM((rows, width), BF16),
             *scatter_buffers(rows, width),
             *[pltpu.SemaphoreType.DMA((6,))] * 4,
             *expert_scratch(experts, slots, width),
@@ -659,13 +679,12 @@
         compiler_params=pltpu.CompilerParams(
             collective_id=layer, has_side_effects=True, vmem_limit_bytes=56 << 20
         ),
-    )(x, gains, w_qkv, w_out, table, kind, router, routes, w_in, w_back)
+    )(gains, table, kind, router, routes, x, w_qkv, w_out, w_in, w_back)
 
 
 def layer_back_kernel(
-    layer, g_ref, x_ref, gains, w_qkv_both, w_out_both, tables, kind_ref, routers, routes_ref,
-    middle_ref, mixed_ref, logits_ref, picked_ref,
-    w_in_both, w_back_both, perm_in, perm_out_in, all_in, proj_in, att_in, ent_in, pre_in,
+    layer, gains, tables, kind_ref, routers, routes_ref,
+    middle_ref, mixed_ref, logits_ref, picked_ref, g_in, x_in, w_qkv_both, w_out_both, w_in_both, w_back_both, perm_in, perm_out_in, all_in, proj_in, att_in, ent_in, pre_in,
     dx_ref, dxb_ref, small_ref, pq_ref, po_ref,
     d_in_out, d_back_out, got_in, got_back, got_pq, got_po, *scratch
 ):
@@ -675,8 +694,11 @@
         d_in, d_back, w_in, w_back, perm_ref, perm_out_ref, all_ref, proj_ref, att_ref,
         ent_ref, pre_ref, sems, save_sems
     ) = scratch[:32]
+    w_qkv, w_out, g_ref, x_ref = scratch[32:36]
+    scratch = scratch[:32] + scratch[36:]
     outs, rets = scratch[32:34], scratch[34:36]
     loads, saves = Loads(sems), Loads(save_sems)
+    loads.start(own_stream(g_in), g_ref)
     loads.start(w_back_both.at[layer], w_back)
     loads.start(w_in_both.at[layer], w_in)
     loads.start(pre_in, pre_ref)
@@ -686,12 +708,15 @@
     loads.start(att_in, att_ref)
     loads.start(perm_in, perm_ref)
     loads.start(perm_out_in, perm_out_ref)
+    loads.start(w_qkv_both.at[layer], w_qkv)
+    loads.start(w_out_both.at[layer], w_out)
+    loads.start(own_stream(x_in), x_ref)
     gain_one, gain_two = gains.at[2 * layer], gains.at[2 * layer + 1]
-    w_qkv, w_out = w_qkv_both.at[layer], w_out_both.at[layer]
     table_ref, router_ref = tables.at[layer], routers.at[layer]
     partner = 1 - lax.axis_index("section")
     ids, wait_all_here = meet_all(partner)
     rows, width = x_ref.shape
+    loads.wait(0)
 
     def across(k, src, dst):
         return remote(src, dst, s_x, r_x, k, "section", partner)
@@ -721,7 +746,7 @@
         dlogits = (hot[0] * dchosen[0] + hot[1] * dchosen[1]).astype(BF16)
         drouter_ref[...] = mm_tn(mixed_ref[...], dlogits)
         dx_ref[...] = mm_nt(dlogits, router_ref[...])
-        loads.wait(0, 1, 2)
+        loads.wait(1, 2, 3)
 
     def block(n, j, expert_part):
         hidden, slope = gelu_parts(pre_ref[n, j])
@@ -741,7 +766,7 @@
         crossing[0].start()
 
     def in_grad():
-        loads.wait(3)
+        loads.wait(4)
         grad = mm_tn(flat(ent_ref), flat(dpre_ref))
         d_in[...] = grad
         saves.start(d_in, d_in_out)
@@ -753,7 +778,7 @@
         (logits_back, back_grad, lambda: None, in_grad), scratch[46:]
     )
     dleft = get_slots(*rets)
-    loads.wait(*range(4, 9))
+    loads.wait(*range(5, 13))
     dmixed = mm(slots[0] + slots[1], dleft) + dx_ref[...]
     dnorm, dgain = norm_back(middle_ref[...], gain_two[...], dmixed)
     small_ref[...] = pack_gain(dgain, 1, small_ref.shape) + pack_router(
@@ -782,7 +807,7 @@
 def layer_backward(g, keep, layer, weights, kind, routes, slots, perm, perm_out):
     x, normed, proj, attended, middle, mixed, logits, picked, entering, pre = keep
     gains, w_qkv, w_out, table, router, w_in, w_back = weights
-    rows, width = x.shape
+    rows, width = x.shape[-2:]
     seq, part, experts = 4 * rows, w_out.shape[1], router.shape[2]
     heads, hid = part // HEAD_DIM, w_in.shape[2]
     w_shape = w_in.shape[1:]
@@ -794,8 +819,8 @@
     return pl.pallas_call(
         functools.partial(layer_back_kernel, layer),
         out_shape=(
-            shape(x.shape, F32),
-            shape(x.shape, BF16),
+            shape((rows, width), F32),
+            shape((rows, width), BF16),
             shape((perm.shape[0] // OWN, SMALL), F32),
             pq,
             po,
@@ -806,7 +831,7 @@
             pq,
             po,
         ),
-        in_specs=[vm] * 13 + [far] * 9,
+        in_specs=[vm] * 9 + [far] * 13,
         out_specs=(vm,) * 5 + (far,) * 6,
         scratch_shapes=[
             pltpu.VMEM((heads, KINDS - 1, SPAN, seq), F32),
@@ -830,8 +855,12 @@
             *[pltpu.VMEM(w_shape, F32)] * 2,
             *[pltpu.VMEM(w_shape, BF16)] * 2,
             *[pltpu.VMEM(a.shape, a.dtype) for a in (perm, perm_out, *loaded)],
-            pltpu.SemaphoreType.DMA((9,)),
+            pltpu.SemaphoreType.DMA((13,)),
             pltpu.SemaphoreType.DMA((2,)),
+            pltpu.VMEM(w_qkv.shape[1:], BF16),
+            pltpu.VMEM(w_out.shape[1:], BF16),
+            pltpu.VMEM((rows, width), BF16),
+            pltpu.VMEM((rows, width), BF16),
             *slot_buffers(experts, width) * 2,
             *scatter_buffers(rows, width),
             *[pltpu.SemaphoreType.DMA((6,))] * 4,
@@ -841,8 +870,8 @@
             collective_id=2 + layer, has_side_effects=True, vmem_limit_bytes=60 << 20
         ),
     )(
-        g, x, gains, w_qkv, w_out, table, kind, router, routes, middle, mixed, logits, picked,
-        w_in, w_back, perm, perm_out, *loaded
+        gains, table, kind, router, routes, middle, mixed, logits, picked, g, x,
+        w_qkv, w_out, w_in, w_back, perm, perm_out, *loaded
     )
 
 
@@ -1131,10 +1160,10 @@
     box_out[0] = pieces_out[exp]
     sent_y[...] = jnp.where(first, y1[...], y0[...])
     cross[1].start()
-    sent_dx[...] = jnp.where(first, dx1[...], dx0[...])
+    sent_dx[...] = jnp.where(first, dx1[...].astype(F32), dx0[...])
     cross[2].start()
     layer_out[section] = jnp.where(first, y0[...], y1[...])
-    input_grad[section] = jnp.where(first, dx0[...], dx1[...])
+    input_grad[section] = jnp.where(first, dx0[...], dx1[...].astype(F32))
     saves = Loads(save_sems)
     loaded(4, 5)
     d_in[...] += gin[...].astype(F32)
@@ -1312,8 +1341,10 @@
     taken = lax.ppermute(given, "section", [(0, 1), (1, 0)])
     layer_routes = (jnp.where(first, kept, taken), jnp.where(first, taken, kept))
     def forward(x, layer):
-        h, *saved = layer_forward(x, layer, weights, kind, layer_routes[layer], slots)
-        return h, (x, *saved)
+        h, middle, mixed, logits, picked, normed, proj, attended, *rest = layer_forward(
+            x, layer, weights, kind, layer_routes[layer], slots
+        )
+        return h, (x, normed, proj, attended, middle, mixed, logits, picked, *rest)
 
     def backward(g, keep, layer):
         dx, dxb, d_small, pq, po, d_in, d_back, g_in, g_back, gq, go = layer_backward(
@@ -1321,16 +1352,14 @@
         )
         return dx, dxb, (pq, gq, po, go, d_small, d_in, g_in, d_back, g_back)
 
-    x = jnp.where(first, inputs[0, 0], inputs[1, 0])
-    cot = jnp.where(first, cotangent[0, 0], cotangent[1, 0])
-    h, keep0 = forward(x, 0)
+    h, keep0 = forward(inputs, 0)
     top, keep1 = forward(h, 1)
-    _, dh, grads1 = backward(cot, keep1, 1)
+    _, dh, grads1 = backward(cotangent, keep1, 1)
     dx, _, grads0 = backward(dh, keep0, 0)
     pq, gq, po, go, d_small, d_in, g_in, d_back, g_back = zip(grads0, grads1)
     pieces, out_grad, d_in, d_back, layer_out, input_grad = sum_at_owners(
         pq, gq, po, go, d_small, place, d_in, g_in, d_back, g_back,
-        (h, top), (dx, dh.astype(F32)), n_exp
+        (h, top), (dx, dh), n_exp
     )
     qkv_grad = pieces[:, :own_rows].reshape(n_ctx, own_rows, 3, part)
     qkv_grad = qkv_grad.transpose(1, 2, 0, 3).reshape(own_rows, 3 * width)

time: 394 us -> 390 us (0.990)
  Pallas kernels: 359 us -> 353 us
  local copies, waits for them, and re-layouts: 20.8 us -> 26.2 us
    unnamed x45 -> x47, local copies, waits for them, and re-layouts: 13.5 us -> 19.1 us
  transfers between devices with their start and end apart: 1 -> 1, of which waited for: 0 -> 0; matrix products, arithmetic and copies ran while one was open for 2% -> 1% of each run, Pallas kernels for 9% -> 9%
where the time goes in v7:
time: 390 us; the launch traced here: 383 us
  Pallas kernels  353 us (91%)
  local copies, waits for them, and re-layouts  26.2 us (7%)
    pallas_call x2, Pallas kernels, layer_backward(): pl.pallas_call(functools.partial(layer_back_kernel, layer), out_shape=(sh...  150 us
    pallas_call x2, Pallas kernels, layer_forward(): pl.pallas_call(functools.partial(layer_kernel, layer), out_shape=(shape((...  139 us
    pallas_call x1, Pallas kernels, gather_weights(): pl.pallas_call(weights_kernel, out_shape=(jax.ShapeDtypeStruct((2, width,...  36.3 us
    pallas_call x1, Pallas kernels, sum_at_owners(): pl.pallas_call(owners_kernel, out_shape=(jax.ShapeDtypeStruct(quarter, F3...  27.3 us
    unnamed x47, local copies, waits for them, and re-layouts  19.1 us
  transfers between devices with their start and end apart: 1, of which 0 were waited for; matrix products, arithmetic and copies ran while one was open for 1% of the time, Pallas kernels for 9%

profile of v7, /device:TPU:2, one launch (start us, length us, event | category | flops | bytes accessed | tf_op | source)
XLA Modules:
  0.0 383.3 jit_solution(916576568960749232)
XLA Ops:
  0.6 0.7 fusion.11
  1.7 0.8 reshape_squeeze.7
  2.5 0.8 fusion.3
  3.3 1.0 reshape_squeeze.6
  4.5 0.8 fusion.10
  5.4 0.7 reshape.49.kind_ref
  6.0 0.7 pad.14.outp_ref
  6.8 1.3 copy-done.3
  8.1 1.3 copy-done.4
  9.3 1.3 copy-done.5
  10.6 0.9 copy-done.11
  11.5 0.8 copy-done.15
  12.2 0.7 copy-done.16
  13.0 0.7 copy-done.17
  13.6 36.3 %shard_map.267 = (bf16[2,768,576]{2,1,0:T(8,128)(2,1)}, bf16[2,192,768]{2,1,0:T(8,128)(2,1)S(1)}, f32[4,1,768]{2,1,0:T(1,128)S(1)}, bf16[2,768,16]{2,1,0:T(8,128...) custom-call(bf16[4,16,576]{2,1,0:T(8,128)(2,1)S(1)} %fusion.2.cols_ref, ...), custom_call_target="tpu_custom_call" | custom-call | tf_op jit(solution)/shard_map/pallas_call | solution.py:1078
  50.0 0.8 copy-done
  50.8 0.7 copy-done.1
  52.8 0.7 bitcast_select_fusion
  53.4 71.0 %shard_map.268 = (bf16[128,768]{1,0:T(8,128)(2,1)}, f32[128,768]{1,0:T(8,128)}, bf16[128,768]{1,0:T(8,128)(2,1)}, f32[128,16]{1,0:T(8,128)}, bf16[2,128,768]{2,1...) custom-call(f32[4,1,768]{2,1,0:T(1,128)} %copy-done.10, ...), custom_call_target="tpu_custom_call" | custom-call | tf_op jit(solution)/shard_map/pallas_call | solution.py:641
  124.5 68.2 %shard_map.269 = (bf16[128,768]{1,0:T(8,128)(2,1)}, f32[128,768]{1,0:T(8,128)}, bf16[128,768]{1,0:T(8,128)(2,1)}, f32[128,16]{1,0:T(8,128)}, bf16[2,128,768]{2,1...) custom-call(f32[4,1,768]{2,1,0:T(1,128)} %copy-done.10, ...), custom_call_target="tpu_custom_call" | custom-call | tf_op jit(solution)/shard_map/pallas_call | solution.py:641
  192.7 75.3 %shard_map.270 = (f32[128,768]{1,0:T(8,128)}, bf16[128,768]{1,0:T(8,128)(2,1)}, f32[64,256]{1,0:T(8,128)}, bf16[768,576]{1,0:T(8,128)(2,1)}, bf16[256,768]{1,0:T...) custom-call(f32[4,1,768]{2,1,0:T(1,128)} %copy-done.10, ...), custom_call_target="tpu_custom_call" | custom-call | tf_op jit(solution)/shard_map/pallas_call | solution.py:819
  268.1 75.1 %shard_map.271 = (f32[128,768]{1,0:T(8,128)}, bf16[128,768]{1,0:T(8,128)(2,1)}, f32[64,256]{1,0:T(8,128)}, bf16[768,576]{1,0:T(8,128)(2,1)}, bf16[256,768]{1,0:T...) custom-call(f32[4,1,768]{2,1,0:T(1,128)} %copy-done.10, ...), custom_call_target="tpu_custom_call" | custom-call | tf_op jit(solution)/shard_map/pallas_call | solution.py:819
  343.3 1.0 copy-done.8
  344.2 0.8 copy-done.14
  345.1 27.3 %shard_map.272 = (f32[4,16,576]{2,1,0:T(8,128)S(1)}, f32[16,768]{1,0:T(8,128)S(1)}, f32[1,1,768,768]{3,2,1,0:T(8,128)}, f32[1,1,768,768]{3,2,1,0:T(8,128)}, bf16...) custom-call(f32[64,256]{1,0:T(8,128)S(1)} %copy-done.14, f32[64,256]{1,0:T(8,128)S(1)} %copy-done.13, ...), custom_call_target="tpu_custom_call" | custom-call | tf_op jit(solution)/shard_map/pallas_call | solution.py:1211
  373.7 0.7 reshape.53
  375.3 0.9 broadcast_in_dim_reshape.4
  376.1 0.7 copy.63
  376.9 2.1 copy.64
  378.9 1.4 copy.65
  380.4 1.1 copy-done.18
  381.5 1.4 copy.66
  (48 shorter events, 4.0 us)
Async XLA Ops:
  1.6 51.2 %collective-permute-start = (s32[128,2]{1,0:T(8,128)S(1)}, s32[128,2]{1,0:T(8,128)S(1)}, u32[]{:S(2)}, u32[]{:S(2)}) collective-permute-start(s32[128,2]{1,0:T(8,128)S(1)} %select_bitcast_fusion), channel_id=1, source_target_pairs={{0,64},{64,0},{1,65},{65,1},{2,66},{66,2},{3,67},{67,3},{4,68},{68... | collective-permute-start | bytes 3080 | tf_op jit(solution)/shard_map/ppermute | solution.py:1341
  6.8 1.3 copy-start.3
  8.1 1.3 copy-start.4
  9.3 1.3 copy-start.5
  10.6 0.9 copy-start.11
  11.5 0.8 copy-start.15
  12.2 0.7 copy-start.16
  13.0 0.7 copy-start.17
  50.0 0.8 copy-start
  50.8 0.7 copy-start.1
  51.5 0.6 copy-start.7
  52.2 0.6 copy-start.10
  268.0 75.2 %copy-start.2 = (bf16[128,768]{1,0:T(8,128)(2,1)S(1)}, bf16[128,768]{1,0:T(8,128)(2,1)}, u32[]{:S(2)}) copy-start(bf16[128,768]{1,0:T(8,128)(2,1)} %get-tuple-element.74.x_in.y0) | copy-start | bytes 589828
  268.0 75.2 %copy-start.6 = (bf16[128,768]{1,0:T(8,128)(2,1)S(1)}, bf16[128,768]{1,0:T(8,128)(2,1)}, u32[]{:S(2)}) copy-start(bf16[128,768]{1,0:T(8,128)(2,1)} %get-tuple-element.84.g_in.dx1) | copy-start | bytes 589828
  268.0 75.2 %copy-start.9 = (bf16[128,768]{1,0:T(8,128)(2,1)S(1)}, bf16[128,768]{1,0:T(8,128)(2,1)}, u32[]{:S(2)}) copy-start(bf16[128,768]{1,0:T(8,128)(2,1)} %get-tuple-element.92.y1) | copy-start | bytes 589828
  268.0 75.2 %copy-start.12 = (bf16[256,64]{1,0:T(8,128)(2,1)S(1)}, bf16[256,64]{1,0:T(8,128)(2,1)}, u32[]{:S(2)}) copy-start(bf16[256,64]{1,0:T(8,128)(2,1)} %constant.35.clone.spread_ref) | copy-start | bytes 98308
  268.1 75.2 %copy-start.13 = (f32[64,256]{1,0:T(8,128)S(1)}, f32[64,256]{1,0:T(8,128)}, u32[]{:S(2)}) copy-start(f32[64,256]{1,0:T(8,128)} %get-tuple-element.91.small1) | copy-start | bytes 196612
  343.2 1.0 copy-start.8
  344.2 0.8 copy-start.14
  372.4 6.5 %copy-start.19 = (f32[1,1,768,768]{3,2,1,0:T(8,128)S(1)}, f32[1,1,768,768]{3,2,1,0:T(8,128)}, u32[]{:S(2)}) copy-start(f32[1,1,768,768]{3,2,1,0:T(8,128)} %get-tuple-element.170) | copy-start | bytes 7077892
  378.9 2.5 copy-start.18
